TPU v7x, 32 devices: a whole 2x2x4 slice. The times are simulated.
32 devices in a mesh: leaf: 8 (over z, y), panel: 4 (over x, core).
Axes of the slice: x: 2, y: 2, z: 4, core: 2. Of those that a mesh axis runs over, the one named last changes fastest.
Arguments:
- border: bfloat16 [8, 128, 8192], P('leaf', 'panel'), may hold values from -0.1875 to 0.1875
- solution: bfloat16 [8, 128, 128], P('leaf', 'panel'), may hold values from -6 to 6
- winv_top: bfloat16 [4096, 4096], P(None, ('leaf', 'panel')), as said below
- winv_mid: bfloat16 [4096, 8192], P(None, ('leaf', 'panel')), as said below
- coupling: bfloat16 [8192, 4096], P(('leaf', 'panel')), may hold values from -0.0625 to 0.0625
Outputs:
- top_adjoint: float32 [4096, 128], P(('leaf', 'panel'))
- mid_adjoint: float32 [8192, 128], P(('leaf', 'panel'))
Inputs may be any that keep to these rules, and one draw needn't show every extreme that they name: `winv_top`: each 4096 x 4096 block of the factor is lower triangular with a positive diagonal. `winv_mid`: each 4096 x 4096 block of the factor is lower triangular with a positive diagonal.
All inputs are finite; a program needn't handle non-finite values.
Results may differ from a plain program's by a relative error of at most 0.0003.
Values sent between devices are 32-bit elements; how exact they have to be, the bound alone decides.
No kernel may reach another device: no remote copies, remote signals or barrier semaphores. Data moves between devices by JAX's collectives and lax.ppermute only.
A program may use at most 64 MiB of HBM per device.

v0:
```python
import functools

import jax
import jax.numpy as jnp
from jax import lax
from jax.experimental import pallas as pl
from jax.experimental.pallas import tpu as pltpu
from jax.sharding import PartitionSpec as P

AXES = ("leaf", "panel")
F32 = jnp.float32
BF16 = jnp.bfloat16
LANES = 128


def plain_body(border, solution, winv_top, winv_mid, coupling):
    leaves = lax.axis_size("leaf")
    panels = lax.axis_size("panel")
    half = leaves // 2
    leaf_id = lax.axis_index("leaf")
    front = winv_top.shape[0]
    top_cols = winv_top.shape[1]
    mid_cols = winv_mid.shape[1]
    contribution = lax.dot_general(
        border[0], solution[0], (((0,), (0,)), ((), ())), preferred_element_type=F32
    )
    groups = [list(range(half)), list(range(half, leaves))]
    device = leaf_id * panels + lax.axis_index("panel")
    in_half = device % (half * panels)
    top_load = lax.psum(contribution[:front], AXES)
    top_block = lax.dynamic_slice_in_dim(top_load, device * top_cols, top_cols, 0)
    mid_load = lax.psum(contribution[front:], "panel")
    mid_load = lax.psum(mid_load, "leaf", axis_index_groups=groups)
    mid_block = lax.dynamic_slice_in_dim(mid_load, in_half * mid_cols, mid_cols, 0)
    top_factor = winv_top.astype(F32)
    mid_factor = winv_mid.astype(F32)
    exact = lax.Precision.HIGHEST
    top_inner = lax.psum(jnp.dot(top_factor, top_block, precision=exact), AXES)
    top_adjoint = jnp.dot(top_factor.T, top_inner, precision=exact)
    top_whole = lax.all_gather(top_adjoint, AXES, axis=0, tiled=True)
    mid_rhs = mid_block - jnp.dot(coupling.astype(F32), top_whole, precision=exact)
    mid_inner = lax.psum(jnp.dot(mid_factor, mid_rhs, precision=exact), "panel")
    mid_inner = lax.psum(mid_inner, "leaf", axis_index_groups=groups)
    mid_adjoint = jnp.dot(mid_factor.T, mid_inner, precision=exact)
    return top_adjoint, mid_adjoint


CHAINS = 2
WIDE = 64


def permute(value, partner):
    return lax.ppermute(value, AXES, [(i, partner(i)) for i in range(32)])


def swap_core(value):
    return permute(value, lambda i: i ^ 1)


def swap_first(value, chain=0):
    return permute(value, lambda i: i ^ (4 if (i ^ chain) & 1 else 2))


def swap_second(value, chain=0):
    return permute(value, lambda i: i ^ (2 if (i ^ chain) & 1 else 4))


def swap_cross(value):
    return permute(value, lambda i: i ^ (3 if i & 1 else 5))


def swap_near(value):
    return permute(value, lambda i: i ^ 8)


def swap_far(value):
    return permute(value, lambda i: i ^ 16)


def coords():
    leaf = lax.axis_index("leaf")
    panel = lax.axis_index("panel")
    return leaf // 2, leaf % 2, panel // 2, panel % 2


def flip(a, k):
    return a + k - 2 * a * k


def z_flip(z, k):
    return flip(z // 2, k // 2) * 2 + flip(z % 2, k % 2)


Z_ORDER = (0, 2, 1, 3)


def plane_at(y, x, c, first, second):
    along_x = first * (1 - c) + second * c
    along_y = first * c + second * (1 - c)
    return flip(y, along_y) * 2 + flip(x, along_x)


def block_starts(deep, chain):
    z, y, x, c = coords()
    c = flip(c, chain)
    starts = []
    for first in range(2):
        for second in range(2):
            plane = plane_at(y, x, c, first, second)
            for j in range(4):
                if deep:
                    start = (z_flip(z, Z_ORDER[j]) * 4 + plane) * 128
                else:
                    start = (flip(z % 2, j // 2) * 4 + plane) * 256 + j % 2 * 128
                starts.append(pl.multiple_of(start, 128))
    return starts


def kernel_call(kernel, outs, ins, scratch=(), flops=0, limit=10, after=()):
    vmem = pl.BlockSpec(memory_space=pltpu.VMEM)
    size = lambda s: s.size * s.dtype.itemsize

    def ordered(*refs):
        kernel(*refs[: len(ins)], *refs[len(ins) + len(after) :])

    return pl.pallas_call(
        ordered,
        out_shape=[jax.ShapeDtypeStruct(*o) for o in outs],
        in_specs=[vmem] * len(ins) + [pl.BlockSpec(memory_space=pl.ANY)] * len(after),
        out_specs=[vmem] * len(outs),
        scratch_shapes=list(scratch),
        compiler_params=pltpu.CompilerParams(vmem_limit_bytes=limit * 2**20),
        cost_estimate=pl.CostEstimate(
            flops=flops,
            transcendentals=0,
            bytes_accessed=sum(map(size, ins))
            + sum(size(jax.ShapeDtypeStruct(*o)) for o in outs),
        ),
    )(*ins, *after)


def glue(fn, *ins, after=()):
    shapes = jax.eval_shape(fn, *ins)

    def kernel(*refs):
        values = fn(*[r[...] for r in refs[: len(ins)]])
        for ref, value in zip(refs[len(ins) :], values):
            ref[...] = value

    return kernel_call(kernel, [(o.shape, o.dtype) for o in shapes], ins, after=after)


def left_lanes(shape):
    return lax.broadcasted_iota(jnp.int32, shape, 1) < WIDE


def pack(low, high):
    left = left_lanes(low.shape)
    return (
        jnp.where(left, low, pltpu.roll(high, WIDE, 1)),
        jnp.where(left, pltpu.roll(low, WIDE, 1), high),
    )


def put_split(rhs_ref, start, block):
    left = left_lanes(block.shape)
    turned = pltpu.roll(block, WIDE, 1)
    for i, rows in enumerate((jnp.where(left, block, turned), jnp.where(left, turned, block))):
        high = rows.astype(BF16).astype(F32)
        both = jnp.where(left, high, rows - high)
        rhs_ref[pl.ds(start + i * WIDE, WIDE), :] = both.astype(BF16)


def product(w_ref, rhs_ref):
    both = jnp.dot(w_ref[...], rhs_ref[...], preferred_element_type=F32)
    return both + pltpu.roll(both, WIDE, 1)


def take_block(total, start):
    low = total[start : start + WIDE]
    high = total[start + WIDE : start + 2 * WIDE]
    return jnp.where(left_lanes(low.shape), low, high)


def prep_top(border_ref, sol_ref, *tops):
    z, y, x, c = coords()
    sol = sol_ref[...].astype(F32)
    for rel in range(4):
        core = flip(c, rel % 2)
        for second in range(2):
            plane = plane_at(y, x, core, rel // 2, second)
            for j in range(4):
                col = pl.multiple_of((z_flip(z, Z_ORDER[j]) * 8 + plane * 2 + core) * 128, 128)
                here = (second * 4 + j) * 128
                tops[rel][:, here : here + 128] = border_ref[:, pl.ds(col, 128)].astype(F32)
        tops[rel][:, 1024:] = sol


def prep_mid(border_ref, *mids):
    z, y, x, c = coords()
    front = border_ref.shape[1] // 2
    for rel in range(4):
        core = flip(c, rel % 2)
        for second in range(2):
            plane = plane_at(y, x, core, rel // 2, second)
            for k in range(2):
                col = front + (flip(z % 2, k) * 8 + plane * 2 + core) * 256
                here = (second * 2 + k) * 256
                mids[rel][:, here : here + 256] = border_ref[
                    :, pl.ds(pl.multiple_of(col, 256), 256)
                ].astype(F32)


def stack_rows(refs, cols, out_ref):
    n = refs[0].shape[0]
    for i, ref in enumerate(refs):
        out_ref[i * n : (i + 1) * n, :] = ref[:, cols].astype(BF16)


def put_loads(sol, rows, outs):
    total = lax.dot_general(
        sol, rows, (((0,), (0,)), ((), ())), preferred_element_type=F32
    )
    for second in range(2):
        for j in range(4):
            here = (second * 4 + j) * 128
            block = total[:, here : here + 128].T
            packed = pack(block[:WIDE], block[WIDE:])
            for h in range(CHAINS):
                outs[h][second][j] = packed[h]


def top_load_kernel(*refs):
    ins, (keep_ref, send_ref, sol_ref, rows_ref) = refs[:4], refs[4:]
    stack_rows(ins, slice(0, 1024), rows_ref)
    stack_rows(ins, slice(1024, 1152), sol_ref)
    outs = [[keep_ref.at[h], send_ref.at[h]] for h in range(CHAINS)]
    put_loads(sol_ref[...], rows_ref[...], outs)


def mid_load_kernel(*refs):
    ins, sol_ref, keep_ref, send_ref, rows_ref = refs[:4], *refs[4:]
    stack_rows(ins, slice(0, 1024), rows_ref)
    outs = [[keep_ref.at[h], send_ref.at[h]] for h in range(CHAINS)]
    put_loads(sol_ref[...], rows_ref[...], outs)


def halve_rows(w_ref, keep_ref, send_ref):
    z, y, x, c = coords()
    rows = w_ref.shape[0] // 2
    keep_ref[...] = w_ref[pl.ds(pl.multiple_of(c * rows, rows), rows), :]
    send_ref[...] = w_ref[pl.ds(pl.multiple_of((1 - c) * rows, rows), rows), :].astype(F32)


def halve_cols(w_ref, keep_ref, send_ref):
    z, y, x, c = coords()
    for i in range(w_ref.shape[1] // 256):
        here = slice(i * 128, (i + 1) * 128)
        kept = pl.multiple_of(i * 256 + c * 128, 128)
        sent = pl.multiple_of(i * 256 + (1 - c) * 128, 128)
        keep_ref[:, here] = w_ref[:, pl.ds(kept, 128)]
        send_ref[:, here] = w_ref[:, pl.ds(sent, 128)].astype(F32)


def join_cols(keep_ref, recv_ref, w_ref, t_ref):
    n = keep_ref.shape[1]
    w_ref[:, :n] = keep_ref[...]
    w_ref[:, n:] = recv_ref[...].astype(BF16)
    t_ref[:n, :] = keep_ref[...].T
    t_ref[n:, :] = recv_ref[...].astype(BF16).T


def join_rows(keep_ref, recv_ref, w_ref):
    n = keep_ref.shape[0]
    w_ref[:n, :] = keep_ref[...]
    w_ref[n:, :] = recv_ref[...].astype(BF16)


def forward(deep, chain, w_ref, *refs):
    vec, (send_ref, next_ref, keep_ref), (rhs_ref, sum_ref) = refs[:-5], refs[-5:-2], refs[-2:]
    blocks = vec[0].shape[0]
    if len(vec) == 2:
        own, other = vec[0][...], vec[1][...]
    else:
        mine, theirs, part, recv = [v[...] for v in vec]
        own = mine - part[:blocks] - recv[blocks:]
        other = theirs - part[blocks:] - recv[:blocks]
    for i in range(blocks):
        put_split(rhs_ref, i * 128, own[i])
        put_split(rhs_ref, (blocks + i) * 128, other[i])
    sum_ref[...] = product(w_ref, rhs_ref)
    left = left_lanes((WIDE, 2 * WIDE))
    for i, start in enumerate(block_starts(deep, chain)):
        low = sum_ref[pl.ds(start, WIDE), :]
        high = sum_ref[pl.ds(start + WIDE, WIDE), :]
        block = jnp.where(left, low, high)
        if i < 4:
            keep_ref[i] = block
        elif i < 8:
            next_ref[i - 4] = block
        else:
            send_ref[i - 8] = block


def backward(deep, chain, w_ref, near_ref, far_ref, *refs):
    outs, rhs_ref = refs[:-1], refs[-1]
    for i, start in enumerate(block_starts(deep, chain)):
        put_split(rhs_ref, start, near_ref[i] if i < 8 else far_ref[i - 8])
    total = product(w_ref, rhs_ref)
    blocks = w_ref.shape[0] // 128
    for i in range(blocks):
        if len(outs) == 1:
            outs[0][i] = take_block(total, i * 128)
        else:
            outs[2 * i // blocks][i % (blocks // 2)] = take_block(total, i * 128)


def run_forward(w, vec, deep, chain, after=()):
    m, k = w.shape
    return kernel_call(
        functools.partial(forward, deep, chain),
        [((8, WIDE, 128), F32), ((4, WIDE, 128), F32), ((4, WIDE, 128), F32)],
        [w, *vec],
        [pltpu.VMEM((k, 128), BF16), pltpu.VMEM((m, 128), F32)],
        flops=2 * m * k * 128,
        after=after,
    )


def run_backward(w, near, far, deep, chain, apart, after=()):
    m, k = w.shape
    return kernel_call(
        functools.partial(backward, deep, chain),
        [((m // 256, WIDE, 128), F32)] * 2 if apart else [((m // 128, WIDE, 128), F32)],
        [w, near, far],
        [pltpu.VMEM((k, 128), BF16)],
        flops=2 * m * k * 128,
        after=after,
    )


def depth_sum(value):
    value = value[:, :2] + swap_near(value[:, 2:])
    return value[:, :1] + swap_far(value[:, 1:])


def plane_sum(send, follow, keep, chain):
    first = swap_first(send, chain)
    second = swap_second(follow + first[4:], chain)
    return keep + first[:4] + second, second


def depth_total(value, deep):
    if not deep:
        return value + swap_near(jnp.concatenate([value[2:], value[:2]], 0))
    keep = value[:2] + swap_near(value[2:])
    keep = keep + swap_far(jnp.concatenate([keep[1:], keep[:1]], 0))
    return jnp.concatenate([keep, swap_near(keep)], 0)


def depth_spread(own):
    pair = jnp.concatenate([own, swap_far(own)], 0)
    return jnp.concatenate([pair, swap_near(pair)], 0)


def plane_spread(line, chain):
    near = jnp.concatenate([line, swap_second(line, chain)], 0)
    return near, swap_first(near, chain)


def unpack_kernel(mine0, recv0, mine1, recv1, out_ref):
    left = left_lanes((WIDE, 128))
    for i in range(mine0.shape[0]):
        p0 = mine0[i] + recv0[i]
        p1 = mine1[i] + recv1[i]
        out_ref[i * 128 : i * 128 + WIDE, :] = jnp.where(left, p0, pltpu.roll(p1, WIDE, 1))
        out_ref[i * 128 + WIDE : (i + 1) * 128, :] = jnp.where(left, pltpu.roll(p0, WIDE, 1), p1)


def unpack(*pairs):
    ins = [array for pair in pairs for array in pair]
    return kernel_call(unpack_kernel, [((ins[0].shape[0] * 128, 128), F32)], ins)[0]


def fast_body(border, solution, winv_top, winv_mid, coupling):
    front = winv_top.shape[0]
    half = front // 2
    tops = ready = kernel_call(
        prep_top, [((32, 1152), F32)] * 4, [border[0], solution[0]]
    )
    tops = [tops[0], swap_core(tops[1]), swap_first(tops[2]), swap_cross(tops[3])]
    keep, send, sol_all = kernel_call(
        top_load_kernel,
        [((CHAINS, 4, WIDE, 128), F32)] * 2 + [((128, 128), BF16)],
        tops,
        [pltpu.VMEM((128, 1024), BF16)],
        flops=2 * 128 * 1024 * 128,
    )
    got = swap_second(send)
    load = depth_sum(keep + got)
    load_other = swap_core(load)

    mids = kernel_call(prep_mid, [((32, 1024), F32)] * 4, [border[0]], after=[got])
    mids = [mids[0], swap_core(mids[1]), swap_first(mids[2]), swap_cross(mids[3])]

    top_keep, top_send = kernel_call(
        halve_rows, [((half, 128), BF16), ((half, 128), F32)], [winv_top], after=ready[:1]
    )
    cou_keep, cou_send = kernel_call(
        halve_cols, [((256, half), BF16), ((256, half), F32)], [coupling]
    )
    mid_keep, mid_send = kernel_call(
        halve_rows, [((half, 256), BF16), ((half, 256), F32)], [winv_mid]
    )
    top_w, top_t = kernel_call(
        join_cols,
        [((half, 256), BF16), ((256, half), BF16)],
        [top_keep, swap_core(top_send)],
    )
    (cou_w,) = kernel_call(
        join_rows, [((512, half), BF16)], [cou_keep, swap_core(cou_send)]
    )

    mid_w, mid_t = kernel_call(
        join_cols,
        [((half, 512), BF16), ((512, half), BF16)],
        [mid_keep, swap_core(mid_send)],
    )

    chains = range(CHAINS)
    values = []
    for h in chains:
        parts = run_forward(top_w, [load[h], load_other[h]], True, h, after=mids)
        values.append(plane_sum(*parts, h)[0])
    keep, send = kernel_call(
        mid_load_kernel,
        [((CHAINS, 4, WIDE, 128), F32)] * 2,
        [*mids, sol_all],
        [pltpu.VMEM((128, 1024), BF16)],
        flops=2 * 128 * 1024 * 128,
    )
    keep, send = glue(
        lambda k, g: ((k + g)[:, :2], (k + g)[:, 2:]), keep, swap_second(send)
    )
    mid_load = keep + swap_near(send)
    mid_other = swap_core(mid_load)
    top_parts, adjoint = [], []
    for h in chains:
        mine, theirs = run_backward(
            top_t,
            *plane_spread(depth_total(values[h], True), h),
            True,
            h,
            True,
            after=[cou_w, mid_w],
        )
        top_parts.append((mine, swap_core(theirs)))
        adjoint.append(mine + top_parts[h][1])
    top_out = unpack(*top_parts)

    mid_parts = []
    for h in chains:
        (both,) = run_backward(
            cou_w, *plane_spread(depth_spread(adjoint[h]), h), True, h, False
        )
        vec = [mid_load[h], mid_other[h], both, swap_core(both)]
        parts = run_forward(mid_w, vec, False, h, after=[top_out] if h else ())
        line = depth_total(plane_sum(*parts, h)[0], False)
        mine, theirs = run_backward(mid_t, *plane_spread(line, h), False, h, True)
        mid_parts.append((mine, swap_core(theirs)))
    return top_out, unpack(*mid_parts)


def solution(mesh):
    placed = (
        P("leaf", "panel", None),
        P("leaf", "panel", None),
        P(None, AXES),
        P(None, AXES),
        P(AXES, None),
    )
    fits = mesh.shape["leaf"] == 8 and mesh.shape["panel"] == 4
    return jax.shard_map(
        fast_body if fits else plain_body,
        mesh=mesh,
        in_specs=placed,
        out_specs=(P(AXES, None), P(AXES, None)),
        check_vma=False,
    )
```

profile of v0, /device:TPU:0, one launch (start us, length us, event | category | flops | bytes accessed | tf_op | source)
XLA Modules:
  0.0 144.6 jit_solution(9193467344214659755)
XLA Ops:
  3.0 2.6 %collective-permute-start.2 = (f32[32,1152]{1,0:T(8,128)S(1)}, f32[32,1152]{1,0:T(8,128)S(1)}, u32[]{:S(2)}, u32[]{:S(2)}) collective-permute-start(f32[32,1152]{1,0:T(8,128)S(1)} %get-tuple-element.53), channel_id=1, source_target_pairs={{0,2},{1,5},{2,0},{3,7},{4,6},{5,1},{6,4},{7,3},{8,10},{9,13},{10,... | collective-permute-start | bytes 442376 | tf_op jit(solution)/shard_map/ppermute | solution.py:53
  5.7 3.6 %collective-permute-done.2.refs_2_ = f32[32,1152]{1,0:T(8,128)S(1)} collective-permute-done((f32[32,1152]{1,0:T(8,128)S(1)}, f32[32,1152]{1,0:T(8,128)S(1)}, u32[]{:S(2)}, u32[]{:S(2)}) %collective-permute-start.2) | collective-permute-done | bytes 147488 | tf_op jit(solution)/shard_map/ppermute | solution.py:53
  10.8 2.1 %collective-permute-start.4 = (f32[2,4,64,128]{3,2,1,0:T(8,128)S(1)}, f32[2,4,64,128]{3,2,1,0:T(8,128)S(1)}, u32[]{:S(2)}, u32[]{:S(2)}) collective-permute-start(f32[2,4,64,128]{3,2,1,0:T(8,128)S(1)} %get-tuple-element.56), channel_id=1, source_target_pairs={{0,4},{1,3},{2,6},{3,1},{4,0},{5,7},{6,2},{7,5},{8,12},{9,11},{10,... | collective-permute-start | bytes 786440 | tf_op jit(solution)/shard_map/ppermute | solution.py:53
  13.0 4.4 %collective-permute-done.4.refs_1_ = f32[2,4,64,128]{3,2,1,0:T(8,128)S(1)} collective-permute-done((f32[2,4,64,128]{3,2,1,0:T(8,128)S(1)}, f32[2,4,64,128]{3,2,1,0:T(8,128)S(1)}, u32[]{:S(2)}, u32[]{:S(2)}) %collective-permute-start.4) | collective-permute-done | bytes 262176 | tf_op jit(solution)/shard_map/ppermute | solution.py:53
  17.4 2.1 %collective-permute-start.5 = (f32[2,2,64,128]{3,2,1,0:T(8,128)S(1)}, f32[2,2,64,128]{3,2,1,0:T(8,128)S(1)}, u32[]{:S(2)}, u32[]{:S(2)}) collective-permute-start(f32[2,2,64,128]{3,2,1,0:T(8,128)S(1)} %slice.129), channel_id=1, source_target_pairs={{0,8},{1,9},{2,10},{3,11},{4,12},{5,13},{6,14},{7,15},{8,0},{9,1},... | collective-permute-start | bytes 393224 | tf_op jit(solution)/shard_map/ppermute | solution.py:53
  19.7 2.8 %collective-permute-done.5 = f32[2,2,64,128]{3,2,1,0:T(8,128)S(1)} collective-permute-done((f32[2,2,64,128]{3,2,1,0:T(8,128)S(1)}, f32[2,2,64,128]{3,2,1,0:T(8,128)S(1)}, u32[]{:S(2)}, u32[]{:S(2)}) %collective-permute-start.5) | collective-permute-done | bytes 131104 | tf_op jit(solution)/shard_map/ppermute | solution.py:53
  22.5 3.1 %collective-permute-start.6 = (f32[2,1,64,128]{3,2,1,0:T(8,128)S(1)}, f32[2,1,64,128]{3,2,1,0:T(8,128)S(1)}, u32[]{:S(2)}, u32[]{:S(2)}) collective-permute-start(f32[2,1,64,128]{3,2,1,0:T(8,128)S(1)} %slice.131), channel_id=1, source_target_pairs={{0,16},{1,17},{2,18},{3,19},{4,20},{5,21},{6,22},{7,23},{8,24},{9,... | collective-permute-start | bytes 196616 | tf_op jit(solution)/shard_map/ppermute | solution.py:53
  25.7 1.5 %collective-permute-start.9 = (f32[32,1024]{1,0:T(8,128)S(1)}, f32[32,1024]{1,0:T(8,128)S(1)}, u32[]{:S(2)}, u32[]{:S(2)}) collective-permute-start(f32[32,1024]{1,0:T(8,128)S(1)} %get-tuple-element.59), channel_id=1, source_target_pairs={{0,2},{1,5},{2,0},{3,7},{4,6},{5,1},{6,4},{7,3},{8,10},{9,13},{10,... | collective-permute-start | bytes 393224 | tf_op jit(solution)/shard_map/ppermute | solution.py:53
  29.6 1.7 %collective-permute-done.9.refs_5_.refs_2_ = f32[32,1024]{1,0:T(8,128)S(1)} collective-permute-done((f32[32,1024]{1,0:T(8,128)S(1)}, f32[32,1024]{1,0:T(8,128)S(1)}, u32[]{:S(2)}, u32[]{:S(2)}) %collective-permute-start.9) | collective-permute-done | bytes 131104 | tf_op jit(solution)/shard_map/ppermute | solution.py:53
  32.8 1.5 %collective-permute-start.11 = (f32[8,64,128]{2,1,0:T(8,128)S(1)}, f32[8,64,128]{2,1,0:T(8,128)S(1)}, u32[]{:S(2)}, u32[]{:S(2)}) collective-permute-start(f32[8,64,128]{2,1,0:T(8,128)S(1)} %get-tuple-element.62), channel_id=1, source_target_pairs={{0,2},{1,5},{2,0},{3,7},{4,6},{5,1},{6,4},{7,3},{8,10},{9,13},{10,... | collective-permute-start | bytes 786440 | tf_op jit(solution)/shard_map/ppermute | solution.py:53
  35.0 1.6 %collective-permute-start.21 = (f32[8,64,128]{2,1,0:T(8,128)S(1)}, f32[8,64,128]{2,1,0:T(8,128)S(1)}, u32[]{:S(2)}, u32[]{:S(2)}) collective-permute-start(f32[8,64,128]{2,1,0:T(8,128)S(1)} %get-tuple-element.72), channel_id=1, source_target_pairs={{0,4},{1,3},{2,6},{3,1},{4,0},{5,7},{6,2},{7,5},{8,12},{9,11},{10,... | collective-permute-start | bytes 786440 | tf_op jit(solution)/shard_map/ppermute | solution.py:53
  38.1 3.4 %collective-permute-done.11 = f32[8,64,128]{2,1,0:T(8,128)S(1)} collective-permute-done((f32[8,64,128]{2,1,0:T(8,128)S(1)}, f32[8,64,128]{2,1,0:T(8,128)S(1)}, u32[]{:S(2)}, u32[]{:S(2)}) %collective-permute-start.11) | collective-permute-done | bytes 262176 | tf_op jit(solution)/shard_map/ppermute | solution.py:53
  41.6 2.1 %collective-permute-start.12 = (f32[4,64,128]{2,1,0:T(8,128)S(1)}, f32[4,64,128]{2,1,0:T(8,128)S(1)}, u32[]{:S(2)}, u32[]{:S(2)}) collective-permute-start(f32[4,64,128]{2,1,0:T(8,128)S(1)} %slice_add_fusion.6), channel_id=1, source_target_pairs={{0,4},{1,3},{2,6},{3,1},{4,0},{5,7},{6,2},{7,5},{8,12},{9,11},{10,... | collective-permute-start | bytes 393224 | tf_op jit(solution)/shard_map/ppermute | solution.py:53
  43.7 1.5 %collective-permute-start.22 = (f32[4,64,128]{2,1,0:T(8,128)S(1)}, f32[4,64,128]{2,1,0:T(8,128)S(1)}, u32[]{:S(2)}, u32[]{:S(2)}) collective-permute-start(f32[4,64,128]{2,1,0:T(8,128)S(1)} %slice_add_fusion.4), channel_id=1, source_target_pairs={{0,2},{1,5},{2,0},{3,7},{4,6},{5,1},{6,4},{7,3},{8,10},{9,13},{10,... | collective-permute-start | bytes 393224 | tf_op jit(solution)/shard_map/ppermute | solution.py:53
  45.2 2.2 %collective-permute-done.12 = f32[4,64,128]{2,1,0:T(8,128)S(1)} collective-permute-done((f32[4,64,128]{2,1,0:T(8,128)S(1)}, f32[4,64,128]{2,1,0:T(8,128)S(1)}, u32[]{:S(2)}, u32[]{:S(2)}) %collective-permute-start.12) | collective-permute-done | bytes 131104 | tf_op jit(solution)/shard_map/ppermute | solution.py:53
  47.4 1.6 %collective-permute-start.13 = (f32[2,64,128]{2,1,0:T(8,128)S(1)}, f32[2,64,128]{2,1,0:T(8,128)S(1)}, u32[]{:S(2)}, u32[]{:S(2)}) collective-permute-start(f32[2,64,128]{2,1,0:T(8,128)S(1)} %slice.137), channel_id=1, source_target_pairs={{0,8},{1,9},{2,10},{3,11},{4,12},{5,13},{6,14},{7,15},{8,0},{9,1},... | collective-permute-start | bytes 196616 | tf_op jit(solution)/shard_map/ppermute | solution.py:53
  52.4 2.2 %collective-permute-done.23 = f32[2,64,128]{2,1,0:T(8,128)S(1)} collective-permute-done((f32[2,64,128]{2,1,0:T(8,128)S(1)}, f32[2,64,128]{2,1,0:T(8,128)S(1)}, u32[]{:S(2)}, u32[]{:S(2)}) %collective-permute-start.23) | collective-permute-done | bytes 65568 | tf_op jit(solution)/shard_map/ppermute | solution.py:53
  54.9 2.2 %collective-permute-done.14 = f32[2,64,128]{2,1,0:T(8,128)S(1)} collective-permute-done((f32[2,64,128]{2,1,0:T(8,128)S(1)}, f32[2,64,128]{2,1,0:T(8,128)S(1)}, u32[]{:S(2)}, u32[]{:S(2)}) %collective-permute-start.14) | collective-permute-done | bytes 65568 | tf_op jit(solution)/shard_map/ppermute | solution.py:53
  57.1 2.2 %collective-permute-start.15 = (f32[2,64,128]{2,1,0:T(8,128)S(1)}, f32[2,64,128]{2,1,0:T(8,128)S(1)}, u32[]{:S(2)}, u32[]{:S(2)}) collective-permute-start(f32[2,64,128]{2,1,0:T(8,128)S(1)} %add.79), channel_id=1, source_target_pairs={{0,8},{1,9},{2,10},{3,11},{4,12},{5,13},{6,14},{7,15},{8,0},{9,1},... | collective-permute-start | bytes 196616 | tf_op jit(solution)/shard_map/ppermute | solution.py:53
  61.6 1.8 %collective-permute-start.16 = (f32[4,64,128]{2,1,0:T(8,128)S(1)}, f32[4,64,128]{2,1,0:T(8,128)S(1)}, u32[]{:S(2)}, u32[]{:S(2)}) collective-permute-start(f32[4,64,128]{2,1,0:T(8,128)S(1)} %pad_maximum_fusion.6), channel_id=1, source_target_pairs={{0,4},{1,3},{2,6},{3,1},{4,0},{5,7},{6,2},{7,5},{8,12},{9,11},{10,... | collective-permute-start | bytes 393224 | tf_op jit(solution)/shard_map/ppermute | solution.py:53
  63.4 1.6 %collective-permute-done.25 = f32[2,64,128]{2,1,0:T(8,128)S(1)} collective-permute-done((f32[2,64,128]{2,1,0:T(8,128)S(1)}, f32[2,64,128]{2,1,0:T(8,128)S(1)}, u32[]{:S(2)}, u32[]{:S(2)}) %collective-permute-start.25) | collective-permute-done | bytes 65568 | tf_op jit(solution)/shard_map/ppermute | solution.py:53
  64.9 1.5 %collective-permute-start.26 = (f32[4,64,128]{2,1,0:T(8,128)S(1)}, f32[4,64,128]{2,1,0:T(8,128)S(1)}, u32[]{:S(2)}, u32[]{:S(2)}) collective-permute-start(f32[4,64,128]{2,1,0:T(8,128)S(1)} %pad_maximum_fusion.7), channel_id=1, source_target_pairs={{0,2},{1,5},{2,0},{3,7},{4,6},{5,1},{6,4},{7,3},{8,10},{9,13},{10,... | collective-permute-start | bytes 393224 | tf_op jit(solution)/shard_map/ppermute | solution.py:53
  66.5 1.6 %collective-permute-done.16 = f32[4,64,128]{2,1,0:T(8,128)S(1)} collective-permute-done((f32[4,64,128]{2,1,0:T(8,128)S(1)}, f32[4,64,128]{2,1,0:T(8,128)S(1)}, u32[]{:S(2)}, u32[]{:S(2)}) %collective-permute-start.16) | collective-permute-done | bytes 131104 | tf_op jit(solution)/shard_map/ppermute | solution.py:53
  68.1 1.5 %collective-permute-start.17 = (f32[8,64,128]{2,1,0:T(8,128)S(1)}, f32[8,64,128]{2,1,0:T(8,128)S(1)}, u32[]{:S(2)}, u32[]{:S(2)}) collective-permute-start(f32[8,64,128]{2,1,0:T(8,128)S(1)} %pad_maximum_fusion.refs_1_), channel_id=1, source_target_pairs={{0,2},{1,5},{2,0},{3,7},{4,6},{5,1},{6,4},{7,3},{8,10},{9,13},{10,... | collective-permute-start | bytes 786440 | tf_op jit(solution)/shard_map/ppermute | solution.py:53
  69.6 1.8 %collective-permute-done.26 = f32[4,64,128]{2,1,0:T(8,128)S(1)} collective-permute-done((f32[4,64,128]{2,1,0:T(8,128)S(1)}, f32[4,64,128]{2,1,0:T(8,128)S(1)}, u32[]{:S(2)}, u32[]{:S(2)}) %collective-permute-start.26) | collective-permute-done | bytes 131104 | tf_op jit(solution)/shard_map/ppermute | solution.py:53
  71.5 1.4 collective-permute-start.27
  76.0 1.9 %collective-permute-done.27.refs_2_ = f32[8,64,128]{2,1,0:T(8,128)S(1)} collective-permute-done((f32[8,64,128]{2,1,0:T(8,128)S(1)}, f32[8,64,128]{2,1,0:T(8,128)S(1)}, u32[]{:S(2)}, u32[]{:S(2)}) %collective-permute-start.27) | collective-permute-done | bytes 262176 | tf_op jit(solution)/shard_map/ppermute | solution.py:53
  79.0 1.8 %collective-permute-done.29.refs_1_ = f32[2,4,64,128]{3,2,1,0:T(8,128)S(1)} collective-permute-done((f32[2,4,64,128]{3,2,1,0:T(8,128)S(1)}, f32[2,4,64,128]{3,2,1,0:T(8,128)S(1)}, u32[]{:S(2)}, u32[]{:S(2)}) %collective-permute-start.29) | collective-permute-done | bytes 262176 | tf_op jit(solution)/shard_map/ppermute | solution.py:53
  81.0 1.7 %collective-permute-start.43 = (f32[1,64,128]{2,1,0:T(8,128)S(1)}, f32[1,64,128]{2,1,0:T(8,128)S(1)}, u32[]{:S(2)}, u32[]{:S(2)}) collective-permute-start(f32[1,64,128]{2,1,0:T(8,128)S(1)} %add.91), channel_id=1, source_target_pairs={{0,16},{1,17},{2,18},{3,19},{4,20},{5,21},{6,22},{7,23},{8,24},{9,... | collective-permute-start | bytes 98312 | tf_op jit(solution)/shard_map/ppermute | solution.py:53
  84.0 2.0 %collective-permute-done.43 = f32[1,64,128]{2,1,0:T(8,128)S(1)} collective-permute-done((f32[1,64,128]{2,1,0:T(8,128)S(1)}, f32[1,64,128]{2,1,0:T(8,128)S(1)}, u32[]{:S(2)}, u32[]{:S(2)}) %collective-permute-start.43) | collective-permute-done | bytes 32800 | tf_op jit(solution)/shard_map/ppermute | solution.py:53
  86.0 2.8 %collective-permute-start.44 = (f32[2,64,128]{2,1,0:T(8,128)S(1)}, f32[2,64,128]{2,1,0:T(8,128)S(1)}, u32[]{:S(2)}, u32[]{:S(2)}) collective-permute-start(f32[2,64,128]{2,1,0:T(8,128)S(1)} %pad_maximum_fusion.15), channel_id=1, source_target_pairs={{0,8},{1,9},{2,10},{3,11},{4,12},{5,13},{6,14},{7,15},{8,0},{9,1},... | collective-permute-start | bytes 196616 | tf_op jit(solution)/shard_map/ppermute | solution.py:53
  88.9 1.4 collective-permute-start.34
  91.1 1.5 %collective-permute-start.45 = (f32[4,64,128]{2,1,0:T(8,128)S(1)}, f32[4,64,128]{2,1,0:T(8,128)S(1)}, u32[]{:S(2)}, u32[]{:S(2)}) collective-permute-start(f32[4,64,128]{2,1,0:T(8,128)S(1)} %pad_maximum_fusion.10), channel_id=1, source_target_pairs={{0,2},{1,5},{2,0},{3,7},{4,6},{5,1},{6,4},{7,3},{8,10},{9,13},{10,... | collective-permute-start | bytes 393224 | tf_op jit(solution)/shard_map/ppermute | solution.py:53
  92.6 1.7 %collective-permute-done.34 = f32[4,64,128]{2,1,0:T(8,128)S(1)} collective-permute-done((f32[4,64,128]{2,1,0:T(8,128)S(1)}, f32[4,64,128]{2,1,0:T(8,128)S(1)}, u32[]{:S(2)}, u32[]{:S(2)}) %collective-permute-start.34) | collective-permute-done | bytes 131104 | tf_op jit(solution)/shard_map/ppermute | solution.py:53
  94.3 1.5 %collective-permute-start.35 = (f32[8,64,128]{2,1,0:T(8,128)S(1)}, f32[8,64,128]{2,1,0:T(8,128)S(1)}, u32[]{:S(2)}, u32[]{:S(2)}) collective-permute-start(f32[8,64,128]{2,1,0:T(8,128)S(1)} %pad_maximum_fusion.2.refs_1_), channel_id=1, source_target_pairs={{0,2},{1,5},{2,0},{3,7},{4,6},{5,1},{6,4},{7,3},{8,10},{9,13},{10,... | collective-permute-start | bytes 786440 | tf_op jit(solution)/shard_map/ppermute | solution.py:53
  96.2 1.8 %collective-permute-start.46 = (f32[8,64,128]{2,1,0:T(8,128)S(1)}, f32[8,64,128]{2,1,0:T(8,128)S(1)}, u32[]{:S(2)}, u32[]{:S(2)}) collective-permute-start(f32[8,64,128]{2,1,0:T(8,128)S(1)} %pad_maximum_fusion.4.refs_1_), channel_id=1, source_target_pairs={{0,4},{1,3},{2,6},{3,1},{4,0},{5,7},{6,2},{7,5},{8,12},{9,11},{10,... | collective-permute-start | bytes 786440 | tf_op jit(solution)/shard_map/ppermute | solution.py:53
  98.0 5.4 %collective-permute-done.35.refs_2_ = f32[8,64,128]{2,1,0:T(8,128)S(1)} collective-permute-done((f32[8,64,128]{2,1,0:T(8,128)S(1)}, f32[8,64,128]{2,1,0:T(8,128)S(1)}, u32[]{:S(2)}, u32[]{:S(2)}) %collective-permute-start.35) | collective-permute-done | bytes 262176 | tf_op jit(solution)/shard_map/ppermute | solution.py:53
  106.8 1.4 collective-permute-start.37
  112.4 1.8 %collective-permute-start.48 = (f32[8,64,128]{2,1,0:T(8,128)S(1)}, f32[8,64,128]{2,1,0:T(8,128)S(1)}, u32[]{:S(2)}, u32[]{:S(2)}) collective-permute-start(f32[8,64,128]{2,1,0:T(8,128)S(1)} %get-tuple-element.88), channel_id=1, source_target_pairs={{0,4},{1,3},{2,6},{3,1},{4,0},{5,7},{6,2},{7,5},{8,12},{9,11},{10,... | collective-permute-start | bytes 786440 | tf_op jit(solution)/shard_map/ppermute | solution.py:53
  114.9 3.9 %collective-permute-done.48 = f32[8,64,128]{2,1,0:T(8,128)S(1)} collective-permute-done((f32[8,64,128]{2,1,0:T(8,128)S(1)}, f32[8,64,128]{2,1,0:T(8,128)S(1)}, u32[]{:S(2)}, u32[]{:S(2)}) %collective-permute-start.48) | collective-permute-done | bytes 262176 | tf_op jit(solution)/shard_map/ppermute | solution.py:53
  118.9 1.4 collective-permute-start.49
  120.9 3.0 %collective-permute-done.49 = f32[4,64,128]{2,1,0:T(8,128)S(1)} collective-permute-done((f32[4,64,128]{2,1,0:T(8,128)S(1)}, f32[4,64,128]{2,1,0:T(8,128)S(1)}, u32[]{:S(2)}, u32[]{:S(2)}) %collective-permute-start.49) | collective-permute-done | bytes 131104 | tf_op jit(solution)/shard_map/ppermute | solution.py:53
  124.5 1.4 collective-permute-done.39
  125.9 1.9 %collective-permute-start.40 = (f32[4,64,128]{2,1,0:T(8,128)S(1)}, f32[4,64,128]{2,1,0:T(8,128)S(1)}, u32[]{:S(2)}, u32[]{:S(2)}) collective-permute-start(f32[4,64,128]{2,1,0:T(8,128)S(1)} %add.90), channel_id=1, source_target_pairs={{0,4},{1,3},{2,6},{3,1},{4,0},{5,7},{6,2},{7,5},{8,12},{9,11},{10,... | collective-permute-start | bytes 393224 | tf_op jit(solution)/shard_map/ppermute | solution.py:53
  129.0 1.4 collective-permute-start.51
  130.4 2.0 %collective-permute-done.40 = f32[4,64,128]{2,1,0:T(8,128)S(1)} collective-permute-done((f32[4,64,128]{2,1,0:T(8,128)S(1)}, f32[4,64,128]{2,1,0:T(8,128)S(1)}, u32[]{:S(2)}, u32[]{:S(2)}) %collective-permute-start.40) | collective-permute-done | bytes 131104 | tf_op jit(solution)/shard_map/ppermute | solution.py:53
  134.1 1.8 %collective-permute-start.52 = (f32[8,64,128]{2,1,0:T(8,128)S(1)}, f32[8,64,128]{2,1,0:T(8,128)S(1)}, u32[]{:S(2)}, u32[]{:S(2)}) collective-permute-start(f32[8,64,128]{2,1,0:T(8,128)S(1)} %pad_maximum_fusion.5.refs_1_), channel_id=1, source_target_pairs={{0,4},{1,3},{2,6},{3,1},{4,0},{5,7},{6,2},{7,5},{8,12},{9,11},{10,... | collective-permute-start | bytes 786440 | tf_op jit(solution)/shard_map/ppermute | solution.py:53
  135.9 4.3 %collective-permute-done.41.refs_2_ = f32[8,64,128]{2,1,0:T(8,128)S(1)} collective-permute-done((f32[8,64,128]{2,1,0:T(8,128)S(1)}, f32[8,64,128]{2,1,0:T(8,128)S(1)}, u32[]{:S(2)}, u32[]{:S(2)}) %collective-permute-start.41) | collective-permute-done | bytes 262176 | tf_op jit(solution)/shard_map/ppermute | solution.py:53
  (145 shorter events, 40.1 us)
Async XLA Ops:
  2.5 3.2 %collective-permute-start.1 = (f32[32,1152]{1,0:T(8,128)S(1)}, f32[32,1152]{1,0:T(8,128)S(1)}, u32[]{:S(2)}, u32[]{:S(2)}) collective-permute-start(f32[32,1152]{1,0:T(8,128)S(1)} %get-tuple-element.52), channel_id=1, source_target_pairs={{0,1},{1,0},{2,3},{3,2},{4,5},{5,4},{6,7},{7,6},{8,9},{9,8},{10,11... | collective-permute-start | bytes 442376 | tf_op jit(solution)/shard_map/ppermute | solution.py:53
  3.0 6.3 %collective-permute-start.2 = (f32[32,1152]{1,0:T(8,128)S(1)}, f32[32,1152]{1,0:T(8,128)S(1)}, u32[]{:S(2)}, u32[]{:S(2)}) collective-permute-start(f32[32,1152]{1,0:T(8,128)S(1)} %get-tuple-element.53), channel_id=1, source_target_pairs={{0,2},{1,5},{2,0},{3,7},{4,6},{5,1},{6,4},{7,3},{8,10},{9,13},{10,... | collective-permute-start | bytes 442376 | tf_op jit(solution)/shard_map/ppermute | solution.py:53
  5.6 4.7 %collective-permute-start.3 = (f32[32,1152]{1,0:T(8,128)S(1)}, f32[32,1152]{1,0:T(8,128)S(1)}, u32[]{:S(2)}, u32[]{:S(2)}) collective-permute-start(f32[32,1152]{1,0:T(8,128)S(1)} %get-tuple-element.54), channel_id=1, source_target_pairs={{0,5},{1,2},{2,7},{3,0},{4,1},{5,6},{6,3},{7,4},{8,13},{9,10},{10,... | collective-permute-start | bytes 442376 | tf_op jit(solution)/shard_map/ppermute | solution.py:53
  10.8 6.5 %collective-permute-start.4 = (f32[2,4,64,128]{3,2,1,0:T(8,128)S(1)}, f32[2,4,64,128]{3,2,1,0:T(8,128)S(1)}, u32[]{:S(2)}, u32[]{:S(2)}) collective-permute-start(f32[2,4,64,128]{3,2,1,0:T(8,128)S(1)} %get-tuple-element.56), channel_id=1, source_target_pairs={{0,4},{1,3},{2,6},{3,1},{4,0},{5,7},{6,2},{7,5},{8,12},{9,11},{10,... | collective-permute-start | bytes 786440 | tf_op jit(solution)/shard_map/ppermute | solution.py:53
  17.4 5.1 %collective-permute-start.5 = (f32[2,2,64,128]{3,2,1,0:T(8,128)S(1)}, f32[2,2,64,128]{3,2,1,0:T(8,128)S(1)}, u32[]{:S(2)}, u32[]{:S(2)}) collective-permute-start(f32[2,2,64,128]{3,2,1,0:T(8,128)S(1)} %slice.129), channel_id=1, source_target_pairs={{0,8},{1,9},{2,10},{3,11},{4,12},{5,13},{6,14},{7,15},{8,0},{9,1},... | collective-permute-start | bytes 393224 | tf_op jit(solution)/shard_map/ppermute | solution.py:53
  19.6 9.6 %collective-permute-start = (f32[2048,128]{1,0:T(8,128)S(1)}, f32[2048,128]{1,0:T(8,128)S(1)}, u32[]{:S(2)}, u32[]{:S(2)}) collective-permute-start(f32[2048,128]{1,0:T(8,128)S(1)} %get-tuple-element.49), channel_id=1, source_target_pairs={{0,1},{1,0},{2,3},{3,2},{4,5},{5,4},{6,7},{7,6},{8,9},{9,8},{10,11... | collective-permute-start | bytes 3145736 | tf_op jit(solution)/shard_map/ppermute | solution.py:53
  22.5 5.3 %collective-permute-start.6 = (f32[2,1,64,128]{3,2,1,0:T(8,128)S(1)}, f32[2,1,64,128]{3,2,1,0:T(8,128)S(1)}, u32[]{:S(2)}, u32[]{:S(2)}) collective-permute-start(f32[2,1,64,128]{3,2,1,0:T(8,128)S(1)} %slice.131), channel_id=1, source_target_pairs={{0,16},{1,17},{2,18},{3,19},{4,20},{5,21},{6,22},{7,23},{8,24},{9,... | collective-permute-start | bytes 196616 | tf_op jit(solution)/shard_map/ppermute | solution.py:53
  25.6 4.0 %collective-permute-start.8 = (f32[32,1024]{1,0:T(8,128)S(1)}, f32[32,1024]{1,0:T(8,128)S(1)}, u32[]{:S(2)}, u32[]{:S(2)}) collective-permute-start(f32[32,1024]{1,0:T(8,128)S(1)} %get-tuple-element.58), channel_id=1, source_target_pairs={{0,1},{1,0},{2,3},{3,2},{4,5},{5,4},{6,7},{7,6},{8,9},{9,8},{10,11... | collective-permute-start | bytes 393224 | tf_op jit(solution)/shard_map/ppermute | solution.py:53
  25.7 5.6 %collective-permute-start.9 = (f32[32,1024]{1,0:T(8,128)S(1)}, f32[32,1024]{1,0:T(8,128)S(1)}, u32[]{:S(2)}, u32[]{:S(2)}) collective-permute-start(f32[32,1024]{1,0:T(8,128)S(1)} %get-tuple-element.59), channel_id=1, source_target_pairs={{0,2},{1,5},{2,0},{3,7},{4,6},{5,1},{6,4},{7,3},{8,10},{9,13},{10,... | collective-permute-start | bytes 393224 | tf_op jit(solution)/shard_map/ppermute | solution.py:53
  27.2 4.9 %collective-permute-start.10 = (f32[32,1024]{1,0:T(8,128)S(1)}, f32[32,1024]{1,0:T(8,128)S(1)}, u32[]{:S(2)}, u32[]{:S(2)}) collective-permute-start(f32[32,1024]{1,0:T(8,128)S(1)} %get-tuple-element.60), channel_id=1, source_target_pairs={{0,5},{1,2},{2,7},{3,0},{4,1},{5,6},{6,3},{7,4},{8,13},{9,10},{10,... | collective-permute-start | bytes 393224 | tf_op jit(solution)/shard_map/ppermute | solution.py:53
  32.8 8.7 %collective-permute-start.11 = (f32[8,64,128]{2,1,0:T(8,128)S(1)}, f32[8,64,128]{2,1,0:T(8,128)S(1)}, u32[]{:S(2)}, u32[]{:S(2)}) collective-permute-start(f32[8,64,128]{2,1,0:T(8,128)S(1)} %get-tuple-element.62), channel_id=1, source_target_pairs={{0,2},{1,5},{2,0},{3,7},{4,6},{5,1},{6,4},{7,3},{8,10},{9,13},{10,... | collective-permute-start | bytes 786440 | tf_op jit(solution)/shard_map/ppermute | solution.py:53
  35.0 8.7 %collective-permute-start.21 = (f32[8,64,128]{2,1,0:T(8,128)S(1)}, f32[8,64,128]{2,1,0:T(8,128)S(1)}, u32[]{:S(2)}, u32[]{:S(2)}) collective-permute-start(f32[8,64,128]{2,1,0:T(8,128)S(1)} %get-tuple-element.72), channel_id=1, source_target_pairs={{0,4},{1,3},{2,6},{3,1},{4,0},{5,7},{6,2},{7,5},{8,12},{9,11},{10,... | collective-permute-start | bytes 786440 | tf_op jit(solution)/shard_map/ppermute | solution.py:53
  36.8 37.4 %collective-permute-start.19 = (f32[2048,256]{1,0:T(8,128)S(1)}, f32[2048,256]{1,0:T(8,128)S(1)}, u32[]{:S(2)}, u32[]{:S(2)}) collective-permute-start(f32[2048,256]{1,0:T(8,128)S(1)} %get-tuple-element.67), channel_id=1, source_target_pairs={{0,1},{1,0},{2,3},{3,2},{4,5},{5,4},{6,7},{7,6},{8,9},{9,8},{10,11... | collective-permute-start | bytes 6291464 | tf_op jit(solution)/shard_map/ppermute | solution.py:53
  37.6 37.4 %collective-permute-start.18 = (f32[256,2048]{1,0:T(8,128)S(1)}, f32[256,2048]{1,0:T(8,128)S(1)}, u32[]{:S(2)}, u32[]{:S(2)}) collective-permute-start(f32[256,2048]{1,0:T(8,128)S(1)} %get-tuple-element.65), channel_id=1, source_target_pairs={{0,1},{1,0},{2,3},{3,2},{4,5},{5,4},{6,7},{7,6},{8,9},{9,8},{10,11... | collective-permute-start | bytes 6291464 | tf_op jit(solution)/shard_map/ppermute | solution.py:53
  41.6 5.8 %collective-permute-start.12 = (f32[4,64,128]{2,1,0:T(8,128)S(1)}, f32[4,64,128]{2,1,0:T(8,128)S(1)}, u32[]{:S(2)}, u32[]{:S(2)}) collective-permute-start(f32[4,64,128]{2,1,0:T(8,128)S(1)} %slice_add_fusion.6), channel_id=1, source_target_pairs={{0,4},{1,3},{2,6},{3,1},{4,0},{5,7},{6,2},{7,5},{8,12},{9,11},{10,... | collective-permute-start | bytes 393224 | tf_op jit(solution)/shard_map/ppermute | solution.py:53
  43.7 5.4 %collective-permute-start.22 = (f32[4,64,128]{2,1,0:T(8,128)S(1)}, f32[4,64,128]{2,1,0:T(8,128)S(1)}, u32[]{:S(2)}, u32[]{:S(2)}) collective-permute-start(f32[4,64,128]{2,1,0:T(8,128)S(1)} %slice_add_fusion.4), channel_id=1, source_target_pairs={{0,2},{1,5},{2,0},{3,7},{4,6},{5,1},{6,4},{7,3},{8,10},{9,13},{10,... | collective-permute-start | bytes 393224 | tf_op jit(solution)/shard_map/ppermute | solution.py:53
  47.4 4.3 %collective-permute-start.13 = (f32[2,64,128]{2,1,0:T(8,128)S(1)}, f32[2,64,128]{2,1,0:T(8,128)S(1)}, u32[]{:S(2)}, u32[]{:S(2)}) collective-permute-start(f32[2,64,128]{2,1,0:T(8,128)S(1)} %slice.137), channel_id=1, source_target_pairs={{0,8},{1,9},{2,10},{3,11},{4,12},{5,13},{6,14},{7,15},{8,0},{9,1},... | collective-permute-start | bytes 196616 | tf_op jit(solution)/shard_map/ppermute | solution.py:53
  49.1 5.5 %collective-permute-start.23 = (f32[2,64,128]{2,1,0:T(8,128)S(1)}, f32[2,64,128]{2,1,0:T(8,128)S(1)}, u32[]{:S(2)}, u32[]{:S(2)}) collective-permute-start(f32[2,64,128]{2,1,0:T(8,128)S(1)} %slice.145), channel_id=1, source_target_pairs={{0,8},{1,9},{2,10},{3,11},{4,12},{5,13},{6,14},{7,15},{8,0},{9,1},... | collective-permute-start | bytes 196616 | tf_op jit(solution)/shard_map/ppermute | solution.py:53
  51.8 5.3 %collective-permute-start.14 = (f32[2,64,128]{2,1,0:T(8,128)S(1)}, f32[2,64,128]{2,1,0:T(8,128)S(1)}, u32[]{:S(2)}, u32[]{:S(2)}) collective-permute-start(f32[2,64,128]{2,1,0:T(8,128)S(1)} %pad_maximum_fusion.12), channel_id=1, source_target_pairs={{0,16},{1,17},{2,18},{3,19},{4,20},{5,21},{6,22},{7,23},{8,24},{9,... | collective-permute-start | bytes 196616 | tf_op jit(solution)/shard_map/ppermute | solution.py:53
  54.6 5.9 %collective-permute-start.24 = (f32[2,64,128]{2,1,0:T(8,128)S(1)}, f32[2,64,128]{2,1,0:T(8,128)S(1)}, u32[]{:S(2)}, u32[]{:S(2)}) collective-permute-start(f32[2,64,128]{2,1,0:T(8,128)S(1)} %pad_maximum_fusion.13), channel_id=1, source_target_pairs={{0,16},{1,17},{2,18},{3,19},{4,20},{5,21},{6,22},{7,23},{8,24},{9,... | collective-permute-start | bytes 196616 | tf_op jit(solution)/shard_map/ppermute | solution.py:53
  57.1 4.5 %collective-permute-start.15 = (f32[2,64,128]{2,1,0:T(8,128)S(1)}, f32[2,64,128]{2,1,0:T(8,128)S(1)}, u32[]{:S(2)}, u32[]{:S(2)}) collective-permute-start(f32[2,64,128]{2,1,0:T(8,128)S(1)} %add.79), channel_id=1, source_target_pairs={{0,8},{1,9},{2,10},{3,11},{4,12},{5,13},{6,14},{7,15},{8,0},{9,1},... | collective-permute-start | bytes 196616 | tf_op jit(solution)/shard_map/ppermute | solution.py:53
  60.6 4.3 %collective-permute-start.25 = (f32[2,64,128]{2,1,0:T(8,128)S(1)}, f32[2,64,128]{2,1,0:T(8,128)S(1)}, u32[]{:S(2)}, u32[]{:S(2)}) collective-permute-start(f32[2,64,128]{2,1,0:T(8,128)S(1)} %add.84), channel_id=1, source_target_pairs={{0,8},{1,9},{2,10},{3,11},{4,12},{5,13},{6,14},{7,15},{8,0},{9,1},... | collective-permute-start | bytes 196616 | tf_op jit(solution)/shard_map/ppermute | solution.py:53
  61.6 6.5 %collective-permute-start.16 = (f32[4,64,128]{2,1,0:T(8,128)S(1)}, f32[4,64,128]{2,1,0:T(8,128)S(1)}, u32[]{:S(2)}, u32[]{:S(2)}) collective-permute-start(f32[4,64,128]{2,1,0:T(8,128)S(1)} %pad_maximum_fusion.6), channel_id=1, source_target_pairs={{0,4},{1,3},{2,6},{3,1},{4,0},{5,7},{6,2},{7,5},{8,12},{9,11},{10,... | collective-permute-start | bytes 393224 | tf_op jit(solution)/shard_map/ppermute | solution.py:53
  64.9 6.5 %collective-permute-start.26 = (f32[4,64,128]{2,1,0:T(8,128)S(1)}, f32[4,64,128]{2,1,0:T(8,128)S(1)}, u32[]{:S(2)}, u32[]{:S(2)}) collective-permute-start(f32[4,64,128]{2,1,0:T(8,128)S(1)} %pad_maximum_fusion.7), channel_id=1, source_target_pairs={{0,2},{1,5},{2,0},{3,7},{4,6},{5,1},{6,4},{7,3},{8,10},{9,13},{10,... | collective-permute-start | bytes 393224 | tf_op jit(solution)/shard_map/ppermute | solution.py:53
  68.1 7.1 %collective-permute-start.17 = (f32[8,64,128]{2,1,0:T(8,128)S(1)}, f32[8,64,128]{2,1,0:T(8,128)S(1)}, u32[]{:S(2)}, u32[]{:S(2)}) collective-permute-start(f32[8,64,128]{2,1,0:T(8,128)S(1)} %pad_maximum_fusion.refs_1_), channel_id=1, source_target_pairs={{0,2},{1,5},{2,0},{3,7},{4,6},{5,1},{6,4},{7,3},{8,10},{9,13},{10,... | collective-permute-start | bytes 786440 | tf_op jit(solution)/shard_map/ppermute | solution.py:53
  71.5 6.4 %collective-permute-start.27 = (f32[8,64,128]{2,1,0:T(8,128)S(1)}, f32[8,64,128]{2,1,0:T(8,128)S(1)}, u32[]{:S(2)}, u32[]{:S(2)}) collective-permute-start(f32[8,64,128]{2,1,0:T(8,128)S(1)} %pad_maximum_fusion.1.refs_1_), channel_id=1, source_target_pairs={{0,4},{1,3},{2,6},{3,1},{4,0},{5,7},{6,2},{7,5},{8,12},{9,11},{10,... | collective-permute-start | bytes 786440 | tf_op jit(solution)/shard_map/ppermute | solution.py:53
  73.4 7.3 %collective-permute-start.29 = (f32[2,4,64,128]{3,2,1,0:T(8,128)S(1)}, f32[2,4,64,128]{3,2,1,0:T(8,128)S(1)}, u32[]{:S(2)}, u32[]{:S(2)}) collective-permute-start(f32[2,4,64,128]{3,2,1,0:T(8,128)S(1)} %get-tuple-element.79), channel_id=1, source_target_pairs={{0,4},{1,3},{2,6},{3,1},{4,0},{5,7},{6,2},{7,5},{8,12},{9,11},{10,... | collective-permute-start | bytes 786440 | tf_op jit(solution)/shard_map/ppermute | solution.py:53
  75.9 2.8 %collective-permute-start.20 = (f32[1,64,128]{2,1,0:T(8,128)S(1)}, f32[1,64,128]{2,1,0:T(8,128)S(1)}, u32[]{:S(2)}, u32[]{:S(2)}) collective-permute-start(f32[1,64,128]{2,1,0:T(8,128)S(1)} %get-tuple-element.70), channel_id=1, source_target_pairs={{0,1},{1,0},{2,3},{3,2},{4,5},{5,4},{6,7},{7,6},{8,9},{9,8},{10,11... | collective-permute-start | bytes 98312 | tf_op jit(solution)/shard_map/ppermute | solution.py:53
  78.7 5.2 %collective-permute-start.32 = (f32[1,64,128]{2,1,0:T(8,128)S(1)}, f32[1,64,128]{2,1,0:T(8,128)S(1)}, u32[]{:S(2)}, u32[]{:S(2)}) collective-permute-start(f32[1,64,128]{2,1,0:T(8,128)S(1)} %add.86), channel_id=1, source_target_pairs={{0,16},{1,17},{2,18},{3,19},{4,20},{5,21},{6,22},{7,23},{8,24},{9,... | collective-permute-start | bytes 98312 | tf_op jit(solution)/shard_map/ppermute | solution.py:53
  80.7 9.5 %collective-permute-start.30 = (f32[2,2,64,128]{3,2,1,0:T(8,128)S(1)}, f32[2,2,64,128]{3,2,1,0:T(8,128)S(1)}, u32[]{:S(2)}, u32[]{:S(2)}) collective-permute-start(f32[2,2,64,128]{3,2,1,0:T(8,128)S(1)} %get-tuple-element.81), channel_id=1, source_target_pairs={{0,8},{1,9},{2,10},{3,11},{4,12},{5,13},{6,14},{7,15},{8,0},{9,1},... | collective-permute-start | bytes 393224 | tf_op jit(solution)/shard_map/ppermute | solution.py:53
  81.0 5.0 %collective-permute-start.43 = (f32[1,64,128]{2,1,0:T(8,128)S(1)}, f32[1,64,128]{2,1,0:T(8,128)S(1)}, u32[]{:S(2)}, u32[]{:S(2)}) collective-permute-start(f32[1,64,128]{2,1,0:T(8,128)S(1)} %add.91), channel_id=1, source_target_pairs={{0,16},{1,17},{2,18},{3,19},{4,20},{5,21},{6,22},{7,23},{8,24},{9,... | collective-permute-start | bytes 98312 | tf_op jit(solution)/shard_map/ppermute | solution.py:53
  83.9 4.9 %collective-permute-start.33 = (f32[2,64,128]{2,1,0:T(8,128)S(1)}, f32[2,64,128]{2,1,0:T(8,128)S(1)}, u32[]{:S(2)}, u32[]{:S(2)}) collective-permute-start(f32[2,64,128]{2,1,0:T(8,128)S(1)} %pad_maximum_fusion.14), channel_id=1, source_target_pairs={{0,8},{1,9},{2,10},{3,11},{4,12},{5,13},{6,14},{7,15},{8,0},{9,1},... | collective-permute-start | bytes 196616 | tf_op jit(solution)/shard_map/ppermute | solution.py:53
  86.0 5.1 %collective-permute-start.44 = (f32[2,64,128]{2,1,0:T(8,128)S(1)}, f32[2,64,128]{2,1,0:T(8,128)S(1)}, u32[]{:S(2)}, u32[]{:S(2)}) collective-permute-start(f32[2,64,128]{2,1,0:T(8,128)S(1)} %pad_maximum_fusion.15), channel_id=1, source_target_pairs={{0,8},{1,9},{2,10},{3,11},{4,12},{5,13},{6,14},{7,15},{8,0},{9,1},... | collective-permute-start | bytes 196616 | tf_op jit(solution)/shard_map/ppermute | solution.py:53
  88.9 5.4 %collective-permute-start.34 = (f32[4,64,128]{2,1,0:T(8,128)S(1)}, f32[4,64,128]{2,1,0:T(8,128)S(1)}, u32[]{:S(2)}, u32[]{:S(2)}) collective-permute-start(f32[4,64,128]{2,1,0:T(8,128)S(1)} %pad_maximum_fusion.8), channel_id=1, source_target_pairs={{0,4},{1,3},{2,6},{3,1},{4,0},{5,7},{6,2},{7,5},{8,12},{9,11},{10,... | collective-permute-start | bytes 393224 | tf_op jit(solution)/shard_map/ppermute | solution.py:53
  90.3 14.2 %collective-permute-start.31 = (f32[2,2,64,128]{3,2,1,0:T(8,128)S(1)}, f32[2,2,64,128]{3,2,1,0:T(8,128)S(1)}, u32[]{:S(2)}, u32[]{:S(2)}) collective-permute-start(f32[2,2,64,128]{3,2,1,0:T(8,128)S(1)} %add.85), channel_id=1, source_target_pairs={{0,1},{1,0},{2,3},{3,2},{4,5},{5,4},{6,7},{7,6},{8,9},{9,8},{10,11... | collective-permute-start | bytes 393224 | tf_op jit(solution)/shard_map/ppermute | solution.py:53
  91.1 5.0 %collective-permute-start.45 = (f32[4,64,128]{2,1,0:T(8,128)S(1)}, f32[4,64,128]{2,1,0:T(8,128)S(1)}, u32[]{:S(2)}, u32[]{:S(2)}) collective-permute-start(f32[4,64,128]{2,1,0:T(8,128)S(1)} %pad_maximum_fusion.10), channel_id=1, source_target_pairs={{0,2},{1,5},{2,0},{3,7},{4,6},{5,1},{6,4},{7,3},{8,10},{9,13},{10,... | collective-permute-start | bytes 393224 | tf_op jit(solution)/shard_map/ppermute | solution.py:53
  94.3 9.1 %collective-permute-start.35 = (f32[8,64,128]{2,1,0:T(8,128)S(1)}, f32[8,64,128]{2,1,0:T(8,128)S(1)}, u32[]{:S(2)}, u32[]{:S(2)}) collective-permute-start(f32[8,64,128]{2,1,0:T(8,128)S(1)} %pad_maximum_fusion.2.refs_1_), channel_id=1, source_target_pairs={{0,2},{1,5},{2,0},{3,7},{4,6},{5,1},{6,4},{7,3},{8,10},{9,13},{10,... | collective-permute-start | bytes 786440 | tf_op jit(solution)/shard_map/ppermute | solution.py:53
  96.2 12.0 %collective-permute-start.46 = (f32[8,64,128]{2,1,0:T(8,128)S(1)}, f32[8,64,128]{2,1,0:T(8,128)S(1)}, u32[]{:S(2)}, u32[]{:S(2)}) collective-permute-start(f32[8,64,128]{2,1,0:T(8,128)S(1)} %pad_maximum_fusion.4.refs_1_), channel_id=1, source_target_pairs={{0,4},{1,3},{2,6},{3,1},{4,0},{5,7},{6,2},{7,5},{8,12},{9,11},{10,... | collective-permute-start | bytes 786440 | tf_op jit(solution)/shard_map/ppermute | solution.py:53
  106.8 7.5 %collective-permute-start.37 = (f32[8,64,128]{2,1,0:T(8,128)S(1)}, f32[8,64,128]{2,1,0:T(8,128)S(1)}, u32[]{:S(2)}, u32[]{:S(2)}) collective-permute-start(f32[8,64,128]{2,1,0:T(8,128)S(1)} %get-tuple-element.83), channel_id=1, source_target_pairs={{0,2},{1,5},{2,0},{3,7},{4,6},{5,1},{6,4},{7,3},{8,10},{9,13},{10,... | collective-permute-start | bytes 786440 | tf_op jit(solution)/shard_map/ppermute | solution.py:53
  112.4 6.4 %collective-permute-start.48 = (f32[8,64,128]{2,1,0:T(8,128)S(1)}, f32[8,64,128]{2,1,0:T(8,128)S(1)}, u32[]{:S(2)}, u32[]{:S(2)}) collective-permute-start(f32[8,64,128]{2,1,0:T(8,128)S(1)} %get-tuple-element.88), channel_id=1, source_target_pairs={{0,4},{1,3},{2,6},{3,1},{4,0},{5,7},{6,2},{7,5},{8,12},{9,11},{10,... | collective-permute-start | bytes 786440 | tf_op jit(solution)/shard_map/ppermute | solution.py:53
  114.3 6.0 %collective-permute-start.38 = (f32[4,64,128]{2,1,0:T(8,128)S(1)}, f32[4,64,128]{2,1,0:T(8,128)S(1)}, u32[]{:S(2)}, u32[]{:S(2)}) collective-permute-start(f32[4,64,128]{2,1,0:T(8,128)S(1)} %slice_add_fusion.2), channel_id=1, source_target_pairs={{0,4},{1,3},{2,6},{3,1},{4,0},{5,7},{6,2},{7,5},{8,12},{9,11},{10,... | collective-permute-start | bytes 393224 | tf_op jit(solution)/shard_map/ppermute | solution.py:53
  118.9 5.0 %collective-permute-start.49 = (f32[4,64,128]{2,1,0:T(8,128)S(1)}, f32[4,64,128]{2,1,0:T(8,128)S(1)}, u32[]{:S(2)}, u32[]{:S(2)}) collective-permute-start(f32[4,64,128]{2,1,0:T(8,128)S(1)} %slice_add_fusion), channel_id=1, source_target_pairs={{0,2},{1,5},{2,0},{3,7},{4,6},{5,1},{6,4},{7,3},{8,10},{9,13},{10,... | collective-permute-start | bytes 393224 | tf_op jit(solution)/shard_map/ppermute | solution.py:53
  120.3 5.6 %collective-permute-start.39 = (f32[4,64,128]{2,1,0:T(8,128)S(1)}, f32[4,64,128]{2,1,0:T(8,128)S(1)}, u32[]{:S(2)}, u32[]{:S(2)}) collective-permute-start(f32[4,64,128]{2,1,0:T(8,128)S(1)} %pad_maximum_fusion.9), channel_id=1, source_target_pairs={{0,8},{1,9},{2,10},{3,11},{4,12},{5,13},{6,14},{7,15},{8,0},{9,1},... | collective-permute-start | bytes 393224 | tf_op jit(solution)/shard_map/ppermute | solution.py:53
  124.0 5.0 %collective-permute-start.50 = (f32[4,64,128]{2,1,0:T(8,128)S(1)}, f32[4,64,128]{2,1,0:T(8,128)S(1)}, u32[]{:S(2)}, u32[]{:S(2)}) collective-permute-start(f32[4,64,128]{2,1,0:T(8,128)S(1)} %pad_maximum_fusion.11), channel_id=1, source_target_pairs={{0,8},{1,9},{2,10},{3,11},{4,12},{5,13},{6,14},{7,15},{8,0},{9,1},... | collective-permute-start | bytes 393224 | tf_op jit(solution)/shard_map/ppermute | solution.py:53
  125.9 6.4 %collective-permute-start.40 = (f32[4,64,128]{2,1,0:T(8,128)S(1)}, f32[4,64,128]{2,1,0:T(8,128)S(1)}, u32[]{:S(2)}, u32[]{:S(2)}) collective-permute-start(f32[4,64,128]{2,1,0:T(8,128)S(1)} %add.90), channel_id=1, source_target_pairs={{0,4},{1,3},{2,6},{3,1},{4,0},{5,7},{6,2},{7,5},{8,12},{9,11},{10,... | collective-permute-start | bytes 393224 | tf_op jit(solution)/shard_map/ppermute | solution.py:53
  129.0 5.0 %collective-permute-start.51 = (f32[4,64,128]{2,1,0:T(8,128)S(1)}, f32[4,64,128]{2,1,0:T(8,128)S(1)}, u32[]{:S(2)}, u32[]{:S(2)}) collective-permute-start(f32[4,64,128]{2,1,0:T(8,128)S(1)} %add.95), channel_id=1, source_target_pairs={{0,2},{1,5},{2,0},{3,7},{4,6},{5,1},{6,4},{7,3},{8,10},{9,13},{10,... | collective-permute-start | bytes 393224 | tf_op jit(solution)/shard_map/ppermute | solution.py:53
  132.4 7.8 %collective-permute-start.41 = (f32[8,64,128]{2,1,0:T(8,128)S(1)}, f32[8,64,128]{2,1,0:T(8,128)S(1)}, u32[]{:S(2)}, u32[]{:S(2)}) collective-permute-start(f32[8,64,128]{2,1,0:T(8,128)S(1)} %pad_maximum_fusion.3.refs_1_), channel_id=1, source_target_pairs={{0,2},{1,5},{2,0},{3,7},{4,6},{5,1},{6,4},{7,3},{8,10},{9,13},{10,... | collective-permute-start | bytes 786440 | tf_op jit(solution)/shard_map/ppermute | solution.py:53
  134.1 7.3 %collective-permute-start.52 = (f32[8,64,128]{2,1,0:T(8,128)S(1)}, f32[8,64,128]{2,1,0:T(8,128)S(1)}, u32[]{:S(2)}, u32[]{:S(2)}) collective-permute-start(f32[8,64,128]{2,1,0:T(8,128)S(1)} %pad_maximum_fusion.5.refs_1_), channel_id=1, source_target_pairs={{0,4},{1,3},{2,6},{3,1},{4,0},{5,7},{6,2},{7,5},{8,12},{9,11},{10,... | collective-permute-start | bytes 786440 | tf_op jit(solution)/shard_map/ppermute | solution.py:53
  (13 other events, 64.1 us)
where the time goes:
time: 145 us
  waiting for transfers between devices  68.3 us (47%)
  starting transfers between devices  58 us (40%)
  Pallas kernels  13.9 us (10%)
  local copies, waits for them, and re-layouts  2.69 us (2%)
    ppermute x54, waiting for transfers between devices, permute(): return lax.ppermute(value, AXES, [(i, partner(i)) for i in range(32)])  68.3 us
    ppermute x54, starting transfers between devices, permute(): return lax.ppermute(value, AXES, [(i, partner(i)) for i in range(32)])  58 us
    pallas_call x23, Pallas kernels, kernel_call(): pl.pallas_call(ordered, out_shape=[jax.ShapeDtypeStruct(*o) for o in outs...  13.9 us
  transfers between devices with their start and end apart: 54, of which 36 were waited for; matrix products, arithmetic and copies ran while one was open for 0% of the time, Pallas kernels for 8%

commit v1 on v0

--- a/solution.py
+++ b/solution.py
@@ -339,9 +339,10 @@
     )
 
 
-def depth_sum(value):
+def depth_sum(value, after):
     value = value[:, :2] + swap_near(value[:, 2:])
-    return value[:, :1] + swap_far(value[:, 1:])
+    got = swap_far(value[:, 1:])
+    return glue(lambda v, g: (v[:, :1] + g,), value, got, after=after)[0]
 
 
 def plane_sum(send, follow, keep, chain):
@@ -397,11 +398,10 @@
         flops=2 * 128 * 1024 * 128,
     )
     got = swap_second(send)
-    load = depth_sum(keep + got)
-    load_other = swap_core(load)
-
     mids = kernel_call(prep_mid, [((32, 1024), F32)] * 4, [border[0]], after=[got])
     mids = [mids[0], swap_core(mids[1]), swap_first(mids[2]), swap_cross(mids[3])]
+    load = depth_sum(keep + got, mids)
+    load_other = swap_core(load)
 
     top_keep, top_send = kernel_call(
         halve_rows, [((half, 128), BF16), ((half, 128), F32)], [winv_top], after=ready[:1]
@@ -430,7 +430,7 @@
     chains = range(CHAINS)
     values = []
     for h in chains:
-        parts = run_forward(top_w, [load[h], load_other[h]], True, h, after=mids)
+        parts = run_forward(top_w, [load[h], load_other[h]], True, h)
         values.append(plane_sum(*parts, h)[0])
     keep, send = kernel_call(
         mid_load_kernel,

time: 145 us -> 143 us (0.986)
  waiting for transfers between devices: 68.3 us -> 53.2 us
  starting transfers between devices: 58 us -> 70.2 us
    ppermute x54, waiting for transfers between devices: 68.3 us -> 53.2 us  [permute(): return lax.ppermute(value, AXES, [(i, partner(i)) for i in range(32)])]
    ppermute x54, starting transfers between devices: 58 us -> 70.2 us  [permute(): return lax.ppermute(value, AXES, [(i, partner(i)) for i in range(32)])]
    pallas_call x23 -> x24, Pallas kernels: 13.9 us -> 13.9 us  [kernel_call(): pl.pallas_call(ordered, out_shape=[jax.ShapeDtypeStruct(*o) for o in outs...]
  transfers between devices with their start and end apart: 54 -> 54, of which waited for: 36 -> 32; matrix products, arithmetic and copies ran while one was open for 0% -> 0% of each run, Pallas kernels for 8% -> 8%
where the time goes in v1:
time: 143 us
  starting transfers between devices  70.2 us (49%)
  waiting for transfers between devices  53.2 us (37%)
  Pallas kernels  13.9 us (10%)
  local copies, waits for them, and re-layouts  3.91 us (3%)
    ppermute x54, starting transfers between devices, permute(): return lax.ppermute(value, AXES, [(i, partner(i)) for i in range(32)])  70.2 us
    ppermute x54, waiting for transfers between devices, permute(): return lax.ppermute(value, AXES, [(i, partner(i)) for i in range(32)])  53.2 us
    pallas_call x24, Pallas kernels, kernel_call(): pl.pallas_call(ordered, out_shape=[jax.ShapeDtypeStruct(*o) for o in outs...  13.9 us
    unnamed x14, local copies, waits for them, and re-layouts  3.81 us
  transfers between devices with their start and end apart: 54, of which 32 were waited for; matrix products, arithmetic and copies ran while one was open for 0% of the time, Pallas kernels for 8%

profile of v1, /device:TPU:0, one launch (start us, length us, event | category | flops | bytes accessed | tf_op | source)
XLA Modules:
  0.0 143.0 jit_solution(15870604826555786369)
XLA Ops:
  3.0 2.6 %collective-permute-start.2 = (f32[32,1152]{1,0:T(8,128)S(1)}, f32[32,1152]{1,0:T(8,128)S(1)}, u32[]{:S(2)}, u32[]{:S(2)}) collective-permute-start(f32[32,1152]{1,0:T(8,128)S(1)} %get-tuple-element.53), channel_id=1, source_target_pairs={{0,2},{1,5},{2,0},{3,7},{4,6},{5,1},{6,4},{7,3},{8,10},{9,13},{10,... | collective-permute-start | bytes 442376 | tf_op jit(solution)/shard_map/ppermute | solution.py:53
  5.6 3.6 %collective-permute-done.2.refs_2_ = f32[32,1152]{1,0:T(8,128)S(1)} collective-permute-done((f32[32,1152]{1,0:T(8,128)S(1)}, f32[32,1152]{1,0:T(8,128)S(1)}, u32[]{:S(2)}, u32[]{:S(2)}) %collective-permute-start.2) | collective-permute-done | bytes 147488 | tf_op jit(solution)/shard_map/ppermute | solution.py:53
  10.8 2.1 %collective-permute-start.4 = (f32[2,4,64,128]{3,2,1,0:T(8,128)S(1)}, f32[2,4,64,128]{3,2,1,0:T(8,128)S(1)}, u32[]{:S(2)}, u32[]{:S(2)}) collective-permute-start(f32[2,4,64,128]{3,2,1,0:T(8,128)S(1)} %get-tuple-element.56), channel_id=1, source_target_pairs={{0,4},{1,3},{2,6},{3,1},{4,0},{5,7},{6,2},{7,5},{8,12},{9,11},{10,... | collective-permute-start | bytes 786440 | tf_op jit(solution)/shard_map/ppermute | solution.py:53
  14.3 2.9 %collective-permute-done.4.refs_1_ = f32[2,4,64,128]{3,2,1,0:T(8,128)S(1)} collective-permute-done((f32[2,4,64,128]{3,2,1,0:T(8,128)S(1)}, f32[2,4,64,128]{3,2,1,0:T(8,128)S(1)}, u32[]{:S(2)}, u32[]{:S(2)}) %collective-permute-start.4) | collective-permute-done | bytes 262176 | tf_op jit(solution)/shard_map/ppermute | solution.py:53
  17.3 2.1 %collective-permute-start.5 = (f32[2,2,64,128]{3,2,1,0:T(8,128)S(1)}, f32[2,2,64,128]{3,2,1,0:T(8,128)S(1)}, u32[]{:S(2)}, u32[]{:S(2)}) collective-permute-start(f32[2,2,64,128]{3,2,1,0:T(8,128)S(1)} %slice.125), channel_id=1, source_target_pairs={{0,8},{1,9},{2,10},{3,11},{4,12},{5,13},{6,14},{7,15},{8,0},{9,1},... | collective-permute-start | bytes 393224 | tf_op jit(solution)/shard_map/ppermute | solution.py:53
  19.6 1.5 %collective-permute-start.8 = (f32[32,1024]{1,0:T(8,128)S(1)}, f32[32,1024]{1,0:T(8,128)S(1)}, u32[]{:S(2)}, u32[]{:S(2)}) collective-permute-start(f32[32,1024]{1,0:T(8,128)S(1)} %get-tuple-element.59), channel_id=1, source_target_pairs={{0,2},{1,5},{2,0},{3,7},{4,6},{5,1},{6,4},{7,3},{8,10},{9,13},{10,... | collective-permute-start | bytes 393224 | tf_op jit(solution)/shard_map/ppermute | solution.py:53
  22.5 3.1 %collective-permute-start.6 = (f32[2,1,64,128]{3,2,1,0:T(8,128)S(1)}, f32[2,1,64,128]{3,2,1,0:T(8,128)S(1)}, u32[]{:S(2)}, u32[]{:S(2)}) collective-permute-start(f32[2,1,64,128]{3,2,1,0:T(8,128)S(1)} %slice.126), channel_id=1, source_target_pairs={{0,16},{1,17},{2,18},{3,19},{4,20},{5,21},{6,22},{7,23},{8,24},{9,... | collective-permute-start | bytes 196616 | tf_op jit(solution)/shard_map/ppermute | solution.py:53
  26.1 1.7 %collective-permute-done.6.refs_1_ = f32[2,1,64,128]{3,2,1,0:T(8,128)S(1)} collective-permute-done((f32[2,1,64,128]{3,2,1,0:T(8,128)S(1)}, f32[2,1,64,128]{3,2,1,0:T(8,128)S(1)}, u32[]{:S(2)}, u32[]{:S(2)}) %collective-permute-start.6) | collective-permute-done | bytes 65568 | tf_op jit(solution)/shard_map/ppermute | solution.py:53
  30.2 1.5 %collective-permute-start.11 = (f32[8,64,128]{2,1,0:T(8,128)S(1)}, f32[8,64,128]{2,1,0:T(8,128)S(1)}, u32[]{:S(2)}, u32[]{:S(2)}) collective-permute-start(f32[8,64,128]{2,1,0:T(8,128)S(1)} %get-tuple-element.62), channel_id=1, source_target_pairs={{0,2},{1,5},{2,0},{3,7},{4,6},{5,1},{6,4},{7,3},{8,10},{9,13},{10,... | collective-permute-start | bytes 786440 | tf_op jit(solution)/shard_map/ppermute | solution.py:53
  32.4 1.9 %collective-permute-start.21 = (f32[8,64,128]{2,1,0:T(8,128)S(1)}, f32[8,64,128]{2,1,0:T(8,128)S(1)}, u32[]{:S(2)}, u32[]{:S(2)}) collective-permute-start(f32[8,64,128]{2,1,0:T(8,128)S(1)} %get-tuple-element.72), channel_id=1, source_target_pairs={{0,4},{1,3},{2,6},{3,1},{4,0},{5,7},{6,2},{7,5},{8,12},{9,11},{10,... | collective-permute-start | bytes 786440 | tf_op jit(solution)/shard_map/ppermute | solution.py:53
  35.9 2.0 %collective-permute-done.11 = f32[8,64,128]{2,1,0:T(8,128)S(1)} collective-permute-done((f32[8,64,128]{2,1,0:T(8,128)S(1)}, f32[8,64,128]{2,1,0:T(8,128)S(1)}, u32[]{:S(2)}, u32[]{:S(2)}) %collective-permute-start.11) | collective-permute-done | bytes 262176 | tf_op jit(solution)/shard_map/ppermute | solution.py:53
  38.0 3.5 %collective-permute-start.12 = (f32[4,64,128]{2,1,0:T(8,128)S(1)}, f32[4,64,128]{2,1,0:T(8,128)S(1)}, u32[]{:S(2)}, u32[]{:S(2)}) collective-permute-start(f32[4,64,128]{2,1,0:T(8,128)S(1)} %slice_add_fusion.6), channel_id=1, source_target_pairs={{0,4},{1,3},{2,6},{3,1},{4,0},{5,7},{6,2},{7,5},{8,12},{9,11},{10,... | collective-permute-start | bytes 393224 | tf_op jit(solution)/shard_map/ppermute | solution.py:53
  41.5 1.5 %collective-permute-start.22 = (f32[4,64,128]{2,1,0:T(8,128)S(1)}, f32[4,64,128]{2,1,0:T(8,128)S(1)}, u32[]{:S(2)}, u32[]{:S(2)}) collective-permute-start(f32[4,64,128]{2,1,0:T(8,128)S(1)} %slice_add_fusion.4), channel_id=1, source_target_pairs={{0,2},{1,5},{2,0},{3,7},{4,6},{5,1},{6,4},{7,3},{8,10},{9,13},{10,... | collective-permute-start | bytes 393224 | tf_op jit(solution)/shard_map/ppermute | solution.py:53
  43.0 2.1 %collective-permute-done.12 = f32[4,64,128]{2,1,0:T(8,128)S(1)} collective-permute-done((f32[4,64,128]{2,1,0:T(8,128)S(1)}, f32[4,64,128]{2,1,0:T(8,128)S(1)}, u32[]{:S(2)}, u32[]{:S(2)}) %collective-permute-start.12) | collective-permute-done | bytes 131104 | tf_op jit(solution)/shard_map/ppermute | solution.py:53
  45.1 1.7 %collective-permute-start.13 = (f32[2,64,128]{2,1,0:T(8,128)S(1)}, f32[2,64,128]{2,1,0:T(8,128)S(1)}, u32[]{:S(2)}, u32[]{:S(2)}) collective-permute-start(f32[2,64,128]{2,1,0:T(8,128)S(1)} %slice.132), channel_id=1, source_target_pairs={{0,8},{1,9},{2,10},{3,11},{4,12},{5,13},{6,14},{7,15},{8,0},{9,1},... | collective-permute-start | bytes 196616 | tf_op jit(solution)/shard_map/ppermute | solution.py:53
  48.0 1.4 collective-permute-done.13
  49.5 3.3 %collective-permute-start.14 = (f32[2,64,128]{2,1,0:T(8,128)S(1)}, f32[2,64,128]{2,1,0:T(8,128)S(1)}, u32[]{:S(2)}, u32[]{:S(2)}) collective-permute-start(f32[2,64,128]{2,1,0:T(8,128)S(1)} %pad_maximum_fusion.12), channel_id=1, source_target_pairs={{0,16},{1,17},{2,18},{3,19},{4,20},{5,21},{6,22},{7,23},{8,24},{9,... | collective-permute-start | bytes 196616 | tf_op jit(solution)/shard_map/ppermute | solution.py:53
  52.8 2.4 %collective-permute-start.24 = (f32[2,64,128]{2,1,0:T(8,128)S(1)}, f32[2,64,128]{2,1,0:T(8,128)S(1)}, u32[]{:S(2)}, u32[]{:S(2)}) collective-permute-start(f32[2,64,128]{2,1,0:T(8,128)S(1)} %pad_maximum_fusion.13), channel_id=1, source_target_pairs={{0,16},{1,17},{2,18},{3,19},{4,20},{5,21},{6,22},{7,23},{8,24},{9,... | collective-permute-start | bytes 196616 | tf_op jit(solution)/shard_map/ppermute | solution.py:53
  55.2 2.5 %collective-permute-start.15 = (f32[2,64,128]{2,1,0:T(8,128)S(1)}, f32[2,64,128]{2,1,0:T(8,128)S(1)}, u32[]{:S(2)}, u32[]{:S(2)}) collective-permute-start(f32[2,64,128]{2,1,0:T(8,128)S(1)} %add.75), channel_id=1, source_target_pairs={{0,8},{1,9},{2,10},{3,11},{4,12},{5,13},{6,14},{7,15},{8,0},{9,1},... | collective-permute-start | bytes 196616 | tf_op jit(solution)/shard_map/ppermute | solution.py:53
  58.0 2.1 %collective-permute-start.25 = (f32[2,64,128]{2,1,0:T(8,128)S(1)}, f32[2,64,128]{2,1,0:T(8,128)S(1)}, u32[]{:S(2)}, u32[]{:S(2)}) collective-permute-start(f32[2,64,128]{2,1,0:T(8,128)S(1)} %add.80), channel_id=1, source_target_pairs={{0,8},{1,9},{2,10},{3,11},{4,12},{5,13},{6,14},{7,15},{8,0},{9,1},... | collective-permute-start | bytes 196616 | tf_op jit(solution)/shard_map/ppermute | solution.py:53
  60.2 1.4 collective-permute-start.16
  62.4 1.5 %collective-permute-start.26 = (f32[4,64,128]{2,1,0:T(8,128)S(1)}, f32[4,64,128]{2,1,0:T(8,128)S(1)}, u32[]{:S(2)}, u32[]{:S(2)}) collective-permute-start(f32[4,64,128]{2,1,0:T(8,128)S(1)} %pad_maximum_fusion.7), channel_id=1, source_target_pairs={{0,2},{1,5},{2,0},{3,7},{4,6},{5,1},{6,4},{7,3},{8,10},{9,13},{10,... | collective-permute-start | bytes 393224 | tf_op jit(solution)/shard_map/ppermute | solution.py:53
  63.9 2.6 %collective-permute-done.16 = f32[4,64,128]{2,1,0:T(8,128)S(1)} collective-permute-done((f32[4,64,128]{2,1,0:T(8,128)S(1)}, f32[4,64,128]{2,1,0:T(8,128)S(1)}, u32[]{:S(2)}, u32[]{:S(2)}) %collective-permute-start.16) | collective-permute-done | bytes 131104 | tf_op jit(solution)/shard_map/ppermute | solution.py:53
  66.6 1.5 %collective-permute-start.17 = (f32[8,64,128]{2,1,0:T(8,128)S(1)}, f32[8,64,128]{2,1,0:T(8,128)S(1)}, u32[]{:S(2)}, u32[]{:S(2)}) collective-permute-start(f32[8,64,128]{2,1,0:T(8,128)S(1)} %pad_maximum_fusion.refs_1_), channel_id=1, source_target_pairs={{0,2},{1,5},{2,0},{3,7},{4,6},{5,1},{6,4},{7,3},{8,10},{9,13},{10,... | collective-permute-start | bytes 786440 | tf_op jit(solution)/shard_map/ppermute | solution.py:53
  69.0 1.4 collective-permute-start.27
  76.2 2.3 %collective-permute-start.32 = (f32[1,64,128]{2,1,0:T(8,128)S(1)}, f32[1,64,128]{2,1,0:T(8,128)S(1)}, u32[]{:S(2)}, u32[]{:S(2)}) collective-permute-start(f32[1,64,128]{2,1,0:T(8,128)S(1)} %add.82), channel_id=1, source_target_pairs={{0,16},{1,17},{2,18},{3,19},{4,20},{5,21},{6,22},{7,23},{8,24},{9,... | collective-permute-start | bytes 98312 | tf_op jit(solution)/shard_map/ppermute | solution.py:53
  78.6 1.7 %collective-permute-start.30 = (f32[2,2,64,128]{3,2,1,0:T(8,128)S(1)}, f32[2,2,64,128]{3,2,1,0:T(8,128)S(1)}, u32[]{:S(2)}, u32[]{:S(2)}) collective-permute-start(f32[2,2,64,128]{3,2,1,0:T(8,128)S(1)} %get-tuple-element.81), channel_id=1, source_target_pairs={{0,8},{1,9},{2,10},{3,11},{4,12},{5,13},{6,14},{7,15},{8,0},{9,1},... | collective-permute-start | bytes 393224 | tf_op jit(solution)/shard_map/ppermute | solution.py:53
  80.3 1.4 %collective-permute-start.43 = (f32[1,64,128]{2,1,0:T(8,128)S(1)}, f32[1,64,128]{2,1,0:T(8,128)S(1)}, u32[]{:S(2)}, u32[]{:S(2)}) collective-permute-start(f32[1,64,128]{2,1,0:T(8,128)S(1)} %add.87), channel_id=1, source_target_pairs={{0,16},{1,17},{2,18},{3,19},{4,20},{5,21},{6,22},{7,23},{8,24},{9,... | collective-permute-start | bytes 98312 | tf_op jit(solution)/shard_map/ppermute | solution.py:53
  81.8 1.6 %collective-permute-start.33 = (f32[2,64,128]{2,1,0:T(8,128)S(1)}, f32[2,64,128]{2,1,0:T(8,128)S(1)}, u32[]{:S(2)}, u32[]{:S(2)}) collective-permute-start(f32[2,64,128]{2,1,0:T(8,128)S(1)} %pad_maximum_fusion.14), channel_id=1, source_target_pairs={{0,8},{1,9},{2,10},{3,11},{4,12},{5,13},{6,14},{7,15},{8,0},{9,1},... | collective-permute-start | bytes 196616 | tf_op jit(solution)/shard_map/ppermute | solution.py:53
  83.4 1.9 %collective-permute-done.43 = f32[1,64,128]{2,1,0:T(8,128)S(1)} collective-permute-done((f32[1,64,128]{2,1,0:T(8,128)S(1)}, f32[1,64,128]{2,1,0:T(8,128)S(1)}, u32[]{:S(2)}, u32[]{:S(2)}) %collective-permute-start.43) | collective-permute-done | bytes 32800 | tf_op jit(solution)/shard_map/ppermute | solution.py:53
  85.3 1.9 %collective-permute-start.44 = (f32[2,64,128]{2,1,0:T(8,128)S(1)}, f32[2,64,128]{2,1,0:T(8,128)S(1)}, u32[]{:S(2)}, u32[]{:S(2)}) collective-permute-start(f32[2,64,128]{2,1,0:T(8,128)S(1)} %pad_maximum_fusion.15), channel_id=1, source_target_pairs={{0,8},{1,9},{2,10},{3,11},{4,12},{5,13},{6,14},{7,15},{8,0},{9,1},... | collective-permute-start | bytes 196616 | tf_op jit(solution)/shard_map/ppermute | solution.py:53
  87.2 1.4 collective-permute-start.34
  89.6 1.5 %collective-permute-start.45 = (f32[4,64,128]{2,1,0:T(8,128)S(1)}, f32[4,64,128]{2,1,0:T(8,128)S(1)}, u32[]{:S(2)}, u32[]{:S(2)}) collective-permute-start(f32[4,64,128]{2,1,0:T(8,128)S(1)} %pad_maximum_fusion.10), channel_id=1, source_target_pairs={{0,2},{1,5},{2,0},{3,7},{4,6},{5,1},{6,4},{7,3},{8,10},{9,13},{10,... | collective-permute-start | bytes 393224 | tf_op jit(solution)/shard_map/ppermute | solution.py:53
  91.1 1.5 %collective-permute-done.34 = f32[4,64,128]{2,1,0:T(8,128)S(1)} collective-permute-done((f32[4,64,128]{2,1,0:T(8,128)S(1)}, f32[4,64,128]{2,1,0:T(8,128)S(1)}, u32[]{:S(2)}, u32[]{:S(2)}) %collective-permute-start.34) | collective-permute-done | bytes 131104 | tf_op jit(solution)/shard_map/ppermute | solution.py:53
  92.6 1.5 %collective-permute-start.35 = (f32[8,64,128]{2,1,0:T(8,128)S(1)}, f32[8,64,128]{2,1,0:T(8,128)S(1)}, u32[]{:S(2)}, u32[]{:S(2)}) collective-permute-start(f32[8,64,128]{2,1,0:T(8,128)S(1)} %pad_maximum_fusion.2.refs_1_), channel_id=1, source_target_pairs={{0,2},{1,5},{2,0},{3,7},{4,6},{5,1},{6,4},{7,3},{8,10},{9,13},{10,... | collective-permute-start | bytes 786440 | tf_op jit(solution)/shard_map/ppermute | solution.py:53
  94.6 1.7 %collective-permute-start.46 = (f32[8,64,128]{2,1,0:T(8,128)S(1)}, f32[8,64,128]{2,1,0:T(8,128)S(1)}, u32[]{:S(2)}, u32[]{:S(2)}) collective-permute-start(f32[8,64,128]{2,1,0:T(8,128)S(1)} %pad_maximum_fusion.4.refs_1_), channel_id=1, source_target_pairs={{0,4},{1,3},{2,6},{3,1},{4,0},{5,7},{6,2},{7,5},{8,12},{9,11},{10,... | collective-permute-start | bytes 786440 | tf_op jit(solution)/shard_map/ppermute | solution.py:53
  96.3 5.3 %collective-permute-done.35.refs_2_ = f32[8,64,128]{2,1,0:T(8,128)S(1)} collective-permute-done((f32[8,64,128]{2,1,0:T(8,128)S(1)}, f32[8,64,128]{2,1,0:T(8,128)S(1)}, u32[]{:S(2)}, u32[]{:S(2)}) %collective-permute-start.35) | collective-permute-done | bytes 262176 | tf_op jit(solution)/shard_map/ppermute | solution.py:53
  102.8 1.3 collective-permute-done.36.refs_4_
  105.0 1.5 %collective-permute-start.37 = (f32[8,64,128]{2,1,0:T(8,128)S(1)}, f32[8,64,128]{2,1,0:T(8,128)S(1)}, u32[]{:S(2)}, u32[]{:S(2)}) collective-permute-start(f32[8,64,128]{2,1,0:T(8,128)S(1)} %get-tuple-element.83), channel_id=1, source_target_pairs={{0,2},{1,5},{2,0},{3,7},{4,6},{5,1},{6,4},{7,3},{8,10},{9,13},{10,... | collective-permute-start | bytes 786440 | tf_op jit(solution)/shard_map/ppermute | solution.py:53
  110.8 1.8 %collective-permute-start.48 = (f32[8,64,128]{2,1,0:T(8,128)S(1)}, f32[8,64,128]{2,1,0:T(8,128)S(1)}, u32[]{:S(2)}, u32[]{:S(2)}) collective-permute-start(f32[8,64,128]{2,1,0:T(8,128)S(1)} %get-tuple-element.88), channel_id=1, source_target_pairs={{0,4},{1,3},{2,6},{3,1},{4,0},{5,7},{6,2},{7,5},{8,12},{9,11},{10,... | collective-permute-start | bytes 786440 | tf_op jit(solution)/shard_map/ppermute | solution.py:53
  113.3 3.9 %collective-permute-done.48 = f32[8,64,128]{2,1,0:T(8,128)S(1)} collective-permute-done((f32[8,64,128]{2,1,0:T(8,128)S(1)}, f32[8,64,128]{2,1,0:T(8,128)S(1)}, u32[]{:S(2)}, u32[]{:S(2)}) %collective-permute-start.48) | collective-permute-done | bytes 262176 | tf_op jit(solution)/shard_map/ppermute | solution.py:53
  119.3 3.0 %collective-permute-done.49 = f32[4,64,128]{2,1,0:T(8,128)S(1)} collective-permute-done((f32[4,64,128]{2,1,0:T(8,128)S(1)}, f32[4,64,128]{2,1,0:T(8,128)S(1)}, u32[]{:S(2)}, u32[]{:S(2)}) %collective-permute-start.49) | collective-permute-done | bytes 131104 | tf_op jit(solution)/shard_map/ppermute | solution.py:53
  123.0 1.4 collective-permute-done.39
  124.4 1.8 %collective-permute-start.40 = (f32[4,64,128]{2,1,0:T(8,128)S(1)}, f32[4,64,128]{2,1,0:T(8,128)S(1)}, u32[]{:S(2)}, u32[]{:S(2)}) collective-permute-start(f32[4,64,128]{2,1,0:T(8,128)S(1)} %add.86), channel_id=1, source_target_pairs={{0,4},{1,3},{2,6},{3,1},{4,0},{5,7},{6,2},{7,5},{8,12},{9,11},{10,... | collective-permute-start | bytes 393224 | tf_op jit(solution)/shard_map/ppermute | solution.py:53
  127.4 1.3 collective-permute-start.51
  128.7 2.0 %collective-permute-done.40 = f32[4,64,128]{2,1,0:T(8,128)S(1)} collective-permute-done((f32[4,64,128]{2,1,0:T(8,128)S(1)}, f32[4,64,128]{2,1,0:T(8,128)S(1)}, u32[]{:S(2)}, u32[]{:S(2)}) %collective-permute-start.40) | collective-permute-done | bytes 131104 | tf_op jit(solution)/shard_map/ppermute | solution.py:53
  132.5 1.8 %collective-permute-start.52 = (f32[8,64,128]{2,1,0:T(8,128)S(1)}, f32[8,64,128]{2,1,0:T(8,128)S(1)}, u32[]{:S(2)}, u32[]{:S(2)}) collective-permute-start(f32[8,64,128]{2,1,0:T(8,128)S(1)} %pad_maximum_fusion.5.refs_1_), channel_id=1, source_target_pairs={{0,4},{1,3},{2,6},{3,1},{4,0},{5,7},{6,2},{7,5},{8,12},{9,11},{10,... | collective-permute-start | bytes 786440 | tf_op jit(solution)/shard_map/ppermute | solution.py:53
  134.3 4.3 %collective-permute-done.41.refs_2_ = f32[8,64,128]{2,1,0:T(8,128)S(1)} collective-permute-done((f32[8,64,128]{2,1,0:T(8,128)S(1)}, f32[8,64,128]{2,1,0:T(8,128)S(1)}, u32[]{:S(2)}, u32[]{:S(2)}) %collective-permute-start.41) | collective-permute-done | bytes 262176 | tf_op jit(solution)/shard_map/ppermute | solution.py:53
  (145 shorter events, 39.7 us)
Async XLA Ops:
  2.5 3.2 %collective-permute-start.1 = (f32[32,1152]{1,0:T(8,128)S(1)}, f32[32,1152]{1,0:T(8,128)S(1)}, u32[]{:S(2)}, u32[]{:S(2)}) collective-permute-start(f32[32,1152]{1,0:T(8,128)S(1)} %get-tuple-element.52), channel_id=1, source_target_pairs={{0,1},{1,0},{2,3},{3,2},{4,5},{5,4},{6,7},{7,6},{8,9},{9,8},{10,11... | collective-permute-start | bytes 442376 | tf_op jit(solution)/shard_map/ppermute | solution.py:53
  3.0 6.3 %collective-permute-start.2 = (f32[32,1152]{1,0:T(8,128)S(1)}, f32[32,1152]{1,0:T(8,128)S(1)}, u32[]{:S(2)}, u32[]{:S(2)}) collective-permute-start(f32[32,1152]{1,0:T(8,128)S(1)} %get-tuple-element.53), channel_id=1, source_target_pairs={{0,2},{1,5},{2,0},{3,7},{4,6},{5,1},{6,4},{7,3},{8,10},{9,13},{10,... | collective-permute-start | bytes 442376 | tf_op jit(solution)/shard_map/ppermute | solution.py:53
  5.5 4.7 %collective-permute-start.3 = (f32[32,1152]{1,0:T(8,128)S(1)}, f32[32,1152]{1,0:T(8,128)S(1)}, u32[]{:S(2)}, u32[]{:S(2)}) collective-permute-start(f32[32,1152]{1,0:T(8,128)S(1)} %get-tuple-element.54), channel_id=1, source_target_pairs={{0,5},{1,2},{2,7},{3,0},{4,1},{5,6},{6,3},{7,4},{8,13},{9,10},{10,... | collective-permute-start | bytes 442376 | tf_op jit(solution)/shard_map/ppermute | solution.py:53
  10.8 6.5 %collective-permute-start.4 = (f32[2,4,64,128]{3,2,1,0:T(8,128)S(1)}, f32[2,4,64,128]{3,2,1,0:T(8,128)S(1)}, u32[]{:S(2)}, u32[]{:S(2)}) collective-permute-start(f32[2,4,64,128]{3,2,1,0:T(8,128)S(1)} %get-tuple-element.56), channel_id=1, source_target_pairs={{0,4},{1,3},{2,6},{3,1},{4,0},{5,7},{6,2},{7,5},{8,12},{9,11},{10,... | collective-permute-start | bytes 786440 | tf_op jit(solution)/shard_map/ppermute | solution.py:53
  14.3 14.9 %collective-permute-start = (f32[2048,128]{1,0:T(8,128)S(1)}, f32[2048,128]{1,0:T(8,128)S(1)}, u32[]{:S(2)}, u32[]{:S(2)}) collective-permute-start(f32[2048,128]{1,0:T(8,128)S(1)} %get-tuple-element.49), channel_id=1, source_target_pairs={{0,1},{1,0},{2,3},{3,2},{4,5},{5,4},{6,7},{7,6},{8,9},{9,8},{10,11... | collective-permute-start | bytes 3145736 | tf_op jit(solution)/shard_map/ppermute | solution.py:53
  17.3 5.1 %collective-permute-start.5 = (f32[2,2,64,128]{3,2,1,0:T(8,128)S(1)}, f32[2,2,64,128]{3,2,1,0:T(8,128)S(1)}, u32[]{:S(2)}, u32[]{:S(2)}) collective-permute-start(f32[2,2,64,128]{3,2,1,0:T(8,128)S(1)} %slice.125), channel_id=1, source_target_pairs={{0,8},{1,9},{2,10},{3,11},{4,12},{5,13},{6,14},{7,15},{8,0},{9,1},... | collective-permute-start | bytes 393224 | tf_op jit(solution)/shard_map/ppermute | solution.py:53
  19.5 6.0 %collective-permute-start.7 = (f32[32,1024]{1,0:T(8,128)S(1)}, f32[32,1024]{1,0:T(8,128)S(1)}, u32[]{:S(2)}, u32[]{:S(2)}) collective-permute-start(f32[32,1024]{1,0:T(8,128)S(1)} %get-tuple-element.58), channel_id=1, source_target_pairs={{0,1},{1,0},{2,3},{3,2},{4,5},{5,4},{6,7},{7,6},{8,9},{9,8},{10,11... | collective-permute-start | bytes 393224 | tf_op jit(solution)/shard_map/ppermute | solution.py:53
  19.6 5.9 %collective-permute-start.8 = (f32[32,1024]{1,0:T(8,128)S(1)}, f32[32,1024]{1,0:T(8,128)S(1)}, u32[]{:S(2)}, u32[]{:S(2)}) collective-permute-start(f32[32,1024]{1,0:T(8,128)S(1)} %get-tuple-element.59), channel_id=1, source_target_pairs={{0,2},{1,5},{2,0},{3,7},{4,6},{5,1},{6,4},{7,3},{8,10},{9,13},{10,... | collective-permute-start | bytes 393224 | tf_op jit(solution)/shard_map/ppermute | solution.py:53
  21.1 4.9 %collective-permute-start.9 = (f32[32,1024]{1,0:T(8,128)S(1)}, f32[32,1024]{1,0:T(8,128)S(1)}, u32[]{:S(2)}, u32[]{:S(2)}) collective-permute-start(f32[32,1024]{1,0:T(8,128)S(1)} %get-tuple-element.60), channel_id=1, source_target_pairs={{0,5},{1,2},{2,7},{3,0},{4,1},{5,6},{6,3},{7,4},{8,13},{9,10},{10,... | collective-permute-start | bytes 393224 | tf_op jit(solution)/shard_map/ppermute | solution.py:53
  22.5 5.3 %collective-permute-start.6 = (f32[2,1,64,128]{3,2,1,0:T(8,128)S(1)}, f32[2,1,64,128]{3,2,1,0:T(8,128)S(1)}, u32[]{:S(2)}, u32[]{:S(2)}) collective-permute-start(f32[2,1,64,128]{3,2,1,0:T(8,128)S(1)} %slice.126), channel_id=1, source_target_pairs={{0,16},{1,17},{2,18},{3,19},{4,20},{5,21},{6,22},{7,23},{8,24},{9,... | collective-permute-start | bytes 196616 | tf_op jit(solution)/shard_map/ppermute | solution.py:53
  30.2 7.7 %collective-permute-start.11 = (f32[8,64,128]{2,1,0:T(8,128)S(1)}, f32[8,64,128]{2,1,0:T(8,128)S(1)}, u32[]{:S(2)}, u32[]{:S(2)}) collective-permute-start(f32[8,64,128]{2,1,0:T(8,128)S(1)} %get-tuple-element.62), channel_id=1, source_target_pairs={{0,2},{1,5},{2,0},{3,7},{4,6},{5,1},{6,4},{7,3},{8,10},{9,13},{10,... | collective-permute-start | bytes 786440 | tf_op jit(solution)/shard_map/ppermute | solution.py:53
  32.4 9.0 %collective-permute-start.21 = (f32[8,64,128]{2,1,0:T(8,128)S(1)}, f32[8,64,128]{2,1,0:T(8,128)S(1)}, u32[]{:S(2)}, u32[]{:S(2)}) collective-permute-start(f32[8,64,128]{2,1,0:T(8,128)S(1)} %get-tuple-element.72), channel_id=1, source_target_pairs={{0,4},{1,3},{2,6},{3,1},{4,0},{5,7},{6,2},{7,5},{8,12},{9,11},{10,... | collective-permute-start | bytes 786440 | tf_op jit(solution)/shard_map/ppermute | solution.py:53
  34.5 37.1 %collective-permute-start.19 = (f32[2048,256]{1,0:T(8,128)S(1)}, f32[2048,256]{1,0:T(8,128)S(1)}, u32[]{:S(2)}, u32[]{:S(2)}) collective-permute-start(f32[2048,256]{1,0:T(8,128)S(1)} %get-tuple-element.67), channel_id=1, source_target_pairs={{0,1},{1,0},{2,3},{3,2},{4,5},{5,4},{6,7},{7,6},{8,9},{9,8},{10,11... | collective-permute-start | bytes 6291464 | tf_op jit(solution)/shard_map/ppermute | solution.py:53
  35.4 37.1 %collective-permute-start.18 = (f32[256,2048]{1,0:T(8,128)S(1)}, f32[256,2048]{1,0:T(8,128)S(1)}, u32[]{:S(2)}, u32[]{:S(2)}) collective-permute-start(f32[256,2048]{1,0:T(8,128)S(1)} %get-tuple-element.65), channel_id=1, source_target_pairs={{0,1},{1,0},{2,3},{3,2},{4,5},{5,4},{6,7},{7,6},{8,9},{9,8},{10,11... | collective-permute-start | bytes 6291464 | tf_op jit(solution)/shard_map/ppermute | solution.py:53
  38.0 7.1 %collective-permute-start.12 = (f32[4,64,128]{2,1,0:T(8,128)S(1)}, f32[4,64,128]{2,1,0:T(8,128)S(1)}, u32[]{:S(2)}, u32[]{:S(2)}) collective-permute-start(f32[4,64,128]{2,1,0:T(8,128)S(1)} %slice_add_fusion.6), channel_id=1, source_target_pairs={{0,4},{1,3},{2,6},{3,1},{4,0},{5,7},{6,2},{7,5},{8,12},{9,11},{10,... | collective-permute-start | bytes 393224 | tf_op jit(solution)/shard_map/ppermute | solution.py:53
  41.5 5.4 %collective-permute-start.22 = (f32[4,64,128]{2,1,0:T(8,128)S(1)}, f32[4,64,128]{2,1,0:T(8,128)S(1)}, u32[]{:S(2)}, u32[]{:S(2)}) collective-permute-start(f32[4,64,128]{2,1,0:T(8,128)S(1)} %slice_add_fusion.4), channel_id=1, source_target_pairs={{0,2},{1,5},{2,0},{3,7},{4,6},{5,1},{6,4},{7,3},{8,10},{9,13},{10,... | collective-permute-start | bytes 393224 | tf_op jit(solution)/shard_map/ppermute | solution.py:53
  45.1 4.3 %collective-permute-start.13 = (f32[2,64,128]{2,1,0:T(8,128)S(1)}, f32[2,64,128]{2,1,0:T(8,128)S(1)}, u32[]{:S(2)}, u32[]{:S(2)}) collective-permute-start(f32[2,64,128]{2,1,0:T(8,128)S(1)} %slice.132), channel_id=1, source_target_pairs={{0,8},{1,9},{2,10},{3,11},{4,12},{5,13},{6,14},{7,15},{8,0},{9,1},... | collective-permute-start | bytes 196616 | tf_op jit(solution)/shard_map/ppermute | solution.py:53
  46.9 5.8 %collective-permute-start.23 = (f32[2,64,128]{2,1,0:T(8,128)S(1)}, f32[2,64,128]{2,1,0:T(8,128)S(1)}, u32[]{:S(2)}, u32[]{:S(2)}) collective-permute-start(f32[2,64,128]{2,1,0:T(8,128)S(1)} %slice.140), channel_id=1, source_target_pairs={{0,8},{1,9},{2,10},{3,11},{4,12},{5,13},{6,14},{7,15},{8,0},{9,1},... | collective-permute-start | bytes 196616 | tf_op jit(solution)/shard_map/ppermute | solution.py:53
  49.5 5.7 %collective-permute-start.14 = (f32[2,64,128]{2,1,0:T(8,128)S(1)}, f32[2,64,128]{2,1,0:T(8,128)S(1)}, u32[]{:S(2)}, u32[]{:S(2)}) collective-permute-start(f32[2,64,128]{2,1,0:T(8,128)S(1)} %pad_maximum_fusion.12), channel_id=1, source_target_pairs={{0,16},{1,17},{2,18},{3,19},{4,20},{5,21},{6,22},{7,23},{8,24},{9,... | collective-permute-start | bytes 196616 | tf_op jit(solution)/shard_map/ppermute | solution.py:53
  52.8 5.2 %collective-permute-start.24 = (f32[2,64,128]{2,1,0:T(8,128)S(1)}, f32[2,64,128]{2,1,0:T(8,128)S(1)}, u32[]{:S(2)}, u32[]{:S(2)}) collective-permute-start(f32[2,64,128]{2,1,0:T(8,128)S(1)} %pad_maximum_fusion.13), channel_id=1, source_target_pairs={{0,16},{1,17},{2,18},{3,19},{4,20},{5,21},{6,22},{7,23},{8,24},{9,... | collective-permute-start | bytes 196616 | tf_op jit(solution)/shard_map/ppermute | solution.py:53
  55.2 5.0 %collective-permute-start.15 = (f32[2,64,128]{2,1,0:T(8,128)S(1)}, f32[2,64,128]{2,1,0:T(8,128)S(1)}, u32[]{:S(2)}, u32[]{:S(2)}) collective-permute-start(f32[2,64,128]{2,1,0:T(8,128)S(1)} %add.75), channel_id=1, source_target_pairs={{0,8},{1,9},{2,10},{3,11},{4,12},{5,13},{6,14},{7,15},{8,0},{9,1},... | collective-permute-start | bytes 196616 | tf_op jit(solution)/shard_map/ppermute | solution.py:53
  58.0 4.4 %collective-permute-start.25 = (f32[2,64,128]{2,1,0:T(8,128)S(1)}, f32[2,64,128]{2,1,0:T(8,128)S(1)}, u32[]{:S(2)}, u32[]{:S(2)}) collective-permute-start(f32[2,64,128]{2,1,0:T(8,128)S(1)} %add.80), channel_id=1, source_target_pairs={{0,8},{1,9},{2,10},{3,11},{4,12},{5,13},{6,14},{7,15},{8,0},{9,1},... | collective-permute-start | bytes 196616 | tf_op jit(solution)/shard_map/ppermute | solution.py:53
  60.2 6.4 %collective-permute-start.16 = (f32[4,64,128]{2,1,0:T(8,128)S(1)}, f32[4,64,128]{2,1,0:T(8,128)S(1)}, u32[]{:S(2)}, u32[]{:S(2)}) collective-permute-start(f32[4,64,128]{2,1,0:T(8,128)S(1)} %pad_maximum_fusion.6), channel_id=1, source_target_pairs={{0,4},{1,3},{2,6},{3,1},{4,0},{5,7},{6,2},{7,5},{8,12},{9,11},{10,... | collective-permute-start | bytes 393224 | tf_op jit(solution)/shard_map/ppermute | solution.py:53
  62.4 6.5 %collective-permute-start.26 = (f32[4,64,128]{2,1,0:T(8,128)S(1)}, f32[4,64,128]{2,1,0:T(8,128)S(1)}, u32[]{:S(2)}, u32[]{:S(2)}) collective-permute-start(f32[4,64,128]{2,1,0:T(8,128)S(1)} %pad_maximum_fusion.7), channel_id=1, source_target_pairs={{0,2},{1,5},{2,0},{3,7},{4,6},{5,1},{6,4},{7,3},{8,10},{9,13},{10,... | collective-permute-start | bytes 393224 | tf_op jit(solution)/shard_map/ppermute | solution.py:53
  66.6 6.9 %collective-permute-start.17 = (f32[8,64,128]{2,1,0:T(8,128)S(1)}, f32[8,64,128]{2,1,0:T(8,128)S(1)}, u32[]{:S(2)}, u32[]{:S(2)}) collective-permute-start(f32[8,64,128]{2,1,0:T(8,128)S(1)} %pad_maximum_fusion.refs_1_), channel_id=1, source_target_pairs={{0,2},{1,5},{2,0},{3,7},{4,6},{5,1},{6,4},{7,3},{8,10},{9,13},{10,... | collective-permute-start | bytes 786440 | tf_op jit(solution)/shard_map/ppermute | solution.py:53
  69.0 6.4 %collective-permute-start.27 = (f32[8,64,128]{2,1,0:T(8,128)S(1)}, f32[8,64,128]{2,1,0:T(8,128)S(1)}, u32[]{:S(2)}, u32[]{:S(2)}) collective-permute-start(f32[8,64,128]{2,1,0:T(8,128)S(1)} %pad_maximum_fusion.1.refs_1_), channel_id=1, source_target_pairs={{0,4},{1,3},{2,6},{3,1},{4,0},{5,7},{6,2},{7,5},{8,12},{9,11},{10,... | collective-permute-start | bytes 786440 | tf_op jit(solution)/shard_map/ppermute | solution.py:53
  70.9 7.6 %collective-permute-start.29 = (f32[2,4,64,128]{3,2,1,0:T(8,128)S(1)}, f32[2,4,64,128]{3,2,1,0:T(8,128)S(1)}, u32[]{:S(2)}, u32[]{:S(2)}) collective-permute-start(f32[2,4,64,128]{3,2,1,0:T(8,128)S(1)} %get-tuple-element.79), channel_id=1, source_target_pairs={{0,4},{1,3},{2,6},{3,1},{4,0},{5,7},{6,2},{7,5},{8,12},{9,11},{10,... | collective-permute-start | bytes 786440 | tf_op jit(solution)/shard_map/ppermute | solution.py:53
  76.1 4.2 %collective-permute-start.28 = (f32[1,64,128]{2,1,0:T(8,128)S(1)}, f32[1,64,128]{2,1,0:T(8,128)S(1)}, u32[]{:S(2)}, u32[]{:S(2)}) collective-permute-start(f32[1,64,128]{2,1,0:T(8,128)S(1)} %get-tuple-element.75), channel_id=1, source_target_pairs={{0,1},{1,0},{2,3},{3,2},{4,5},{5,4},{6,7},{7,6},{8,9},{9,8},{10,11... | collective-permute-start | bytes 98312 | tf_op jit(solution)/shard_map/ppermute | solution.py:53
  76.2 5.5 %collective-permute-start.32 = (f32[1,64,128]{2,1,0:T(8,128)S(1)}, f32[1,64,128]{2,1,0:T(8,128)S(1)}, u32[]{:S(2)}, u32[]{:S(2)}) collective-permute-start(f32[1,64,128]{2,1,0:T(8,128)S(1)} %add.82), channel_id=1, source_target_pairs={{0,16},{1,17},{2,18},{3,19},{4,20},{5,21},{6,22},{7,23},{8,24},{9,... | collective-permute-start | bytes 98312 | tf_op jit(solution)/shard_map/ppermute | solution.py:53
  78.6 10.0 %collective-permute-start.30 = (f32[2,2,64,128]{3,2,1,0:T(8,128)S(1)}, f32[2,2,64,128]{3,2,1,0:T(8,128)S(1)}, u32[]{:S(2)}, u32[]{:S(2)}) collective-permute-start(f32[2,2,64,128]{3,2,1,0:T(8,128)S(1)} %get-tuple-element.81), channel_id=1, source_target_pairs={{0,8},{1,9},{2,10},{3,11},{4,12},{5,13},{6,14},{7,15},{8,0},{9,1},... | collective-permute-start | bytes 393224 | tf_op jit(solution)/shard_map/ppermute | solution.py:53
  80.3 5.0 %collective-permute-start.43 = (f32[1,64,128]{2,1,0:T(8,128)S(1)}, f32[1,64,128]{2,1,0:T(8,128)S(1)}, u32[]{:S(2)}, u32[]{:S(2)}) collective-permute-start(f32[1,64,128]{2,1,0:T(8,128)S(1)} %add.87), channel_id=1, source_target_pairs={{0,16},{1,17},{2,18},{3,19},{4,20},{5,21},{6,22},{7,23},{8,24},{9,... | collective-permute-start | bytes 98312 | tf_op jit(solution)/shard_map/ppermute | solution.py:53
  81.8 5.4 %collective-permute-start.33 = (f32[2,64,128]{2,1,0:T(8,128)S(1)}, f32[2,64,128]{2,1,0:T(8,128)S(1)}, u32[]{:S(2)}, u32[]{:S(2)}) collective-permute-start(f32[2,64,128]{2,1,0:T(8,128)S(1)} %pad_maximum_fusion.14), channel_id=1, source_target_pairs={{0,8},{1,9},{2,10},{3,11},{4,12},{5,13},{6,14},{7,15},{8,0},{9,1},... | collective-permute-start | bytes 196616 | tf_op jit(solution)/shard_map/ppermute | solution.py:53
  85.3 4.3 %collective-permute-start.44 = (f32[2,64,128]{2,1,0:T(8,128)S(1)}, f32[2,64,128]{2,1,0:T(8,128)S(1)}, u32[]{:S(2)}, u32[]{:S(2)}) collective-permute-start(f32[2,64,128]{2,1,0:T(8,128)S(1)} %pad_maximum_fusion.15), channel_id=1, source_target_pairs={{0,8},{1,9},{2,10},{3,11},{4,12},{5,13},{6,14},{7,15},{8,0},{9,1},... | collective-permute-start | bytes 196616 | tf_op jit(solution)/shard_map/ppermute | solution.py:53
  87.2 5.4 %collective-permute-start.34 = (f32[4,64,128]{2,1,0:T(8,128)S(1)}, f32[4,64,128]{2,1,0:T(8,128)S(1)}, u32[]{:S(2)}, u32[]{:S(2)}) collective-permute-start(f32[4,64,128]{2,1,0:T(8,128)S(1)} %pad_maximum_fusion.8), channel_id=1, source_target_pairs={{0,4},{1,3},{2,6},{3,1},{4,0},{5,7},{6,2},{7,5},{8,12},{9,11},{10,... | collective-permute-start | bytes 393224 | tf_op jit(solution)/shard_map/ppermute | solution.py:53
  88.6 14.1 %collective-permute-start.31 = (f32[2,2,64,128]{3,2,1,0:T(8,128)S(1)}, f32[2,2,64,128]{3,2,1,0:T(8,128)S(1)}, u32[]{:S(2)}, u32[]{:S(2)}) collective-permute-start(f32[2,2,64,128]{3,2,1,0:T(8,128)S(1)} %add.81), channel_id=1, source_target_pairs={{0,1},{1,0},{2,3},{3,2},{4,5},{5,4},{6,7},{7,6},{8,9},{9,8},{10,11... | collective-permute-start | bytes 393224 | tf_op jit(solution)/shard_map/ppermute | solution.py:53
  89.6 5.0 %collective-permute-start.45 = (f32[4,64,128]{2,1,0:T(8,128)S(1)}, f32[4,64,128]{2,1,0:T(8,128)S(1)}, u32[]{:S(2)}, u32[]{:S(2)}) collective-permute-start(f32[4,64,128]{2,1,0:T(8,128)S(1)} %pad_maximum_fusion.10), channel_id=1, source_target_pairs={{0,2},{1,5},{2,0},{3,7},{4,6},{5,1},{6,4},{7,3},{8,10},{9,13},{10,... | collective-permute-start | bytes 393224 | tf_op jit(solution)/shard_map/ppermute | solution.py:53
  92.6 9.0 %collective-permute-start.35 = (f32[8,64,128]{2,1,0:T(8,128)S(1)}, f32[8,64,128]{2,1,0:T(8,128)S(1)}, u32[]{:S(2)}, u32[]{:S(2)}) collective-permute-start(f32[8,64,128]{2,1,0:T(8,128)S(1)} %pad_maximum_fusion.2.refs_1_), channel_id=1, source_target_pairs={{0,2},{1,5},{2,0},{3,7},{4,6},{5,1},{6,4},{7,3},{8,10},{9,13},{10,... | collective-permute-start | bytes 786440 | tf_op jit(solution)/shard_map/ppermute | solution.py:53
  94.6 11.9 %collective-permute-start.46 = (f32[8,64,128]{2,1,0:T(8,128)S(1)}, f32[8,64,128]{2,1,0:T(8,128)S(1)}, u32[]{:S(2)}, u32[]{:S(2)}) collective-permute-start(f32[8,64,128]{2,1,0:T(8,128)S(1)} %pad_maximum_fusion.4.refs_1_), channel_id=1, source_target_pairs={{0,4},{1,3},{2,6},{3,1},{4,0},{5,7},{6,2},{7,5},{8,12},{9,11},{10,... | collective-permute-start | bytes 786440 | tf_op jit(solution)/shard_map/ppermute | solution.py:53
  105.0 7.6 %collective-permute-start.37 = (f32[8,64,128]{2,1,0:T(8,128)S(1)}, f32[8,64,128]{2,1,0:T(8,128)S(1)}, u32[]{:S(2)}, u32[]{:S(2)}) collective-permute-start(f32[8,64,128]{2,1,0:T(8,128)S(1)} %get-tuple-element.83), channel_id=1, source_target_pairs={{0,2},{1,5},{2,0},{3,7},{4,6},{5,1},{6,4},{7,3},{8,10},{9,13},{10,... | collective-permute-start | bytes 786440 | tf_op jit(solution)/shard_map/ppermute | solution.py:53
  110.8 6.4 %collective-permute-start.48 = (f32[8,64,128]{2,1,0:T(8,128)S(1)}, f32[8,64,128]{2,1,0:T(8,128)S(1)}, u32[]{:S(2)}, u32[]{:S(2)}) collective-permute-start(f32[8,64,128]{2,1,0:T(8,128)S(1)} %get-tuple-element.88), channel_id=1, source_target_pairs={{0,4},{1,3},{2,6},{3,1},{4,0},{5,7},{6,2},{7,5},{8,12},{9,11},{10,... | collective-permute-start | bytes 786440 | tf_op jit(solution)/shard_map/ppermute | solution.py:53
  112.6 6.0 %collective-permute-start.38 = (f32[4,64,128]{2,1,0:T(8,128)S(1)}, f32[4,64,128]{2,1,0:T(8,128)S(1)}, u32[]{:S(2)}, u32[]{:S(2)}) collective-permute-start(f32[4,64,128]{2,1,0:T(8,128)S(1)} %slice_add_fusion.2), channel_id=1, source_target_pairs={{0,4},{1,3},{2,6},{3,1},{4,0},{5,7},{6,2},{7,5},{8,12},{9,11},{10,... | collective-permute-start | bytes 393224 | tf_op jit(solution)/shard_map/ppermute | solution.py:53
  117.3 5.0 %collective-permute-start.49 = (f32[4,64,128]{2,1,0:T(8,128)S(1)}, f32[4,64,128]{2,1,0:T(8,128)S(1)}, u32[]{:S(2)}, u32[]{:S(2)}) collective-permute-start(f32[4,64,128]{2,1,0:T(8,128)S(1)} %slice_add_fusion), channel_id=1, source_target_pairs={{0,2},{1,5},{2,0},{3,7},{4,6},{5,1},{6,4},{7,3},{8,10},{9,13},{10,... | collective-permute-start | bytes 393224 | tf_op jit(solution)/shard_map/ppermute | solution.py:53
  118.7 5.6 %collective-permute-start.39 = (f32[4,64,128]{2,1,0:T(8,128)S(1)}, f32[4,64,128]{2,1,0:T(8,128)S(1)}, u32[]{:S(2)}, u32[]{:S(2)}) collective-permute-start(f32[4,64,128]{2,1,0:T(8,128)S(1)} %pad_maximum_fusion.9), channel_id=1, source_target_pairs={{0,8},{1,9},{2,10},{3,11},{4,12},{5,13},{6,14},{7,15},{8,0},{9,1},... | collective-permute-start | bytes 393224 | tf_op jit(solution)/shard_map/ppermute | solution.py:53
  122.4 5.0 %collective-permute-start.50 = (f32[4,64,128]{2,1,0:T(8,128)S(1)}, f32[4,64,128]{2,1,0:T(8,128)S(1)}, u32[]{:S(2)}, u32[]{:S(2)}) collective-permute-start(f32[4,64,128]{2,1,0:T(8,128)S(1)} %pad_maximum_fusion.11), channel_id=1, source_target_pairs={{0,8},{1,9},{2,10},{3,11},{4,12},{5,13},{6,14},{7,15},{8,0},{9,1},... | collective-permute-start | bytes 393224 | tf_op jit(solution)/shard_map/ppermute | solution.py:53
  124.4 6.3 %collective-permute-start.40 = (f32[4,64,128]{2,1,0:T(8,128)S(1)}, f32[4,64,128]{2,1,0:T(8,128)S(1)}, u32[]{:S(2)}, u32[]{:S(2)}) collective-permute-start(f32[4,64,128]{2,1,0:T(8,128)S(1)} %add.86), channel_id=1, source_target_pairs={{0,4},{1,3},{2,6},{3,1},{4,0},{5,7},{6,2},{7,5},{8,12},{9,11},{10,... | collective-permute-start | bytes 393224 | tf_op jit(solution)/shard_map/ppermute | solution.py:53
  127.4 5.0 %collective-permute-start.51 = (f32[4,64,128]{2,1,0:T(8,128)S(1)}, f32[4,64,128]{2,1,0:T(8,128)S(1)}, u32[]{:S(2)}, u32[]{:S(2)}) collective-permute-start(f32[4,64,128]{2,1,0:T(8,128)S(1)} %add.91), channel_id=1, source_target_pairs={{0,2},{1,5},{2,0},{3,7},{4,6},{5,1},{6,4},{7,3},{8,10},{9,13},{10,... | collective-permute-start | bytes 393224 | tf_op jit(solution)/shard_map/ppermute | solution.py:53
  130.7 7.9 %collective-permute-start.41 = (f32[8,64,128]{2,1,0:T(8,128)S(1)}, f32[8,64,128]{2,1,0:T(8,128)S(1)}, u32[]{:S(2)}, u32[]{:S(2)}) collective-permute-start(f32[8,64,128]{2,1,0:T(8,128)S(1)} %pad_maximum_fusion.3.refs_1_), channel_id=1, source_target_pairs={{0,2},{1,5},{2,0},{3,7},{4,6},{5,1},{6,4},{7,3},{8,10},{9,13},{10,... | collective-permute-start | bytes 786440 | tf_op jit(solution)/shard_map/ppermute | solution.py:53
  132.5 7.2 %collective-permute-start.52 = (f32[8,64,128]{2,1,0:T(8,128)S(1)}, f32[8,64,128]{2,1,0:T(8,128)S(1)}, u32[]{:S(2)}, u32[]{:S(2)}) collective-permute-start(f32[8,64,128]{2,1,0:T(8,128)S(1)} %pad_maximum_fusion.5.refs_1_), channel_id=1, source_target_pairs={{0,4},{1,3},{2,6},{3,1},{4,0},{5,7},{6,2},{7,5},{8,12},{9,11},{10,... | collective-permute-start | bytes 786440 | tf_op jit(solution)/shard_map/ppermute | solution.py:53
  (13 other events, 41.8 us)

commit v2 on v1

--- a/solution.py
+++ b/solution.py
@@ -302,10 +302,10 @@
             send_ref[i - 8] = block
 
 
-def backward(deep, chain, w_ref, near_ref, far_ref, *refs):
-    outs, rhs_ref = refs[:-1], refs[-1]
+def backward(deep, chain, w_ref, *refs):
+    pieces, outs, rhs_ref = refs[:4], refs[4:-1], refs[-1]
     for i, start in enumerate(block_starts(deep, chain)):
-        put_split(rhs_ref, start, near_ref[i] if i < 8 else far_ref[i - 8])
+        put_split(rhs_ref, start, pieces[i // 4][i % 4])
     total = product(w_ref, rhs_ref)
     blocks = w_ref.shape[0] // 128
     for i in range(blocks):
@@ -327,12 +327,12 @@
     )
 
 
-def run_backward(w, near, far, deep, chain, apart, after=()):
+def run_backward(w, pieces, deep, chain, apart, after=()):
     m, k = w.shape
     return kernel_call(
         functools.partial(backward, deep, chain),
         [((m // 256, WIDE, 128), F32)] * 2 if apart else [((m // 128, WIDE, 128), F32)],
-        [w, near, far],
+        [w, *pieces],
         [pltpu.VMEM((k, 128), BF16)],
         flops=2 * m * k * 128,
         after=after,
@@ -365,8 +365,8 @@
 
 
 def plane_spread(line, chain):
-    near = jnp.concatenate([line, swap_second(line, chain)], 0)
-    return near, swap_first(near, chain)
+    second = swap_second(line, chain)
+    return line, second, swap_first(line, chain), swap_first(second, chain)
 
 
 def unpack_kernel(mine0, recv0, mine1, recv1, out_ref):
@@ -448,7 +448,7 @@
     for h in chains:
         mine, theirs = run_backward(
             top_t,
-            *plane_spread(depth_total(values[h], True), h),
+            plane_spread(depth_total(values[h], True), h),
             True,
             h,
             True,
@@ -461,12 +461,12 @@
     mid_parts = []
     for h in chains:
         (both,) = run_backward(
-            cou_w, *plane_spread(depth_spread(adjoint[h]), h), True, h, False
+            cou_w, plane_spread(depth_spread(adjoint[h]), h), True, h, False
         )
         vec = [mid_load[h], mid_other[h], both, swap_core(both)]
         parts = run_forward(mid_w, vec, False, h, after=[top_out] if h else ())
         line = depth_total(plane_sum(*parts, h)[0], False)
-        mine, theirs = run_backward(mid_t, *plane_spread(line, h), False, h, True)
+        mine, theirs = run_backward(mid_t, plane_spread(line, h), False, h, True)
         mid_parts.append((mine, swap_core(theirs)))
     return top_out, unpack(*mid_parts)
 

time: 143 us -> 140 us (0.979)
  starting transfers between devices: 70.2 us -> 62.9 us
  waiting for transfers between devices: 53.2 us -> 57.4 us
    ppermute x54 -> x60, starting transfers between devices: 70.2 us -> 62.9 us  [permute(): return lax.ppermute(value, AXES, [(i, partner(i)) for i in range(32)])]
    ppermute x54 -> x60, waiting for transfers between devices: 53.2 us -> 57.4 us  [permute(): return lax.ppermute(value, AXES, [(i, partner(i)) for i in range(32)])]
  transfers between devices with their start and end apart: 54 -> 60, of which waited for: 32 -> 37; matrix products, arithmetic and copies ran while one was open for 0% -> 0% of each run, Pallas kernels for 8% -> 8%
where the time goes in v2:
time: 140 us
  starting transfers between devices  62.9 us (45%)
  waiting for transfers between devices  57.4 us (41%)
  Pallas kernels  13.9 us (10%)
  local copies, waits for them, and re-layouts  3.91 us (3%)
    ppermute x60, starting transfers between devices, permute(): return lax.ppermute(value, AXES, [(i, partner(i)) for i in range(32)])  62.9 us
    ppermute x60, waiting for transfers between devices, permute(): return lax.ppermute(value, AXES, [(i, partner(i)) for i in range(32)])  57.4 us
    pallas_call x24, Pallas kernels, kernel_call(): pl.pallas_call(ordered, out_shape=[jax.ShapeDtypeStruct(*o) for o in outs...  13.9 us
    unnamed x14, local copies, waits for them, and re-layouts  3.81 us
  transfers between devices with their start and end apart: 60, of which 37 were waited for; matrix products, arithmetic and copies ran while one was open for 0% of the time, Pallas kernels for 8%

profile of v2, /device:TPU:0, one launch (start us, length us, event | category | flops | bytes accessed | tf_op | source)
XLA Modules:
  0.0 139.7 jit_solution(5909236654470638416)
XLA Ops:
  3.0 2.6 %collective-permute-start.2 = (f32[32,1152]{1,0:T(8,128)S(1)}, f32[32,1152]{1,0:T(8,128)S(1)}, u32[]{:S(2)}, u32[]{:S(2)}) collective-permute-start(f32[32,1152]{1,0:T(8,128)S(1)} %get-tuple-element.53), channel_id=1, source_target_pairs={{0,2},{1,5},{2,0},{3,7},{4,6},{5,1},{6,4},{7,3},{8,10},{9,13},{10,... | collective-permute-start | bytes 442376 | tf_op jit(solution)/shard_map/ppermute | solution.py:53
  5.6 3.6 %collective-permute-done.2.refs_2_ = f32[32,1152]{1,0:T(8,128)S(1)} collective-permute-done((f32[32,1152]{1,0:T(8,128)S(1)}, f32[32,1152]{1,0:T(8,128)S(1)}, u32[]{:S(2)}, u32[]{:S(2)}) %collective-permute-start.2) | collective-permute-done | bytes 147488 | tf_op jit(solution)/shard_map/ppermute | solution.py:53
  10.8 2.1 %collective-permute-start.4 = (f32[2,4,64,128]{3,2,1,0:T(8,128)S(1)}, f32[2,4,64,128]{3,2,1,0:T(8,128)S(1)}, u32[]{:S(2)}, u32[]{:S(2)}) collective-permute-start(f32[2,4,64,128]{3,2,1,0:T(8,128)S(1)} %get-tuple-element.56), channel_id=1, source_target_pairs={{0,4},{1,3},{2,6},{3,1},{4,0},{5,7},{6,2},{7,5},{8,12},{9,11},{10,... | collective-permute-start | bytes 786440 | tf_op jit(solution)/shard_map/ppermute | solution.py:53
  14.3 2.9 %collective-permute-done.4.refs_1_ = f32[2,4,64,128]{3,2,1,0:T(8,128)S(1)} collective-permute-done((f32[2,4,64,128]{3,2,1,0:T(8,128)S(1)}, f32[2,4,64,128]{3,2,1,0:T(8,128)S(1)}, u32[]{:S(2)}, u32[]{:S(2)}) %collective-permute-start.4) | collective-permute-done | bytes 262176 | tf_op jit(solution)/shard_map/ppermute | solution.py:53
  17.3 2.1 %collective-permute-start.5 = (f32[2,2,64,128]{3,2,1,0:T(8,128)S(1)}, f32[2,2,64,128]{3,2,1,0:T(8,128)S(1)}, u32[]{:S(2)}, u32[]{:S(2)}) collective-permute-start(f32[2,2,64,128]{3,2,1,0:T(8,128)S(1)} %slice.125), channel_id=1, source_target_pairs={{0,8},{1,9},{2,10},{3,11},{4,12},{5,13},{6,14},{7,15},{8,0},{9,1},... | collective-permute-start | bytes 393224 | tf_op jit(solution)/shard_map/ppermute | solution.py:53
  19.6 1.5 %collective-permute-start.8 = (f32[32,1024]{1,0:T(8,128)S(1)}, f32[32,1024]{1,0:T(8,128)S(1)}, u32[]{:S(2)}, u32[]{:S(2)}) collective-permute-start(f32[32,1024]{1,0:T(8,128)S(1)} %get-tuple-element.59), channel_id=1, source_target_pairs={{0,2},{1,5},{2,0},{3,7},{4,6},{5,1},{6,4},{7,3},{8,10},{9,13},{10,... | collective-permute-start | bytes 393224 | tf_op jit(solution)/shard_map/ppermute | solution.py:53
  22.5 3.1 %collective-permute-start.6 = (f32[2,1,64,128]{3,2,1,0:T(8,128)S(1)}, f32[2,1,64,128]{3,2,1,0:T(8,128)S(1)}, u32[]{:S(2)}, u32[]{:S(2)}) collective-permute-start(f32[2,1,64,128]{3,2,1,0:T(8,128)S(1)} %slice.126), channel_id=1, source_target_pairs={{0,16},{1,17},{2,18},{3,19},{4,20},{5,21},{6,22},{7,23},{8,24},{9,... | collective-permute-start | bytes 196616 | tf_op jit(solution)/shard_map/ppermute | solution.py:53
  26.1 1.7 %collective-permute-done.6.refs_1_ = f32[2,1,64,128]{3,2,1,0:T(8,128)S(1)} collective-permute-done((f32[2,1,64,128]{3,2,1,0:T(8,128)S(1)}, f32[2,1,64,128]{3,2,1,0:T(8,128)S(1)}, u32[]{:S(2)}, u32[]{:S(2)}) %collective-permute-start.6) | collective-permute-done | bytes 65568 | tf_op jit(solution)/shard_map/ppermute | solution.py:53
  30.2 1.9 %collective-permute-start.22 = (f32[8,64,128]{2,1,0:T(8,128)S(1)}, f32[8,64,128]{2,1,0:T(8,128)S(1)}, u32[]{:S(2)}, u32[]{:S(2)}) collective-permute-start(f32[8,64,128]{2,1,0:T(8,128)S(1)} %get-tuple-element.72), channel_id=1, source_target_pairs={{0,4},{1,3},{2,6},{3,1},{4,0},{5,7},{6,2},{7,5},{8,12},{9,11},{10,... | collective-permute-start | bytes 786440 | tf_op jit(solution)/shard_map/ppermute | solution.py:53
  32.8 1.5 %collective-permute-start.11 = (f32[8,64,128]{2,1,0:T(8,128)S(1)}, f32[8,64,128]{2,1,0:T(8,128)S(1)}, u32[]{:S(2)}, u32[]{:S(2)}) collective-permute-start(f32[8,64,128]{2,1,0:T(8,128)S(1)} %get-tuple-element.62), channel_id=1, source_target_pairs={{0,2},{1,5},{2,0},{3,7},{4,6},{5,1},{6,4},{7,3},{8,10},{9,13},{10,... | collective-permute-start | bytes 786440 | tf_op jit(solution)/shard_map/ppermute | solution.py:53
  35.9 2.4 %collective-permute-done.22 = f32[8,64,128]{2,1,0:T(8,128)S(1)} collective-permute-done((f32[8,64,128]{2,1,0:T(8,128)S(1)}, f32[8,64,128]{2,1,0:T(8,128)S(1)}, u32[]{:S(2)}, u32[]{:S(2)}) %collective-permute-start.22) | collective-permute-done | bytes 262176 | tf_op jit(solution)/shard_map/ppermute | solution.py:53
  38.3 2.4 %collective-permute-start.23 = (f32[4,64,128]{2,1,0:T(8,128)S(1)}, f32[4,64,128]{2,1,0:T(8,128)S(1)}, u32[]{:S(2)}, u32[]{:S(2)}) collective-permute-start(f32[4,64,128]{2,1,0:T(8,128)S(1)} %slice_add_fusion.4), channel_id=1, source_target_pairs={{0,2},{1,5},{2,0},{3,7},{4,6},{5,1},{6,4},{7,3},{8,10},{9,13},{10,... | collective-permute-start | bytes 393224 | tf_op jit(solution)/shard_map/ppermute | solution.py:53
  40.7 2.0 %collective-permute-start.12 = (f32[4,64,128]{2,1,0:T(8,128)S(1)}, f32[4,64,128]{2,1,0:T(8,128)S(1)}, u32[]{:S(2)}, u32[]{:S(2)}) collective-permute-start(f32[4,64,128]{2,1,0:T(8,128)S(1)} %slice_add_fusion.6), channel_id=1, source_target_pairs={{0,4},{1,3},{2,6},{3,1},{4,0},{5,7},{6,2},{7,5},{8,12},{9,11},{10,... | collective-permute-start | bytes 393224 | tf_op jit(solution)/shard_map/ppermute | solution.py:53
  42.8 2.1 %collective-permute-done.23 = f32[4,64,128]{2,1,0:T(8,128)S(1)} collective-permute-done((f32[4,64,128]{2,1,0:T(8,128)S(1)}, f32[4,64,128]{2,1,0:T(8,128)S(1)}, u32[]{:S(2)}, u32[]{:S(2)}) %collective-permute-start.23) | collective-permute-done | bytes 131104 | tf_op jit(solution)/shard_map/ppermute | solution.py:53
  44.9 1.9 %collective-permute-start.24 = (f32[2,64,128]{2,1,0:T(8,128)S(1)}, f32[2,64,128]{2,1,0:T(8,128)S(1)}, u32[]{:S(2)}, u32[]{:S(2)}) collective-permute-start(f32[2,64,128]{2,1,0:T(8,128)S(1)} %slice.140), channel_id=1, source_target_pairs={{0,8},{1,9},{2,10},{3,11},{4,12},{5,13},{6,14},{7,15},{8,0},{9,1},... | collective-permute-start | bytes 196616 | tf_op jit(solution)/shard_map/ppermute | solution.py:53
  47.9 1.3 collective-permute-done.24
  49.3 3.6 %collective-permute-start.25 = (f32[2,64,128]{2,1,0:T(8,128)S(1)}, f32[2,64,128]{2,1,0:T(8,128)S(1)}, u32[]{:S(2)}, u32[]{:S(2)}) collective-permute-start(f32[2,64,128]{2,1,0:T(8,128)S(1)} %pad_maximum_fusion.7), channel_id=1, source_target_pairs={{0,16},{1,17},{2,18},{3,19},{4,20},{5,21},{6,22},{7,23},{8,24},{9,... | collective-permute-start | bytes 196616 | tf_op jit(solution)/shard_map/ppermute | solution.py:53
  52.9 2.0 %collective-permute-start.14 = (f32[2,64,128]{2,1,0:T(8,128)S(1)}, f32[2,64,128]{2,1,0:T(8,128)S(1)}, u32[]{:S(2)}, u32[]{:S(2)}) collective-permute-start(f32[2,64,128]{2,1,0:T(8,128)S(1)} %pad_maximum_fusion.6), channel_id=1, source_target_pairs={{0,16},{1,17},{2,18},{3,19},{4,20},{5,21},{6,22},{7,23},{8,24},{9,... | collective-permute-start | bytes 196616 | tf_op jit(solution)/shard_map/ppermute | solution.py:53
  55.3 2.5 %collective-permute-start.26 = (f32[2,64,128]{2,1,0:T(8,128)S(1)}, f32[2,64,128]{2,1,0:T(8,128)S(1)}, u32[]{:S(2)}, u32[]{:S(2)}) collective-permute-start(f32[2,64,128]{2,1,0:T(8,128)S(1)} %add.80), channel_id=1, source_target_pairs={{0,8},{1,9},{2,10},{3,11},{4,12},{5,13},{6,14},{7,15},{8,0},{9,1},... | collective-permute-start | bytes 196616 | tf_op jit(solution)/shard_map/ppermute | solution.py:53
  58.2 2.1 %collective-permute-start.15 = (f32[2,64,128]{2,1,0:T(8,128)S(1)}, f32[2,64,128]{2,1,0:T(8,128)S(1)}, u32[]{:S(2)}, u32[]{:S(2)}) collective-permute-start(f32[2,64,128]{2,1,0:T(8,128)S(1)} %add.75), channel_id=1, source_target_pairs={{0,8},{1,9},{2,10},{3,11},{4,12},{5,13},{6,14},{7,15},{8,0},{9,1},... | collective-permute-start | bytes 196616 | tf_op jit(solution)/shard_map/ppermute | solution.py:53
  62.6 1.6 %collective-permute-start.16 = (f32[4,64,128]{2,1,0:T(8,128)S(1)}, f32[4,64,128]{2,1,0:T(8,128)S(1)}, u32[]{:S(2)}, u32[]{:S(2)}) collective-permute-start(f32[4,64,128]{2,1,0:T(8,128)S(1)} %pad_maximum_fusion.refs_1_), channel_id=1, source_target_pairs={{0,4},{1,3},{2,6},{3,1},{4,0},{5,7},{6,2},{7,5},{8,12},{9,11},{10,... | collective-permute-start | bytes 393224 | tf_op jit(solution)/shard_map/ppermute | solution.py:53
  65.3 1.5 %collective-permute-done.27.refs_2_ = f32[4,64,128]{2,1,0:T(8,128)S(1)} collective-permute-done((f32[4,64,128]{2,1,0:T(8,128)S(1)}, f32[4,64,128]{2,1,0:T(8,128)S(1)}, u32[]{:S(2)}, u32[]{:S(2)}) %collective-permute-start.27) | collective-permute-done | bytes 131104 | tf_op jit(solution)/shard_map/ppermute | solution.py:53
  66.8 1.5 %collective-permute-start.28 = (f32[4,64,128]{2,1,0:T(8,128)S(1)}, f32[4,64,128]{2,1,0:T(8,128)S(1)}, u32[]{:S(2)}, u32[]{:S(2)}) collective-permute-start(f32[4,64,128]{2,1,0:T(8,128)S(1)} %pad_maximum_fusion.1.refs_1_), channel_id=1, source_target_pairs={{0,4},{1,3},{2,6},{3,1},{4,0},{5,7},{6,2},{7,5},{8,12},{9,11},{10,... | collective-permute-start | bytes 393224 | tf_op jit(solution)/shard_map/ppermute | solution.py:53
  69.0 1.5 %collective-permute-start.29 = (f32[4,64,128]{2,1,0:T(8,128)S(1)}, f32[4,64,128]{2,1,0:T(8,128)S(1)}, u32[]{:S(2)}, u32[]{:S(2)}) collective-permute-start(f32[4,64,128]{2,1,0:T(8,128)S(1)} %collective-permute-done.27.refs_2_), channel_id=1, source_target_pairs={{0,4},{1,3},{2,6},{3,1},{4,0},{5,7},{6,2},{7,5},{8,12},{9,11},{10,... | collective-permute-start | bytes 393224 | tf_op jit(solution)/shard_map/ppermute | solution.py:53
  71.0 1.6 %collective-permute-start.18 = (f32[4,64,128]{2,1,0:T(8,128)S(1)}, f32[4,64,128]{2,1,0:T(8,128)S(1)}, u32[]{:S(2)}, u32[]{:S(2)}) collective-permute-start(f32[4,64,128]{2,1,0:T(8,128)S(1)} %collective-permute-done.16.refs_2_), channel_id=1, source_target_pairs={{0,2},{1,5},{2,0},{3,7},{4,6},{5,1},{6,4},{7,3},{8,10},{9,13},{10,... | collective-permute-start | bytes 393224 | tf_op jit(solution)/shard_map/ppermute | solution.py:53
  75.5 1.4 %collective-permute-done.18.refs_4_ = f32[4,64,128]{2,1,0:T(8,128)S(1)} collective-permute-done((f32[4,64,128]{2,1,0:T(8,128)S(1)}, f32[4,64,128]{2,1,0:T(8,128)S(1)}, u32[]{:S(2)}, u32[]{:S(2)}) %collective-permute-start.18) | collective-permute-done | bytes 131104 | tf_op jit(solution)/shard_map/ppermute | solution.py:53
  77.8 1.7 %collective-permute-start.47 = (f32[1,64,128]{2,1,0:T(8,128)S(1)}, f32[1,64,128]{2,1,0:T(8,128)S(1)}, u32[]{:S(2)}, u32[]{:S(2)}) collective-permute-start(f32[1,64,128]{2,1,0:T(8,128)S(1)} %add.87), channel_id=1, source_target_pairs={{0,16},{1,17},{2,18},{3,19},{4,20},{5,21},{6,22},{7,23},{8,24},{9,... | collective-permute-start | bytes 98312 | tf_op jit(solution)/shard_map/ppermute | solution.py:53
  79.5 1.4 %collective-permute-start.32 = (f32[2,2,64,128]{3,2,1,0:T(8,128)S(1)}, f32[2,2,64,128]{3,2,1,0:T(8,128)S(1)}, u32[]{:S(2)}, u32[]{:S(2)}) collective-permute-start(f32[2,2,64,128]{3,2,1,0:T(8,128)S(1)} %get-tuple-element.81), channel_id=1, source_target_pairs={{0,8},{1,9},{2,10},{3,11},{4,12},{5,13},{6,14},{7,15},{8,0},{9,1},... | collective-permute-start | bytes 393224 | tf_op jit(solution)/shard_map/ppermute | solution.py:53
  81.6 1.6 %collective-permute-done.47 = f32[1,64,128]{2,1,0:T(8,128)S(1)} collective-permute-done((f32[1,64,128]{2,1,0:T(8,128)S(1)}, f32[1,64,128]{2,1,0:T(8,128)S(1)}, u32[]{:S(2)}, u32[]{:S(2)}) %collective-permute-start.47) | collective-permute-done | bytes 32800 | tf_op jit(solution)/shard_map/ppermute | solution.py:53
  83.4 2.8 %collective-permute-done.34 = f32[1,64,128]{2,1,0:T(8,128)S(1)} collective-permute-done((f32[1,64,128]{2,1,0:T(8,128)S(1)}, f32[1,64,128]{2,1,0:T(8,128)S(1)}, u32[]{:S(2)}, u32[]{:S(2)}) %collective-permute-start.34) | collective-permute-done | bytes 32800 | tf_op jit(solution)/shard_map/ppermute | solution.py:53
  90.4 1.6 %collective-permute-start.36 = (f32[4,64,128]{2,1,0:T(8,128)S(1)}, f32[4,64,128]{2,1,0:T(8,128)S(1)}, u32[]{:S(2)}, u32[]{:S(2)}) collective-permute-start(f32[4,64,128]{2,1,0:T(8,128)S(1)} %pad_maximum_fusion.2.refs_1_), channel_id=1, source_target_pairs={{0,4},{1,3},{2,6},{3,1},{4,0},{5,7},{6,2},{7,5},{8,12},{9,11},{10,... | collective-permute-start | bytes 393224 | tf_op jit(solution)/shard_map/ppermute | solution.py:53
  92.1 2.6 %collective-permute-done.49.refs_2_ = f32[4,64,128]{2,1,0:T(8,128)S(1)} collective-permute-done((f32[4,64,128]{2,1,0:T(8,128)S(1)}, f32[4,64,128]{2,1,0:T(8,128)S(1)}, u32[]{:S(2)}, u32[]{:S(2)}) %collective-permute-start.49) | collective-permute-done | bytes 131104 | tf_op jit(solution)/shard_map/ppermute | solution.py:53
  94.8 1.3 collective-permute-done.36.refs_2_
  96.0 2.0 %collective-permute-start.38 = (f32[4,64,128]{2,1,0:T(8,128)S(1)}, f32[4,64,128]{2,1,0:T(8,128)S(1)}, u32[]{:S(2)}, u32[]{:S(2)}) collective-permute-start(f32[4,64,128]{2,1,0:T(8,128)S(1)} %collective-permute-done.36.refs_2_), channel_id=1, source_target_pairs={{0,2},{1,5},{2,0},{3,7},{4,6},{5,1},{6,4},{7,3},{8,10},{9,13},{10,... | collective-permute-start | bytes 393224 | tf_op jit(solution)/shard_map/ppermute | solution.py:53
  98.1 2.5 %collective-permute-done.51.refs_4_ = f32[4,64,128]{2,1,0:T(8,128)S(1)} collective-permute-done((f32[4,64,128]{2,1,0:T(8,128)S(1)}, f32[4,64,128]{2,1,0:T(8,128)S(1)}, u32[]{:S(2)}, u32[]{:S(2)}) %collective-permute-start.51) | collective-permute-done | bytes 131104 | tf_op jit(solution)/shard_map/ppermute | solution.py:53
  108.3 1.6 %collective-permute-start.40 = (f32[8,64,128]{2,1,0:T(8,128)S(1)}, f32[8,64,128]{2,1,0:T(8,128)S(1)}, u32[]{:S(2)}, u32[]{:S(2)}) collective-permute-start(f32[8,64,128]{2,1,0:T(8,128)S(1)} %get-tuple-element.83), channel_id=1, source_target_pairs={{0,2},{1,5},{2,0},{3,7},{4,6},{5,1},{6,4},{7,3},{8,10},{9,13},{10,... | collective-permute-start | bytes 786440 | tf_op jit(solution)/shard_map/ppermute | solution.py:53
  109.9 1.4 collective-permute-done.53
  111.4 3.4 %collective-permute-done.40 = f32[8,64,128]{2,1,0:T(8,128)S(1)} collective-permute-done((f32[8,64,128]{2,1,0:T(8,128)S(1)}, f32[8,64,128]{2,1,0:T(8,128)S(1)}, u32[]{:S(2)}, u32[]{:S(2)}) %collective-permute-start.40) | collective-permute-done | bytes 262176 | tf_op jit(solution)/shard_map/ppermute | solution.py:53
  114.8 2.1 %collective-permute-start.41 = (f32[4,64,128]{2,1,0:T(8,128)S(1)}, f32[4,64,128]{2,1,0:T(8,128)S(1)}, u32[]{:S(2)}, u32[]{:S(2)}) collective-permute-start(f32[4,64,128]{2,1,0:T(8,128)S(1)} %slice_add_fusion.2), channel_id=1, source_target_pairs={{0,4},{1,3},{2,6},{3,1},{4,0},{5,7},{6,2},{7,5},{8,12},{9,11},{10,... | collective-permute-start | bytes 393224 | tf_op jit(solution)/shard_map/ppermute | solution.py:53
  117.3 2.5 %collective-permute-done.41 = f32[4,64,128]{2,1,0:T(8,128)S(1)} collective-permute-done((f32[4,64,128]{2,1,0:T(8,128)S(1)}, f32[4,64,128]{2,1,0:T(8,128)S(1)}, u32[]{:S(2)}, u32[]{:S(2)}) %collective-permute-start.41) | collective-permute-done | bytes 131104 | tf_op jit(solution)/shard_map/ppermute | solution.py:53
  120.9 2.1 %collective-permute-done.55 = f32[4,64,128]{2,1,0:T(8,128)S(1)} collective-permute-done((f32[4,64,128]{2,1,0:T(8,128)S(1)}, f32[4,64,128]{2,1,0:T(8,128)S(1)}, u32[]{:S(2)}, u32[]{:S(2)}) %collective-permute-start.55) | collective-permute-done | bytes 131104 | tf_op jit(solution)/shard_map/ppermute | solution.py:53
  123.2 1.7 %collective-permute-done.42 = f32[4,64,128]{2,1,0:T(8,128)S(1)} collective-permute-done((f32[4,64,128]{2,1,0:T(8,128)S(1)}, f32[4,64,128]{2,1,0:T(8,128)S(1)}, u32[]{:S(2)}, u32[]{:S(2)}) %collective-permute-start.42) | collective-permute-done | bytes 131104 | tf_op jit(solution)/shard_map/ppermute | solution.py:53
  124.9 2.1 %collective-permute-start.43 = (f32[4,64,128]{2,1,0:T(8,128)S(1)}, f32[4,64,128]{2,1,0:T(8,128)S(1)}, u32[]{:S(2)}, u32[]{:S(2)}) collective-permute-start(f32[4,64,128]{2,1,0:T(8,128)S(1)} %add.86.refs_1_), channel_id=1, source_target_pairs={{0,4},{1,3},{2,6},{3,1},{4,0},{5,7},{6,2},{7,5},{8,12},{9,11},{10,... | collective-permute-start | bytes 393224 | tf_op jit(solution)/shard_map/ppermute | solution.py:53
  127.1 2.4 %collective-permute-done.56.refs_2_ = f32[4,64,128]{2,1,0:T(8,128)S(1)} collective-permute-done((f32[4,64,128]{2,1,0:T(8,128)S(1)}, f32[4,64,128]{2,1,0:T(8,128)S(1)}, u32[]{:S(2)}, u32[]{:S(2)}) %collective-permute-start.56) | collective-permute-done | bytes 131104 | tf_op jit(solution)/shard_map/ppermute | solution.py:53
  130.7 1.5 %collective-permute-start.45 = (f32[4,64,128]{2,1,0:T(8,128)S(1)}, f32[4,64,128]{2,1,0:T(8,128)S(1)}, u32[]{:S(2)}, u32[]{:S(2)}) collective-permute-start(f32[4,64,128]{2,1,0:T(8,128)S(1)} %collective-permute-done.43.refs_2_), channel_id=1, source_target_pairs={{0,2},{1,5},{2,0},{3,7},{4,6},{5,1},{6,4},{7,3},{8,10},{9,13},{10,... | collective-permute-start | bytes 393224 | tf_op jit(solution)/shard_map/ppermute | solution.py:53
  132.3 1.3 collective-permute-done.57.refs_3_
  133.5 1.4 %collective-permute-done.58.refs_4_ = f32[4,64,128]{2,1,0:T(8,128)S(1)} collective-permute-done((f32[4,64,128]{2,1,0:T(8,128)S(1)}, f32[4,64,128]{2,1,0:T(8,128)S(1)}, u32[]{:S(2)}, u32[]{:S(2)}) %collective-permute-start.58) | collective-permute-done | bytes 131104 | tf_op jit(solution)/shard_map/ppermute | solution.py:53
  137.7 1.2 collective-permute-done.46.refs_1_
  (151 shorter events, 41.5 us)
Async XLA Ops:
  3.0 6.3 %collective-permute-start.2 = (f32[32,1152]{1,0:T(8,128)S(1)}, f32[32,1152]{1,0:T(8,128)S(1)}, u32[]{:S(2)}, u32[]{:S(2)}) collective-permute-start(f32[32,1152]{1,0:T(8,128)S(1)} %get-tuple-element.53), channel_id=1, source_target_pairs={{0,2},{1,5},{2,0},{3,7},{4,6},{5,1},{6,4},{7,3},{8,10},{9,13},{10,... | collective-permute-start | bytes 442376 | tf_op jit(solution)/shard_map/ppermute | solution.py:53
  10.8 6.5 %collective-permute-start.4 = (f32[2,4,64,128]{3,2,1,0:T(8,128)S(1)}, f32[2,4,64,128]{3,2,1,0:T(8,128)S(1)}, u32[]{:S(2)}, u32[]{:S(2)}) collective-permute-start(f32[2,4,64,128]{3,2,1,0:T(8,128)S(1)} %get-tuple-element.56), channel_id=1, source_target_pairs={{0,4},{1,3},{2,6},{3,1},{4,0},{5,7},{6,2},{7,5},{8,12},{9,11},{10,... | collective-permute-start | bytes 786440 | tf_op jit(solution)/shard_map/ppermute | solution.py:53
  14.3 14.9 %collective-permute-start = (f32[2048,128]{1,0:T(8,128)S(1)}, f32[2048,128]{1,0:T(8,128)S(1)}, u32[]{:S(2)}, u32[]{:S(2)}) collective-permute-start(f32[2048,128]{1,0:T(8,128)S(1)} %get-tuple-element.49), channel_id=1, source_target_pairs={{0,1},{1,0},{2,3},{3,2},{4,5},{5,4},{6,7},{7,6},{8,9},{9,8},{10,11... | collective-permute-start | bytes 3145736 | tf_op jit(solution)/shard_map/ppermute | solution.py:53
  17.3 5.1 %collective-permute-start.5 = (f32[2,2,64,128]{3,2,1,0:T(8,128)S(1)}, f32[2,2,64,128]{3,2,1,0:T(8,128)S(1)}, u32[]{:S(2)}, u32[]{:S(2)}) collective-permute-start(f32[2,2,64,128]{3,2,1,0:T(8,128)S(1)} %slice.125), channel_id=1, source_target_pairs={{0,8},{1,9},{2,10},{3,11},{4,12},{5,13},{6,14},{7,15},{8,0},{9,1},... | collective-permute-start | bytes 393224 | tf_op jit(solution)/shard_map/ppermute | solution.py:53
  19.5 6.0 %collective-permute-start.7 = (f32[32,1024]{1,0:T(8,128)S(1)}, f32[32,1024]{1,0:T(8,128)S(1)}, u32[]{:S(2)}, u32[]{:S(2)}) collective-permute-start(f32[32,1024]{1,0:T(8,128)S(1)} %get-tuple-element.58), channel_id=1, source_target_pairs={{0,1},{1,0},{2,3},{3,2},{4,5},{5,4},{6,7},{7,6},{8,9},{9,8},{10,11... | collective-permute-start | bytes 393224 | tf_op jit(solution)/shard_map/ppermute | solution.py:53
  19.6 5.9 %collective-permute-start.8 = (f32[32,1024]{1,0:T(8,128)S(1)}, f32[32,1024]{1,0:T(8,128)S(1)}, u32[]{:S(2)}, u32[]{:S(2)}) collective-permute-start(f32[32,1024]{1,0:T(8,128)S(1)} %get-tuple-element.59), channel_id=1, source_target_pairs={{0,2},{1,5},{2,0},{3,7},{4,6},{5,1},{6,4},{7,3},{8,10},{9,13},{10,... | collective-permute-start | bytes 393224 | tf_op jit(solution)/shard_map/ppermute | solution.py:53
  21.1 4.9 %collective-permute-start.9 = (f32[32,1024]{1,0:T(8,128)S(1)}, f32[32,1024]{1,0:T(8,128)S(1)}, u32[]{:S(2)}, u32[]{:S(2)}) collective-permute-start(f32[32,1024]{1,0:T(8,128)S(1)} %get-tuple-element.60), channel_id=1, source_target_pairs={{0,5},{1,2},{2,7},{3,0},{4,1},{5,6},{6,3},{7,4},{8,13},{9,10},{10,... | collective-permute-start | bytes 393224 | tf_op jit(solution)/shard_map/ppermute | solution.py:53
  22.5 5.3 %collective-permute-start.6 = (f32[2,1,64,128]{3,2,1,0:T(8,128)S(1)}, f32[2,1,64,128]{3,2,1,0:T(8,128)S(1)}, u32[]{:S(2)}, u32[]{:S(2)}) collective-permute-start(f32[2,1,64,128]{3,2,1,0:T(8,128)S(1)} %slice.126), channel_id=1, source_target_pairs={{0,16},{1,17},{2,18},{3,19},{4,20},{5,21},{6,22},{7,23},{8,24},{9,... | collective-permute-start | bytes 196616 | tf_op jit(solution)/shard_map/ppermute | solution.py:53
  30.2 8.0 %collective-permute-start.22 = (f32[8,64,128]{2,1,0:T(8,128)S(1)}, f32[8,64,128]{2,1,0:T(8,128)S(1)}, u32[]{:S(2)}, u32[]{:S(2)}) collective-permute-start(f32[8,64,128]{2,1,0:T(8,128)S(1)} %get-tuple-element.72), channel_id=1, source_target_pairs={{0,4},{1,3},{2,6},{3,1},{4,0},{5,7},{6,2},{7,5},{8,12},{9,11},{10,... | collective-permute-start | bytes 786440 | tf_op jit(solution)/shard_map/ppermute | solution.py:53
  32.8 7.9 %collective-permute-start.11 = (f32[8,64,128]{2,1,0:T(8,128)S(1)}, f32[8,64,128]{2,1,0:T(8,128)S(1)}, u32[]{:S(2)}, u32[]{:S(2)}) collective-permute-start(f32[8,64,128]{2,1,0:T(8,128)S(1)} %get-tuple-element.62), channel_id=1, source_target_pairs={{0,2},{1,5},{2,0},{3,7},{4,6},{5,1},{6,4},{7,3},{8,10},{9,13},{10,... | collective-permute-start | bytes 786440 | tf_op jit(solution)/shard_map/ppermute | solution.py:53
  34.5 36.0 %collective-permute-start.20 = (f32[2048,256]{1,0:T(8,128)S(1)}, f32[2048,256]{1,0:T(8,128)S(1)}, u32[]{:S(2)}, u32[]{:S(2)}) collective-permute-start(f32[2048,256]{1,0:T(8,128)S(1)} %get-tuple-element.67), channel_id=1, source_target_pairs={{0,1},{1,0},{2,3},{3,2},{4,5},{5,4},{6,7},{7,6},{8,9},{9,8},{10,11... | collective-permute-start | bytes 6291464 | tf_op jit(solution)/shard_map/ppermute | solution.py:53
  35.4 35.7 %collective-permute-start.19 = (f32[256,2048]{1,0:T(8,128)S(1)}, f32[256,2048]{1,0:T(8,128)S(1)}, u32[]{:S(2)}, u32[]{:S(2)}) collective-permute-start(f32[256,2048]{1,0:T(8,128)S(1)} %get-tuple-element.65), channel_id=1, source_target_pairs={{0,1},{1,0},{2,3},{3,2},{4,5},{5,4},{6,7},{7,6},{8,9},{9,8},{10,11... | collective-permute-start | bytes 6291464 | tf_op jit(solution)/shard_map/ppermute | solution.py:53
  38.3 6.6 %collective-permute-start.23 = (f32[4,64,128]{2,1,0:T(8,128)S(1)}, f32[4,64,128]{2,1,0:T(8,128)S(1)}, u32[]{:S(2)}, u32[]{:S(2)}) collective-permute-start(f32[4,64,128]{2,1,0:T(8,128)S(1)} %slice_add_fusion.4), channel_id=1, source_target_pairs={{0,2},{1,5},{2,0},{3,7},{4,6},{5,1},{6,4},{7,3},{8,10},{9,13},{10,... | collective-permute-start | bytes 393224 | tf_op jit(solution)/shard_map/ppermute | solution.py:53
  40.7 6.1 %collective-permute-start.12 = (f32[4,64,128]{2,1,0:T(8,128)S(1)}, f32[4,64,128]{2,1,0:T(8,128)S(1)}, u32[]{:S(2)}, u32[]{:S(2)}) collective-permute-start(f32[4,64,128]{2,1,0:T(8,128)S(1)} %slice_add_fusion.6), channel_id=1, source_target_pairs={{0,4},{1,3},{2,6},{3,1},{4,0},{5,7},{6,2},{7,5},{8,12},{9,11},{10,... | collective-permute-start | bytes 393224 | tf_op jit(solution)/shard_map/ppermute | solution.py:53
  46.9 6.0 %collective-permute-start.13 = (f32[2,64,128]{2,1,0:T(8,128)S(1)}, f32[2,64,128]{2,1,0:T(8,128)S(1)}, u32[]{:S(2)}, u32[]{:S(2)}) collective-permute-start(f32[2,64,128]{2,1,0:T(8,128)S(1)} %slice.132), channel_id=1, source_target_pairs={{0,8},{1,9},{2,10},{3,11},{4,12},{5,13},{6,14},{7,15},{8,0},{9,1},... | collective-permute-start | bytes 196616 | tf_op jit(solution)/shard_map/ppermute | solution.py:53
  49.3 6.1 %collective-permute-start.25 = (f32[2,64,128]{2,1,0:T(8,128)S(1)}, f32[2,64,128]{2,1,0:T(8,128)S(1)}, u32[]{:S(2)}, u32[]{:S(2)}) collective-permute-start(f32[2,64,128]{2,1,0:T(8,128)S(1)} %pad_maximum_fusion.7), channel_id=1, source_target_pairs={{0,16},{1,17},{2,18},{3,19},{4,20},{5,21},{6,22},{7,23},{8,24},{9,... | collective-permute-start | bytes 196616 | tf_op jit(solution)/shard_map/ppermute | solution.py:53
  52.9 5.2 %collective-permute-start.14 = (f32[2,64,128]{2,1,0:T(8,128)S(1)}, f32[2,64,128]{2,1,0:T(8,128)S(1)}, u32[]{:S(2)}, u32[]{:S(2)}) collective-permute-start(f32[2,64,128]{2,1,0:T(8,128)S(1)} %pad_maximum_fusion.6), channel_id=1, source_target_pairs={{0,16},{1,17},{2,18},{3,19},{4,20},{5,21},{6,22},{7,23},{8,24},{9,... | collective-permute-start | bytes 196616 | tf_op jit(solution)/shard_map/ppermute | solution.py:53
  55.3 5.0 %collective-permute-start.26 = (f32[2,64,128]{2,1,0:T(8,128)S(1)}, f32[2,64,128]{2,1,0:T(8,128)S(1)}, u32[]{:S(2)}, u32[]{:S(2)}) collective-permute-start(f32[2,64,128]{2,1,0:T(8,128)S(1)} %add.80), channel_id=1, source_target_pairs={{0,8},{1,9},{2,10},{3,11},{4,12},{5,13},{6,14},{7,15},{8,0},{9,1},... | collective-permute-start | bytes 196616 | tf_op jit(solution)/shard_map/ppermute | solution.py:53
  60.3 6.5 %collective-permute-start.27 = (f32[4,64,128]{2,1,0:T(8,128)S(1)}, f32[4,64,128]{2,1,0:T(8,128)S(1)}, u32[]{:S(2)}, u32[]{:S(2)}) collective-permute-start(f32[4,64,128]{2,1,0:T(8,128)S(1)} %pad_maximum_fusion.1.refs_1_), channel_id=1, source_target_pairs={{0,2},{1,5},{2,0},{3,7},{4,6},{5,1},{6,4},{7,3},{8,10},{9,13},{10,... | collective-permute-start | bytes 393224 | tf_op jit(solution)/shard_map/ppermute | solution.py:53
  62.6 6.5 %collective-permute-start.16 = (f32[4,64,128]{2,1,0:T(8,128)S(1)}, f32[4,64,128]{2,1,0:T(8,128)S(1)}, u32[]{:S(2)}, u32[]{:S(2)}) collective-permute-start(f32[4,64,128]{2,1,0:T(8,128)S(1)} %pad_maximum_fusion.refs_1_), channel_id=1, source_target_pairs={{0,4},{1,3},{2,6},{3,1},{4,0},{5,7},{6,2},{7,5},{8,12},{9,11},{10,... | collective-permute-start | bytes 393224 | tf_op jit(solution)/shard_map/ppermute | solution.py:53
  64.7 14.8 %collective-permute-start.31 = (f32[2,4,64,128]{3,2,1,0:T(8,128)S(1)}, f32[2,4,64,128]{3,2,1,0:T(8,128)S(1)}, u32[]{:S(2)}, u32[]{:S(2)}) collective-permute-start(f32[2,4,64,128]{3,2,1,0:T(8,128)S(1)} %get-tuple-element.79), channel_id=1, source_target_pairs={{0,4},{1,3},{2,6},{3,1},{4,0},{5,7},{6,2},{7,5},{8,12},{9,11},{10,... | collective-permute-start | bytes 786440 | tf_op jit(solution)/shard_map/ppermute | solution.py:53
  66.8 6.7 %collective-permute-start.28 = (f32[4,64,128]{2,1,0:T(8,128)S(1)}, f32[4,64,128]{2,1,0:T(8,128)S(1)}, u32[]{:S(2)}, u32[]{:S(2)}) collective-permute-start(f32[4,64,128]{2,1,0:T(8,128)S(1)} %pad_maximum_fusion.1.refs_1_), channel_id=1, source_target_pairs={{0,4},{1,3},{2,6},{3,1},{4,0},{5,7},{6,2},{7,5},{8,12},{9,11},{10,... | collective-permute-start | bytes 393224 | tf_op jit(solution)/shard_map/ppermute | solution.py:53
  69.0 5.7 %collective-permute-start.29 = (f32[4,64,128]{2,1,0:T(8,128)S(1)}, f32[4,64,128]{2,1,0:T(8,128)S(1)}, u32[]{:S(2)}, u32[]{:S(2)}) collective-permute-start(f32[4,64,128]{2,1,0:T(8,128)S(1)} %collective-permute-done.27.refs_2_), channel_id=1, source_target_pairs={{0,4},{1,3},{2,6},{3,1},{4,0},{5,7},{6,2},{7,5},{8,12},{9,11},{10,... | collective-permute-start | bytes 393224 | tf_op jit(solution)/shard_map/ppermute | solution.py:53
  70.6 5.0 %collective-permute-start.17 = (f32[4,64,128]{2,1,0:T(8,128)S(1)}, f32[4,64,128]{2,1,0:T(8,128)S(1)}, u32[]{:S(2)}, u32[]{:S(2)}) collective-permute-start(f32[4,64,128]{2,1,0:T(8,128)S(1)} %pad_maximum_fusion.refs_1_), channel_id=1, source_target_pairs={{0,2},{1,5},{2,0},{3,7},{4,6},{5,1},{6,4},{7,3},{8,10},{9,13},{10,... | collective-permute-start | bytes 393224 | tf_op jit(solution)/shard_map/ppermute | solution.py:53
  71.0 5.9 %collective-permute-start.18 = (f32[4,64,128]{2,1,0:T(8,128)S(1)}, f32[4,64,128]{2,1,0:T(8,128)S(1)}, u32[]{:S(2)}, u32[]{:S(2)}) collective-permute-start(f32[4,64,128]{2,1,0:T(8,128)S(1)} %collective-permute-done.16.refs_2_), channel_id=1, source_target_pairs={{0,2},{1,5},{2,0},{3,7},{4,6},{5,1},{6,4},{7,3},{8,10},{9,13},{10,... | collective-permute-start | bytes 393224 | tf_op jit(solution)/shard_map/ppermute | solution.py:53
  77.8 5.5 %collective-permute-start.47 = (f32[1,64,128]{2,1,0:T(8,128)S(1)}, f32[1,64,128]{2,1,0:T(8,128)S(1)}, u32[]{:S(2)}, u32[]{:S(2)}) collective-permute-start(f32[1,64,128]{2,1,0:T(8,128)S(1)} %add.87), channel_id=1, source_target_pairs={{0,16},{1,17},{2,18},{3,19},{4,20},{5,21},{6,22},{7,23},{8,24},{9,... | collective-permute-start | bytes 98312 | tf_op jit(solution)/shard_map/ppermute | solution.py:53
  79.5 9.2 %collective-permute-start.32 = (f32[2,2,64,128]{3,2,1,0:T(8,128)S(1)}, f32[2,2,64,128]{3,2,1,0:T(8,128)S(1)}, u32[]{:S(2)}, u32[]{:S(2)}) collective-permute-start(f32[2,2,64,128]{3,2,1,0:T(8,128)S(1)} %get-tuple-element.81), channel_id=1, source_target_pairs={{0,8},{1,9},{2,10},{3,11},{4,12},{5,13},{6,14},{7,15},{8,0},{9,1},... | collective-permute-start | bytes 393224 | tf_op jit(solution)/shard_map/ppermute | solution.py:53
  81.0 5.2 %collective-permute-start.34 = (f32[1,64,128]{2,1,0:T(8,128)S(1)}, f32[1,64,128]{2,1,0:T(8,128)S(1)}, u32[]{:S(2)}, u32[]{:S(2)}) collective-permute-start(f32[1,64,128]{2,1,0:T(8,128)S(1)} %add.82), channel_id=1, source_target_pairs={{0,16},{1,17},{2,18},{3,19},{4,20},{5,21},{6,22},{7,23},{8,24},{9,... | collective-permute-start | bytes 98312 | tf_op jit(solution)/shard_map/ppermute | solution.py:53
  83.3 5.0 %collective-permute-start.48 = (f32[2,64,128]{2,1,0:T(8,128)S(1)}, f32[2,64,128]{2,1,0:T(8,128)S(1)}, u32[]{:S(2)}, u32[]{:S(2)}) collective-permute-start(f32[2,64,128]{2,1,0:T(8,128)S(1)} %pad_maximum_fusion.9), channel_id=1, source_target_pairs={{0,8},{1,9},{2,10},{3,11},{4,12},{5,13},{6,14},{7,15},{8,0},{9,1},... | collective-permute-start | bytes 196616 | tf_op jit(solution)/shard_map/ppermute | solution.py:53
  88.3 6.4 %collective-permute-start.49 = (f32[4,64,128]{2,1,0:T(8,128)S(1)}, f32[4,64,128]{2,1,0:T(8,128)S(1)}, u32[]{:S(2)}, u32[]{:S(2)}) collective-permute-start(f32[4,64,128]{2,1,0:T(8,128)S(1)} %pad_maximum_fusion.4.refs_1_), channel_id=1, source_target_pairs={{0,2},{1,5},{2,0},{3,7},{4,6},{5,1},{6,4},{7,3},{8,10},{9,13},{10,... | collective-permute-start | bytes 393224 | tf_op jit(solution)/shard_map/ppermute | solution.py:53
  88.8 12.9 %collective-permute-start.33 = (f32[2,2,64,128]{3,2,1,0:T(8,128)S(1)}, f32[2,2,64,128]{3,2,1,0:T(8,128)S(1)}, u32[]{:S(2)}, u32[]{:S(2)}) collective-permute-start(f32[2,2,64,128]{3,2,1,0:T(8,128)S(1)} %add.81), channel_id=1, source_target_pairs={{0,1},{1,0},{2,3},{3,2},{4,5},{5,4},{6,7},{7,6},{8,9},{9,8},{10,11... | collective-permute-start | bytes 393224 | tf_op jit(solution)/shard_map/ppermute | solution.py:53
  88.9 9.2 %collective-permute-start.50 = (f32[4,64,128]{2,1,0:T(8,128)S(1)}, f32[4,64,128]{2,1,0:T(8,128)S(1)}, u32[]{:S(2)}, u32[]{:S(2)}) collective-permute-start(f32[4,64,128]{2,1,0:T(8,128)S(1)} %pad_maximum_fusion.4.refs_1_), channel_id=1, source_target_pairs={{0,4},{1,3},{2,6},{3,1},{4,0},{5,7},{6,2},{7,5},{8,12},{9,11},{10,... | collective-permute-start | bytes 393224 | tf_op jit(solution)/shard_map/ppermute | solution.py:53
  90.4 5.6 %collective-permute-start.36 = (f32[4,64,128]{2,1,0:T(8,128)S(1)}, f32[4,64,128]{2,1,0:T(8,128)S(1)}, u32[]{:S(2)}, u32[]{:S(2)}) collective-permute-start(f32[4,64,128]{2,1,0:T(8,128)S(1)} %pad_maximum_fusion.2.refs_1_), channel_id=1, source_target_pairs={{0,4},{1,3},{2,6},{3,1},{4,0},{5,7},{6,2},{7,5},{8,12},{9,11},{10,... | collective-permute-start | bytes 393224 | tf_op jit(solution)/shard_map/ppermute | solution.py:53
  94.7 5.9 %collective-permute-start.51 = (f32[4,64,128]{2,1,0:T(8,128)S(1)}, f32[4,64,128]{2,1,0:T(8,128)S(1)}, u32[]{:S(2)}, u32[]{:S(2)}) collective-permute-start(f32[4,64,128]{2,1,0:T(8,128)S(1)} %collective-permute-done.49.refs_2_), channel_id=1, source_target_pairs={{0,4},{1,3},{2,6},{3,1},{4,0},{5,7},{6,2},{7,5},{8,12},{9,11},{10,... | collective-permute-start | bytes 393224 | tf_op jit(solution)/shard_map/ppermute | solution.py:53
  94.7 10.2 %collective-permute-start.37 = (f32[4,64,128]{2,1,0:T(8,128)S(1)}, f32[4,64,128]{2,1,0:T(8,128)S(1)}, u32[]{:S(2)}, u32[]{:S(2)}) collective-permute-start(f32[4,64,128]{2,1,0:T(8,128)S(1)} %pad_maximum_fusion.2.refs_1_), channel_id=1, source_target_pairs={{0,2},{1,5},{2,0},{3,7},{4,6},{5,1},{6,4},{7,3},{8,10},{9,13},{10,... | collective-permute-start | bytes 393224 | tf_op jit(solution)/shard_map/ppermute | solution.py:53
  96.0 8.9 %collective-permute-start.38 = (f32[4,64,128]{2,1,0:T(8,128)S(1)}, f32[4,64,128]{2,1,0:T(8,128)S(1)}, u32[]{:S(2)}, u32[]{:S(2)}) collective-permute-start(f32[4,64,128]{2,1,0:T(8,128)S(1)} %collective-permute-done.36.refs_2_), channel_id=1, source_target_pairs={{0,2},{1,5},{2,0},{3,7},{4,6},{5,1},{6,4},{7,3},{8,10},{9,13},{10,... | collective-permute-start | bytes 393224 | tf_op jit(solution)/shard_map/ppermute | solution.py:53
  104.8 6.4 %collective-permute-start.53 = (f32[8,64,128]{2,1,0:T(8,128)S(1)}, f32[8,64,128]{2,1,0:T(8,128)S(1)}, u32[]{:S(2)}, u32[]{:S(2)}) collective-permute-start(f32[8,64,128]{2,1,0:T(8,128)S(1)} %get-tuple-element.88), channel_id=1, source_target_pairs={{0,4},{1,3},{2,6},{3,1},{4,0},{5,7},{6,2},{7,5},{8,12},{9,11},{10,... | collective-permute-start | bytes 786440 | tf_op jit(solution)/shard_map/ppermute | solution.py:53
  108.3 6.4 %collective-permute-start.40 = (f32[8,64,128]{2,1,0:T(8,128)S(1)}, f32[8,64,128]{2,1,0:T(8,128)S(1)}, u32[]{:S(2)}, u32[]{:S(2)}) collective-permute-start(f32[8,64,128]{2,1,0:T(8,128)S(1)} %get-tuple-element.83), channel_id=1, source_target_pairs={{0,2},{1,5},{2,0},{3,7},{4,6},{5,1},{6,4},{7,3},{8,10},{9,13},{10,... | collective-permute-start | bytes 786440 | tf_op jit(solution)/shard_map/ppermute | solution.py:53
  111.3 5.6 %collective-permute-start.54 = (f32[4,64,128]{2,1,0:T(8,128)S(1)}, f32[4,64,128]{2,1,0:T(8,128)S(1)}, u32[]{:S(2)}, u32[]{:S(2)}) collective-permute-start(f32[4,64,128]{2,1,0:T(8,128)S(1)} %slice_add_fusion), channel_id=1, source_target_pairs={{0,2},{1,5},{2,0},{3,7},{4,6},{5,1},{6,4},{7,3},{8,10},{9,13},{10,... | collective-permute-start | bytes 393224 | tf_op jit(solution)/shard_map/ppermute | solution.py:53
  114.8 5.0 %collective-permute-start.41 = (f32[4,64,128]{2,1,0:T(8,128)S(1)}, f32[4,64,128]{2,1,0:T(8,128)S(1)}, u32[]{:S(2)}, u32[]{:S(2)}) collective-permute-start(f32[4,64,128]{2,1,0:T(8,128)S(1)} %slice_add_fusion.2), channel_id=1, source_target_pairs={{0,4},{1,3},{2,6},{3,1},{4,0},{5,7},{6,2},{7,5},{8,12},{9,11},{10,... | collective-permute-start | bytes 393224 | tf_op jit(solution)/shard_map/ppermute | solution.py:53
  116.9 6.1 %collective-permute-start.55 = (f32[4,64,128]{2,1,0:T(8,128)S(1)}, f32[4,64,128]{2,1,0:T(8,128)S(1)}, u32[]{:S(2)}, u32[]{:S(2)}) collective-permute-start(f32[4,64,128]{2,1,0:T(8,128)S(1)} %pad_maximum_fusion.5), channel_id=1, source_target_pairs={{0,8},{1,9},{2,10},{3,11},{4,12},{5,13},{6,14},{7,15},{8,0},{9,1},... | collective-permute-start | bytes 393224 | tf_op jit(solution)/shard_map/ppermute | solution.py:53
  119.9 5.0 %collective-permute-start.42 = (f32[4,64,128]{2,1,0:T(8,128)S(1)}, f32[4,64,128]{2,1,0:T(8,128)S(1)}, u32[]{:S(2)}, u32[]{:S(2)}) collective-permute-start(f32[4,64,128]{2,1,0:T(8,128)S(1)} %pad_maximum_fusion.3), channel_id=1, source_target_pairs={{0,8},{1,9},{2,10},{3,11},{4,12},{5,13},{6,14},{7,15},{8,0},{9,1},... | collective-permute-start | bytes 393224 | tf_op jit(solution)/shard_map/ppermute | solution.py:53
  123.1 6.4 %collective-permute-start.56 = (f32[4,64,128]{2,1,0:T(8,128)S(1)}, f32[4,64,128]{2,1,0:T(8,128)S(1)}, u32[]{:S(2)}, u32[]{:S(2)}) collective-permute-start(f32[4,64,128]{2,1,0:T(8,128)S(1)} %add.91.refs_1_), channel_id=1, source_target_pairs={{0,2},{1,5},{2,0},{3,7},{4,6},{5,1},{6,4},{7,3},{8,10},{9,13},{10,... | collective-permute-start | bytes 393224 | tf_op jit(solution)/shard_map/ppermute | solution.py:53
  124.9 5.8 %collective-permute-start.43 = (f32[4,64,128]{2,1,0:T(8,128)S(1)}, f32[4,64,128]{2,1,0:T(8,128)S(1)}, u32[]{:S(2)}, u32[]{:S(2)}) collective-permute-start(f32[4,64,128]{2,1,0:T(8,128)S(1)} %add.86.refs_1_), channel_id=1, source_target_pairs={{0,4},{1,3},{2,6},{3,1},{4,0},{5,7},{6,2},{7,5},{8,12},{9,11},{10,... | collective-permute-start | bytes 393224 | tf_op jit(solution)/shard_map/ppermute | solution.py:53
  127.0 6.5 %collective-permute-start.57 = (f32[4,64,128]{2,1,0:T(8,128)S(1)}, f32[4,64,128]{2,1,0:T(8,128)S(1)}, u32[]{:S(2)}, u32[]{:S(2)}) collective-permute-start(f32[4,64,128]{2,1,0:T(8,128)S(1)} %add.91.refs_1_), channel_id=1, source_target_pairs={{0,4},{1,3},{2,6},{3,1},{4,0},{5,7},{6,2},{7,5},{8,12},{9,11},{10,... | collective-permute-start | bytes 393224 | tf_op jit(solution)/shard_map/ppermute | solution.py:53
  129.5 5.5 %collective-permute-start.58 = (f32[4,64,128]{2,1,0:T(8,128)S(1)}, f32[4,64,128]{2,1,0:T(8,128)S(1)}, u32[]{:S(2)}, u32[]{:S(2)}) collective-permute-start(f32[4,64,128]{2,1,0:T(8,128)S(1)} %collective-permute-done.56.refs_2_), channel_id=1, source_target_pairs={{0,4},{1,3},{2,6},{3,1},{4,0},{5,7},{6,2},{7,5},{8,12},{9,11},{10,... | collective-permute-start | bytes 393224 | tf_op jit(solution)/shard_map/ppermute | solution.py:53
  130.2 5.8 %collective-permute-start.44 = (f32[4,64,128]{2,1,0:T(8,128)S(1)}, f32[4,64,128]{2,1,0:T(8,128)S(1)}, u32[]{:S(2)}, u32[]{:S(2)}) collective-permute-start(f32[4,64,128]{2,1,0:T(8,128)S(1)} %add.86.refs_1_), channel_id=1, source_target_pairs={{0,2},{1,5},{2,0},{3,7},{4,6},{5,1},{6,4},{7,3},{8,10},{9,13},{10,... | collective-permute-start | bytes 393224 | tf_op jit(solution)/shard_map/ppermute | solution.py:53
  130.7 5.9 %collective-permute-start.45 = (f32[4,64,128]{2,1,0:T(8,128)S(1)}, f32[4,64,128]{2,1,0:T(8,128)S(1)}, u32[]{:S(2)}, u32[]{:S(2)}) collective-permute-start(f32[4,64,128]{2,1,0:T(8,128)S(1)} %collective-permute-done.43.refs_2_), channel_id=1, source_target_pairs={{0,2},{1,5},{2,0},{3,7},{4,6},{5,1},{6,4},{7,3},{8,10},{9,13},{10,... | collective-permute-start | bytes 393224 | tf_op jit(solution)/shard_map/ppermute | solution.py:53
  (19 other events, 66.1 us)

commit v3 on v2

--- a/solution.py
+++ b/solution.py
@@ -277,7 +277,7 @@
 
 
 def forward(deep, chain, w_ref, *refs):
-    vec, (send_ref, next_ref, keep_ref), (rhs_ref, sum_ref) = refs[:-5], refs[-5:-2], refs[-2:]
+    vec, outs, (rhs_ref, sum_ref) = refs[:-6], refs[-6:-2], refs[-2:]
     blocks = vec[0].shape[0]
     if len(vec) == 2:
         own, other = vec[0][...], vec[1][...]
@@ -294,12 +294,7 @@
         low = sum_ref[pl.ds(start, WIDE), :]
         high = sum_ref[pl.ds(start + WIDE, WIDE), :]
         block = jnp.where(left, low, high)
-        if i < 4:
-            keep_ref[i] = block
-        elif i < 8:
-            next_ref[i - 4] = block
-        else:
-            send_ref[i - 8] = block
+        outs[i // 4][i % 4] = block
 
 
 def backward(deep, chain, w_ref, *refs):
@@ -319,7 +314,7 @@
     m, k = w.shape
     return kernel_call(
         functools.partial(forward, deep, chain),
-        [((8, WIDE, 128), F32), ((4, WIDE, 128), F32), ((4, WIDE, 128), F32)],
+        [((4, WIDE, 128), F32)] * 4,
         [w, *vec],
         [pltpu.VMEM((k, 128), BF16), pltpu.VMEM((m, 128), F32)],
         flops=2 * m * k * 128,
@@ -345,10 +340,11 @@
     return glue(lambda v, g: (v[:, :1] + g,), value, got, after=after)[0]
 
 
-def plane_sum(send, follow, keep, chain):
+def plane_sum(keep, follow, send, send_ahead, chain):
+    ahead = swap_first(send_ahead, chain)
     first = swap_first(send, chain)
-    second = swap_second(follow + first[4:], chain)
-    return keep + first[:4] + second, second
+    second = swap_second(follow + ahead, chain)
+    return keep + first + second, second
 
 
 def depth_total(value, deep):

time: 140 us -> 139 us (level)
  waiting for transfers between devices: 57.4 us -> 52.2 us
  starting transfers between devices: 62.9 us -> 67.3 us
    ppermute x60 -> x64, waiting for transfers between devices: 57.4 us -> 52.2 us  [permute(): return lax.ppermute(value, AXES, [(i, partner(i)) for i in range(32)])]
    ppermute x60 -> x64, starting transfers between devices: 62.9 us -> 67.3 us  [permute(): return lax.ppermute(value, AXES, [(i, partner(i)) for i in range(32)])]
  transfers between devices with their start and end apart: 60 -> 64, of which waited for: 37 -> 36; matrix products, arithmetic and copies ran while one was open for 0% -> 0% of each run, Pallas kernels for 8% -> 8%
where the time goes in v3:
time: 139 us
  starting transfers between devices  67.3 us (48%)
  waiting for transfers between devices  52.2 us (38%)
  Pallas kernels  13.9 us (10%)
  local copies, waits for them, and re-layouts  3.91 us (3%)
    ppermute x64, starting transfers between devices, permute(): return lax.ppermute(value, AXES, [(i, partner(i)) for i in range(32)])  67.3 us
    ppermute x64, waiting for transfers between devices, permute(): return lax.ppermute(value, AXES, [(i, partner(i)) for i in range(32)])  52.2 us
    pallas_call x24, Pallas kernels, kernel_call(): pl.pallas_call(ordered, out_shape=[jax.ShapeDtypeStruct(*o) for o in outs...  13.9 us
    unnamed x14, local copies, waits for them, and re-layouts  3.81 us
  transfers between devices with their start and end apart: 64, of which 36 were waited for; matrix products, arithmetic and copies ran while one was open for 0% of the time, Pallas kernels for 8%

profile of v3, /device:TPU:0, one launch (start us, length us, event | category | flops | bytes accessed | tf_op | source)
XLA Modules:
  0.0 138.9 jit_solution(8330811300957208829)
XLA Ops:
  3.0 2.6 %collective-permute-start.2 = (f32[32,1152]{1,0:T(8,128)S(1)}, f32[32,1152]{1,0:T(8,128)S(1)}, u32[]{:S(2)}, u32[]{:S(2)}) collective-permute-start(f32[32,1152]{1,0:T(8,128)S(1)} %get-tuple-element.57), channel_id=1, source_target_pairs={{0,2},{1,5},{2,0},{3,7},{4,6},{5,1},{6,4},{7,3},{8,10},{9,13},{10,... | collective-permute-start | bytes 442376 | tf_op jit(solution)/shard_map/ppermute | solution.py:53
  5.6 3.6 %collective-permute-done.2.refs_2_ = f32[32,1152]{1,0:T(8,128)S(1)} collective-permute-done((f32[32,1152]{1,0:T(8,128)S(1)}, f32[32,1152]{1,0:T(8,128)S(1)}, u32[]{:S(2)}, u32[]{:S(2)}) %collective-permute-start.2) | collective-permute-done | bytes 147488 | tf_op jit(solution)/shard_map/ppermute | solution.py:53
  10.8 2.1 %collective-permute-start.4 = (f32[2,4,64,128]{3,2,1,0:T(8,128)S(1)}, f32[2,4,64,128]{3,2,1,0:T(8,128)S(1)}, u32[]{:S(2)}, u32[]{:S(2)}) collective-permute-start(f32[2,4,64,128]{3,2,1,0:T(8,128)S(1)} %get-tuple-element.60), channel_id=1, source_target_pairs={{0,4},{1,3},{2,6},{3,1},{4,0},{5,7},{6,2},{7,5},{8,12},{9,11},{10,... | collective-permute-start | bytes 786440 | tf_op jit(solution)/shard_map/ppermute | solution.py:53
  12.9 1.2 copy-done.4
  14.3 2.9 %collective-permute-done.4.refs_1_ = f32[2,4,64,128]{3,2,1,0:T(8,128)S(1)} collective-permute-done((f32[2,4,64,128]{3,2,1,0:T(8,128)S(1)}, f32[2,4,64,128]{3,2,1,0:T(8,128)S(1)}, u32[]{:S(2)}, u32[]{:S(2)}) %collective-permute-start.4) | collective-permute-done | bytes 262176 | tf_op jit(solution)/shard_map/ppermute | solution.py:53
  17.3 2.1 %collective-permute-start.5 = (f32[2,2,64,128]{3,2,1,0:T(8,128)S(1)}, f32[2,2,64,128]{3,2,1,0:T(8,128)S(1)}, u32[]{:S(2)}, u32[]{:S(2)}) collective-permute-start(f32[2,2,64,128]{3,2,1,0:T(8,128)S(1)} %slice.93), channel_id=1, source_target_pairs={{0,8},{1,9},{2,10},{3,11},{4,12},{5,13},{6,14},{7,15},{8,0},{9,1},... | collective-permute-start | bytes 393224 | tf_op jit(solution)/shard_map/ppermute | solution.py:53
  19.6 1.5 %collective-permute-start.8 = (f32[32,1024]{1,0:T(8,128)S(1)}, f32[32,1024]{1,0:T(8,128)S(1)}, u32[]{:S(2)}, u32[]{:S(2)}) collective-permute-start(f32[32,1024]{1,0:T(8,128)S(1)} %get-tuple-element.63), channel_id=1, source_target_pairs={{0,2},{1,5},{2,0},{3,7},{4,6},{5,1},{6,4},{7,3},{8,10},{9,13},{10,... | collective-permute-start | bytes 393224 | tf_op jit(solution)/shard_map/ppermute | solution.py:53
  22.5 3.1 %collective-permute-start.6 = (f32[2,1,64,128]{3,2,1,0:T(8,128)S(1)}, f32[2,1,64,128]{3,2,1,0:T(8,128)S(1)}, u32[]{:S(2)}, u32[]{:S(2)}) collective-permute-start(f32[2,1,64,128]{3,2,1,0:T(8,128)S(1)} %slice.94), channel_id=1, source_target_pairs={{0,16},{1,17},{2,18},{3,19},{4,20},{5,21},{6,22},{7,23},{8,24},{9,... | collective-permute-start | bytes 196616 | tf_op jit(solution)/shard_map/ppermute | solution.py:53
  26.1 1.8 %collective-permute-done.6.refs_1_ = f32[2,1,64,128]{3,2,1,0:T(8,128)S(1)} collective-permute-done((f32[2,1,64,128]{3,2,1,0:T(8,128)S(1)}, f32[2,1,64,128]{3,2,1,0:T(8,128)S(1)}, u32[]{:S(2)}, u32[]{:S(2)}) %collective-permute-start.6) | collective-permute-done | bytes 65568 | tf_op jit(solution)/shard_map/ppermute | solution.py:53
  27.9 1.2 collective-permute-done.10
  30.2 1.9 %collective-permute-start.24 = (f32[4,64,128]{2,1,0:T(8,128)S(1)}, f32[4,64,128]{2,1,0:T(8,128)S(1)}, u32[]{:S(2)}, u32[]{:S(2)}) collective-permute-start(f32[4,64,128]{2,1,0:T(8,128)S(1)} %get-tuple-element.79), channel_id=1, source_target_pairs={{0,4},{1,3},{2,6},{3,1},{4,0},{5,7},{6,2},{7,5},{8,12},{9,11},{10,... | collective-permute-start | bytes 393224 | tf_op jit(solution)/shard_map/ppermute | solution.py:53
  32.8 1.5 %collective-permute-start.12 = (f32[4,64,128]{2,1,0:T(8,128)S(1)}, f32[4,64,128]{2,1,0:T(8,128)S(1)}, u32[]{:S(2)}, u32[]{:S(2)}) collective-permute-start(f32[4,64,128]{2,1,0:T(8,128)S(1)} %get-tuple-element.68), channel_id=1, source_target_pairs={{0,2},{1,5},{2,0},{3,7},{4,6},{5,1},{6,4},{7,3},{8,10},{9,13},{10,... | collective-permute-start | bytes 393224 | tf_op jit(solution)/shard_map/ppermute | solution.py:53
  35.5 2.4 %collective-permute-start.25 = (f32[4,64,128]{2,1,0:T(8,128)S(1)}, f32[4,64,128]{2,1,0:T(8,128)S(1)}, u32[]{:S(2)}, u32[]{:S(2)}) collective-permute-start(f32[4,64,128]{2,1,0:T(8,128)S(1)} %add.77), channel_id=1, source_target_pairs={{0,2},{1,5},{2,0},{3,7},{4,6},{5,1},{6,4},{7,3},{8,10},{9,13},{10,... | collective-permute-start | bytes 393224 | tf_op jit(solution)/shard_map/ppermute | solution.py:53
  40.2 1.4 %collective-permute-start.13 = (f32[4,64,128]{2,1,0:T(8,128)S(1)}, f32[4,64,128]{2,1,0:T(8,128)S(1)}, u32[]{:S(2)}, u32[]{:S(2)}) collective-permute-start(f32[4,64,128]{2,1,0:T(8,128)S(1)} %add.72), channel_id=1, source_target_pairs={{0,4},{1,3},{2,6},{3,1},{4,0},{5,7},{6,2},{7,5},{8,12},{9,11},{10,... | collective-permute-start | bytes 393224 | tf_op jit(solution)/shard_map/ppermute | solution.py:53
  41.6 1.6 %collective-permute-start.26 = (f32[2,64,128]{2,1,0:T(8,128)S(1)}, f32[2,64,128]{2,1,0:T(8,128)S(1)}, u32[]{:S(2)}, u32[]{:S(2)}) collective-permute-start(f32[2,64,128]{2,1,0:T(8,128)S(1)} %slice.104), channel_id=1, source_target_pairs={{0,8},{1,9},{2,10},{3,11},{4,12},{5,13},{6,14},{7,15},{8,0},{9,1},... | collective-permute-start | bytes 196616 | tf_op jit(solution)/shard_map/ppermute | solution.py:53
  43.3 1.7 %collective-permute-done.11 = f32[4,64,128]{2,1,0:T(8,128)S(1)} collective-permute-done((f32[4,64,128]{2,1,0:T(8,128)S(1)}, f32[4,64,128]{2,1,0:T(8,128)S(1)}, u32[]{:S(2)}, u32[]{:S(2)}) %collective-permute-start.11) | collective-permute-done | bytes 131104 | tf_op jit(solution)/shard_map/ppermute | solution.py:53
  45.2 2.4 %collective-permute-start.14 = (f32[2,64,128]{2,1,0:T(8,128)S(1)}, f32[2,64,128]{2,1,0:T(8,128)S(1)}, u32[]{:S(2)}, u32[]{:S(2)}) collective-permute-start(f32[2,64,128]{2,1,0:T(8,128)S(1)} %slice.98), channel_id=1, source_target_pairs={{0,8},{1,9},{2,10},{3,11},{4,12},{5,13},{6,14},{7,15},{8,0},{9,1},... | collective-permute-start | bytes 196616 | tf_op jit(solution)/shard_map/ppermute | solution.py:53
  47.7 3.2 %collective-permute-start.27 = (f32[2,64,128]{2,1,0:T(8,128)S(1)}, f32[2,64,128]{2,1,0:T(8,128)S(1)}, u32[]{:S(2)}, u32[]{:S(2)}) collective-permute-start(f32[2,64,128]{2,1,0:T(8,128)S(1)} %pad_maximum_fusion.7), channel_id=1, source_target_pairs={{0,16},{1,17},{2,18},{3,19},{4,20},{5,21},{6,22},{7,23},{8,24},{9,... | collective-permute-start | bytes 196616 | tf_op jit(solution)/shard_map/ppermute | solution.py:53
  50.9 3.0 %collective-permute-start.15 = (f32[2,64,128]{2,1,0:T(8,128)S(1)}, f32[2,64,128]{2,1,0:T(8,128)S(1)}, u32[]{:S(2)}, u32[]{:S(2)}) collective-permute-start(f32[2,64,128]{2,1,0:T(8,128)S(1)} %pad_maximum_fusion.6), channel_id=1, source_target_pairs={{0,16},{1,17},{2,18},{3,19},{4,20},{5,21},{6,22},{7,23},{8,24},{9,... | collective-permute-start | bytes 196616 | tf_op jit(solution)/shard_map/ppermute | solution.py:53
  53.9 1.5 %collective-permute-done.27 = f32[2,64,128]{2,1,0:T(8,128)S(1)} collective-permute-done((f32[2,64,128]{2,1,0:T(8,128)S(1)}, f32[2,64,128]{2,1,0:T(8,128)S(1)}, u32[]{:S(2)}, u32[]{:S(2)}) %collective-permute-start.27) | collective-permute-done | bytes 65568 | tf_op jit(solution)/shard_map/ppermute | solution.py:53
  56.7 2.4 %collective-permute-start.16 = (f32[2,64,128]{2,1,0:T(8,128)S(1)}, f32[2,64,128]{2,1,0:T(8,128)S(1)}, u32[]{:S(2)}, u32[]{:S(2)}) collective-permute-start(f32[2,64,128]{2,1,0:T(8,128)S(1)} %add.75), channel_id=1, source_target_pairs={{0,8},{1,9},{2,10},{3,11},{4,12},{5,13},{6,14},{7,15},{8,0},{9,1},... | collective-permute-start | bytes 196616 | tf_op jit(solution)/shard_map/ppermute | solution.py:53
  59.1 1.3 collective-permute-done.28
  62.8 1.2 collective-permute-start.33
  64.1 2.8 %collective-permute-done.29.refs_2_ = f32[4,64,128]{2,1,0:T(8,128)S(1)} collective-permute-done((f32[4,64,128]{2,1,0:T(8,128)S(1)}, f32[4,64,128]{2,1,0:T(8,128)S(1)}, u32[]{:S(2)}, u32[]{:S(2)}) %collective-permute-start.29) | collective-permute-done | bytes 131104 | tf_op jit(solution)/shard_map/ppermute | solution.py:53
  67.4 1.4 %collective-permute-start.19 = (f32[4,64,128]{2,1,0:T(8,128)S(1)}, f32[4,64,128]{2,1,0:T(8,128)S(1)}, u32[]{:S(2)}, u32[]{:S(2)}) collective-permute-start(f32[4,64,128]{2,1,0:T(8,128)S(1)} %collective-permute-done.17.refs_2_), channel_id=1, source_target_pairs={{0,2},{1,5},{2,0},{3,7},{4,6},{5,1},{6,4},{7,3},{8,10},{9,13},{10,... | collective-permute-start | bytes 393224 | tf_op jit(solution)/shard_map/ppermute | solution.py:53
  69.1 1.8 %collective-permute-start.31 = (f32[4,64,128]{2,1,0:T(8,128)S(1)}, f32[4,64,128]{2,1,0:T(8,128)S(1)}, u32[]{:S(2)}, u32[]{:S(2)}) collective-permute-start(f32[4,64,128]{2,1,0:T(8,128)S(1)} %collective-permute-done.29.refs_2_), channel_id=1, source_target_pairs={{0,4},{1,3},{2,6},{3,1},{4,0},{5,7},{6,2},{7,5},{8,12},{9,11},{10,... | collective-permute-start | bytes 393224 | tf_op jit(solution)/shard_map/ppermute | solution.py:53
  71.9 1.2 collective-permute-done.18.refs_3_
  73.0 1.4 %collective-permute-done.19.refs_4_ = f32[4,64,128]{2,1,0:T(8,128)S(1)} collective-permute-done((f32[4,64,128]{2,1,0:T(8,128)S(1)}, f32[4,64,128]{2,1,0:T(8,128)S(1)}, u32[]{:S(2)}, u32[]{:S(2)}) %collective-permute-start.19) | collective-permute-done | bytes 131104 | tf_op jit(solution)/shard_map/ppermute | solution.py:53
  77.8 1.9 %collective-permute-start.34 = (f32[2,2,64,128]{3,2,1,0:T(8,128)S(1)}, f32[2,2,64,128]{3,2,1,0:T(8,128)S(1)}, u32[]{:S(2)}, u32[]{:S(2)}) collective-permute-start(f32[2,2,64,128]{3,2,1,0:T(8,128)S(1)} %get-tuple-element.87), channel_id=1, source_target_pairs={{0,8},{1,9},{2,10},{3,11},{4,12},{5,13},{6,14},{7,15},{8,0},{9,1},... | collective-permute-start | bytes 393224 | tf_op jit(solution)/shard_map/ppermute | solution.py:53
  80.2 1.6 %collective-permute-done.36 = f32[1,64,128]{2,1,0:T(8,128)S(1)} collective-permute-done((f32[1,64,128]{2,1,0:T(8,128)S(1)}, f32[1,64,128]{2,1,0:T(8,128)S(1)}, u32[]{:S(2)}, u32[]{:S(2)}) %collective-permute-start.36) | collective-permute-done | bytes 32800 | tf_op jit(solution)/shard_map/ppermute | solution.py:53
  81.9 2.7 %collective-permute-done.50 = f32[1,64,128]{2,1,0:T(8,128)S(1)} collective-permute-done((f32[1,64,128]{2,1,0:T(8,128)S(1)}, f32[1,64,128]{2,1,0:T(8,128)S(1)}, u32[]{:S(2)}, u32[]{:S(2)}) %collective-permute-start.50) | collective-permute-done | bytes 32800 | tf_op jit(solution)/shard_map/ppermute | solution.py:53
  86.1 1.4 %collective-permute-start.38 = (f32[4,64,128]{2,1,0:T(8,128)S(1)}, f32[4,64,128]{2,1,0:T(8,128)S(1)}, u32[]{:S(2)}, u32[]{:S(2)}) collective-permute-start(f32[4,64,128]{2,1,0:T(8,128)S(1)} %pad_maximum_fusion.2.refs_1_), channel_id=1, source_target_pairs={{0,4},{1,3},{2,6},{3,1},{4,0},{5,7},{6,2},{7,5},{8,12},{9,11},{10,... | collective-permute-start | bytes 393224 | tf_op jit(solution)/shard_map/ppermute | solution.py:53
  87.5 1.4 %collective-permute-done.51 = f32[2,64,128]{2,1,0:T(8,128)S(1)} collective-permute-done((f32[2,64,128]{2,1,0:T(8,128)S(1)}, f32[2,64,128]{2,1,0:T(8,128)S(1)}, u32[]{:S(2)}, u32[]{:S(2)}) %collective-permute-start.51) | collective-permute-done | bytes 65568 | tf_op jit(solution)/shard_map/ppermute | solution.py:53
  88.9 2.2 %collective-permute-start.52 = (f32[4,64,128]{2,1,0:T(8,128)S(1)}, f32[4,64,128]{2,1,0:T(8,128)S(1)}, u32[]{:S(2)}, u32[]{:S(2)}) collective-permute-start(f32[4,64,128]{2,1,0:T(8,128)S(1)} %pad_maximum_fusion.4.refs_1_), channel_id=1, source_target_pairs={{0,2},{1,5},{2,0},{3,7},{4,6},{5,1},{6,4},{7,3},{8,10},{9,13},{10,... | collective-permute-start | bytes 393224 | tf_op jit(solution)/shard_map/ppermute | solution.py:53
  91.3 1.6 %collective-permute-start.53 = (f32[4,64,128]{2,1,0:T(8,128)S(1)}, f32[4,64,128]{2,1,0:T(8,128)S(1)}, u32[]{:S(2)}, u32[]{:S(2)}) collective-permute-start(f32[4,64,128]{2,1,0:T(8,128)S(1)} %pad_maximum_fusion.4.refs_1_), channel_id=1, source_target_pairs={{0,4},{1,3},{2,6},{3,1},{4,0},{5,7},{6,2},{7,5},{8,12},{9,11},{10,... | collective-permute-start | bytes 393224 | tf_op jit(solution)/shard_map/ppermute | solution.py:53
  94.1 1.6 %collective-permute-start.54 = (f32[4,64,128]{2,1,0:T(8,128)S(1)}, f32[4,64,128]{2,1,0:T(8,128)S(1)}, u32[]{:S(2)}, u32[]{:S(2)}) collective-permute-start(f32[4,64,128]{2,1,0:T(8,128)S(1)} %collective-permute-done.52.refs_2_), channel_id=1, source_target_pairs={{0,4},{1,3},{2,6},{3,1},{4,0},{5,7},{6,2},{7,5},{8,12},{9,11},{10,... | collective-permute-start | bytes 393224 | tf_op jit(solution)/shard_map/ppermute | solution.py:53
  95.7 2.0 %collective-permute-done.39.refs_3_ = f32[4,64,128]{2,1,0:T(8,128)S(1)} collective-permute-done((f32[4,64,128]{2,1,0:T(8,128)S(1)}, f32[4,64,128]{2,1,0:T(8,128)S(1)}, u32[]{:S(2)}, u32[]{:S(2)}) %collective-permute-start.39) | collective-permute-done | bytes 131104 | tf_op jit(solution)/shard_map/ppermute | solution.py:53
  97.7 2.6 %collective-permute-done.40.refs_4_ = f32[4,64,128]{2,1,0:T(8,128)S(1)} collective-permute-done((f32[4,64,128]{2,1,0:T(8,128)S(1)}, f32[4,64,128]{2,1,0:T(8,128)S(1)}, u32[]{:S(2)}, u32[]{:S(2)}) %collective-permute-start.40) | collective-permute-done | bytes 131104 | tf_op jit(solution)/shard_map/ppermute | solution.py:53
  104.0 1.5 %collective-permute-start.43 = (f32[4,64,128]{2,1,0:T(8,128)S(1)}, f32[4,64,128]{2,1,0:T(8,128)S(1)}, u32[]{:S(2)}, u32[]{:S(2)}) collective-permute-start(f32[4,64,128]{2,1,0:T(8,128)S(1)} %get-tuple-element.91), channel_id=1, source_target_pairs={{0,2},{1,5},{2,0},{3,7},{4,6},{5,1},{6,4},{7,3},{8,10},{9,13},{10,... | collective-permute-start | bytes 393224 | tf_op jit(solution)/shard_map/ppermute | solution.py:53
  109.3 1.5 %collective-permute-start.44 = (f32[4,64,128]{2,1,0:T(8,128)S(1)}, f32[4,64,128]{2,1,0:T(8,128)S(1)}, u32[]{:S(2)}, u32[]{:S(2)}) collective-permute-start(f32[4,64,128]{2,1,0:T(8,128)S(1)} %add.84), channel_id=1, source_target_pairs={{0,4},{1,3},{2,6},{3,1},{4,0},{5,7},{6,2},{7,5},{8,12},{9,11},{10,... | collective-permute-start | bytes 393224 | tf_op jit(solution)/shard_map/ppermute | solution.py:53
  111.4 2.2 %collective-permute-done.57 = f32[4,64,128]{2,1,0:T(8,128)S(1)} collective-permute-done((f32[4,64,128]{2,1,0:T(8,128)S(1)}, f32[4,64,128]{2,1,0:T(8,128)S(1)}, u32[]{:S(2)}, u32[]{:S(2)}) %collective-permute-start.57) | collective-permute-done | bytes 131104 | tf_op jit(solution)/shard_map/ppermute | solution.py:53
  119.3 2.9 %collective-permute-done.45 = f32[4,64,128]{2,1,0:T(8,128)S(1)} collective-permute-done((f32[4,64,128]{2,1,0:T(8,128)S(1)}, f32[4,64,128]{2,1,0:T(8,128)S(1)}, u32[]{:S(2)}, u32[]{:S(2)}) %collective-permute-start.45) | collective-permute-done | bytes 131104 | tf_op jit(solution)/shard_map/ppermute | solution.py:53
  122.2 1.6 %collective-permute-start.46 = (f32[4,64,128]{2,1,0:T(8,128)S(1)}, f32[4,64,128]{2,1,0:T(8,128)S(1)}, u32[]{:S(2)}, u32[]{:S(2)}) collective-permute-start(f32[4,64,128]{2,1,0:T(8,128)S(1)} %add.86.refs_1_), channel_id=1, source_target_pairs={{0,4},{1,3},{2,6},{3,1},{4,0},{5,7},{6,2},{7,5},{8,12},{9,11},{10,... | collective-permute-start | bytes 393224 | tf_op jit(solution)/shard_map/ppermute | solution.py:53
  124.5 1.4 %collective-permute-start.47 = (f32[4,64,128]{2,1,0:T(8,128)S(1)}, f32[4,64,128]{2,1,0:T(8,128)S(1)}, u32[]{:S(2)}, u32[]{:S(2)}) collective-permute-start(f32[4,64,128]{2,1,0:T(8,128)S(1)} %add.86.refs_1_), channel_id=1, source_target_pairs={{0,2},{1,5},{2,0},{3,7},{4,6},{5,1},{6,4},{7,3},{8,10},{9,13},{10,... | collective-permute-start | bytes 393224 | tf_op jit(solution)/shard_map/ppermute | solution.py:53
  126.0 2.7 %collective-permute-done.46.refs_2_ = f32[4,64,128]{2,1,0:T(8,128)S(1)} collective-permute-done((f32[4,64,128]{2,1,0:T(8,128)S(1)}, f32[4,64,128]{2,1,0:T(8,128)S(1)}, u32[]{:S(2)}, u32[]{:S(2)}) %collective-permute-start.46) | collective-permute-done | bytes 131104 | tf_op jit(solution)/shard_map/ppermute | solution.py:53
  128.7 1.5 %collective-permute-start.61 = (f32[4,64,128]{2,1,0:T(8,128)S(1)}, f32[4,64,128]{2,1,0:T(8,128)S(1)}, u32[]{:S(2)}, u32[]{:S(2)}) collective-permute-start(f32[4,64,128]{2,1,0:T(8,128)S(1)} %add.91.refs_1_), channel_id=1, source_target_pairs={{0,4},{1,3},{2,6},{3,1},{4,0},{5,7},{6,2},{7,5},{8,12},{9,11},{10,... | collective-permute-start | bytes 393224 | tf_op jit(solution)/shard_map/ppermute | solution.py:53
  130.9 2.0 %collective-permute-done.47.refs_3_ = f32[4,64,128]{2,1,0:T(8,128)S(1)} collective-permute-done((f32[4,64,128]{2,1,0:T(8,128)S(1)}, f32[4,64,128]{2,1,0:T(8,128)S(1)}, u32[]{:S(2)}, u32[]{:S(2)}) %collective-permute-start.47) | collective-permute-done | bytes 131104 | tf_op jit(solution)/shard_map/ppermute | solution.py:53
  132.9 1.6 %collective-permute-done.48.refs_4_ = f32[4,64,128]{2,1,0:T(8,128)S(1)} collective-permute-done((f32[4,64,128]{2,1,0:T(8,128)S(1)}, f32[4,64,128]{2,1,0:T(8,128)S(1)}, u32[]{:S(2)}, u32[]{:S(2)}) %collective-permute-start.48) | collective-permute-done | bytes 131104 | tf_op jit(solution)/shard_map/ppermute | solution.py:53
  (159 shorter events, 43.3 us)
Async XLA Ops:
  3.0 6.3 %collective-permute-start.2 = (f32[32,1152]{1,0:T(8,128)S(1)}, f32[32,1152]{1,0:T(8,128)S(1)}, u32[]{:S(2)}, u32[]{:S(2)}) collective-permute-start(f32[32,1152]{1,0:T(8,128)S(1)} %get-tuple-element.57), channel_id=1, source_target_pairs={{0,2},{1,5},{2,0},{3,7},{4,6},{5,1},{6,4},{7,3},{8,10},{9,13},{10,... | collective-permute-start | bytes 442376 | tf_op jit(solution)/shard_map/ppermute | solution.py:53
  10.8 6.5 %collective-permute-start.4 = (f32[2,4,64,128]{3,2,1,0:T(8,128)S(1)}, f32[2,4,64,128]{3,2,1,0:T(8,128)S(1)}, u32[]{:S(2)}, u32[]{:S(2)}) collective-permute-start(f32[2,4,64,128]{3,2,1,0:T(8,128)S(1)} %get-tuple-element.60), channel_id=1, source_target_pairs={{0,4},{1,3},{2,6},{3,1},{4,0},{5,7},{6,2},{7,5},{8,12},{9,11},{10,... | collective-permute-start | bytes 786440 | tf_op jit(solution)/shard_map/ppermute | solution.py:53
  14.3 14.9 %collective-permute-start = (f32[2048,128]{1,0:T(8,128)S(1)}, f32[2048,128]{1,0:T(8,128)S(1)}, u32[]{:S(2)}, u32[]{:S(2)}) collective-permute-start(f32[2048,128]{1,0:T(8,128)S(1)} %get-tuple-element.53), channel_id=1, source_target_pairs={{0,1},{1,0},{2,3},{3,2},{4,5},{5,4},{6,7},{7,6},{8,9},{9,8},{10,11... | collective-permute-start | bytes 3145736 | tf_op jit(solution)/shard_map/ppermute | solution.py:53
  17.3 5.1 %collective-permute-start.5 = (f32[2,2,64,128]{3,2,1,0:T(8,128)S(1)}, f32[2,2,64,128]{3,2,1,0:T(8,128)S(1)}, u32[]{:S(2)}, u32[]{:S(2)}) collective-permute-start(f32[2,2,64,128]{3,2,1,0:T(8,128)S(1)} %slice.93), channel_id=1, source_target_pairs={{0,8},{1,9},{2,10},{3,11},{4,12},{5,13},{6,14},{7,15},{8,0},{9,1},... | collective-permute-start | bytes 393224 | tf_op jit(solution)/shard_map/ppermute | solution.py:53
  19.5 6.0 %collective-permute-start.7 = (f32[32,1024]{1,0:T(8,128)S(1)}, f32[32,1024]{1,0:T(8,128)S(1)}, u32[]{:S(2)}, u32[]{:S(2)}) collective-permute-start(f32[32,1024]{1,0:T(8,128)S(1)} %get-tuple-element.62), channel_id=1, source_target_pairs={{0,1},{1,0},{2,3},{3,2},{4,5},{5,4},{6,7},{7,6},{8,9},{9,8},{10,11... | collective-permute-start | bytes 393224 | tf_op jit(solution)/shard_map/ppermute | solution.py:53
  19.6 6.0 %collective-permute-start.8 = (f32[32,1024]{1,0:T(8,128)S(1)}, f32[32,1024]{1,0:T(8,128)S(1)}, u32[]{:S(2)}, u32[]{:S(2)}) collective-permute-start(f32[32,1024]{1,0:T(8,128)S(1)} %get-tuple-element.63), channel_id=1, source_target_pairs={{0,2},{1,5},{2,0},{3,7},{4,6},{5,1},{6,4},{7,3},{8,10},{9,13},{10,... | collective-permute-start | bytes 393224 | tf_op jit(solution)/shard_map/ppermute | solution.py:53
  22.5 5.3 %collective-permute-start.6 = (f32[2,1,64,128]{3,2,1,0:T(8,128)S(1)}, f32[2,1,64,128]{3,2,1,0:T(8,128)S(1)}, u32[]{:S(2)}, u32[]{:S(2)}) collective-permute-start(f32[2,1,64,128]{3,2,1,0:T(8,128)S(1)} %slice.94), channel_id=1, source_target_pairs={{0,16},{1,17},{2,18},{3,19},{4,20},{5,21},{6,22},{7,23},{8,24},{9,... | collective-permute-start | bytes 196616 | tf_op jit(solution)/shard_map/ppermute | solution.py:53
  30.2 5.2 %collective-permute-start.24 = (f32[4,64,128]{2,1,0:T(8,128)S(1)}, f32[4,64,128]{2,1,0:T(8,128)S(1)}, u32[]{:S(2)}, u32[]{:S(2)}) collective-permute-start(f32[4,64,128]{2,1,0:T(8,128)S(1)} %get-tuple-element.79), channel_id=1, source_target_pairs={{0,4},{1,3},{2,6},{3,1},{4,0},{5,7},{6,2},{7,5},{8,12},{9,11},{10,... | collective-permute-start | bytes 393224 | tf_op jit(solution)/shard_map/ppermute | solution.py:53
  32.8 6.7 %collective-permute-start.12 = (f32[4,64,128]{2,1,0:T(8,128)S(1)}, f32[4,64,128]{2,1,0:T(8,128)S(1)}, u32[]{:S(2)}, u32[]{:S(2)}) collective-permute-start(f32[4,64,128]{2,1,0:T(8,128)S(1)} %get-tuple-element.68), channel_id=1, source_target_pairs={{0,2},{1,5},{2,0},{3,7},{4,6},{5,1},{6,4},{7,3},{8,10},{9,13},{10,... | collective-permute-start | bytes 393224 | tf_op jit(solution)/shard_map/ppermute | solution.py:53
  34.3 5.8 %collective-permute-start.23 = (f32[4,64,128]{2,1,0:T(8,128)S(1)}, f32[4,64,128]{2,1,0:T(8,128)S(1)}, u32[]{:S(2)}, u32[]{:S(2)}) collective-permute-start(f32[4,64,128]{2,1,0:T(8,128)S(1)} %get-tuple-element.77), channel_id=1, source_target_pairs={{0,4},{1,3},{2,6},{3,1},{4,0},{5,7},{6,2},{7,5},{8,12},{9,11},{10,... | collective-permute-start | bytes 393224 | tf_op jit(solution)/shard_map/ppermute | solution.py:53
  35.5 6.1 %collective-permute-start.25 = (f32[4,64,128]{2,1,0:T(8,128)S(1)}, f32[4,64,128]{2,1,0:T(8,128)S(1)}, u32[]{:S(2)}, u32[]{:S(2)}) collective-permute-start(f32[4,64,128]{2,1,0:T(8,128)S(1)} %add.77), channel_id=1, source_target_pairs={{0,2},{1,5},{2,0},{3,7},{4,6},{5,1},{6,4},{7,3},{8,10},{9,13},{10,... | collective-permute-start | bytes 393224 | tf_op jit(solution)/shard_map/ppermute | solution.py:53
  38.1 30.8 %collective-permute-start.21 = (f32[2048,256]{1,0:T(8,128)S(1)}, f32[2048,256]{1,0:T(8,128)S(1)}, u32[]{:S(2)}, u32[]{:S(2)}) collective-permute-start(f32[2048,256]{1,0:T(8,128)S(1)} %get-tuple-element.72), channel_id=1, source_target_pairs={{0,1},{1,0},{2,3},{3,2},{4,5},{5,4},{6,7},{7,6},{8,9},{9,8},{10,11... | collective-permute-start | bytes 6291464 | tf_op jit(solution)/shard_map/ppermute | solution.py:53
  38.9 30.2 %collective-permute-start.20 = (f32[256,2048]{1,0:T(8,128)S(1)}, f32[256,2048]{1,0:T(8,128)S(1)}, u32[]{:S(2)}, u32[]{:S(2)}) collective-permute-start(f32[256,2048]{1,0:T(8,128)S(1)} %get-tuple-element.70), channel_id=1, source_target_pairs={{0,1},{1,0},{2,3},{3,2},{4,5},{5,4},{6,7},{7,6},{8,9},{9,8},{10,11... | collective-permute-start | bytes 6291464 | tf_op jit(solution)/shard_map/ppermute | solution.py:53
  39.5 5.5 %collective-permute-start.11 = (f32[4,64,128]{2,1,0:T(8,128)S(1)}, f32[4,64,128]{2,1,0:T(8,128)S(1)}, u32[]{:S(2)}, u32[]{:S(2)}) collective-permute-start(f32[4,64,128]{2,1,0:T(8,128)S(1)} %get-tuple-element.66), channel_id=1, source_target_pairs={{0,2},{1,5},{2,0},{3,7},{4,6},{5,1},{6,4},{7,3},{8,10},{9,13},{10,... | collective-permute-start | bytes 393224 | tf_op jit(solution)/shard_map/ppermute | solution.py:53
  41.6 6.0 %collective-permute-start.26 = (f32[2,64,128]{2,1,0:T(8,128)S(1)}, f32[2,64,128]{2,1,0:T(8,128)S(1)}, u32[]{:S(2)}, u32[]{:S(2)}) collective-permute-start(f32[2,64,128]{2,1,0:T(8,128)S(1)} %slice.104), channel_id=1, source_target_pairs={{0,8},{1,9},{2,10},{3,11},{4,12},{5,13},{6,14},{7,15},{8,0},{9,1},... | collective-permute-start | bytes 196616 | tf_op jit(solution)/shard_map/ppermute | solution.py:53
  45.2 5.7 %collective-permute-start.14 = (f32[2,64,128]{2,1,0:T(8,128)S(1)}, f32[2,64,128]{2,1,0:T(8,128)S(1)}, u32[]{:S(2)}, u32[]{:S(2)}) collective-permute-start(f32[2,64,128]{2,1,0:T(8,128)S(1)} %slice.98), channel_id=1, source_target_pairs={{0,8},{1,9},{2,10},{3,11},{4,12},{5,13},{6,14},{7,15},{8,0},{9,1},... | collective-permute-start | bytes 196616 | tf_op jit(solution)/shard_map/ppermute | solution.py:53
  47.7 7.8 %collective-permute-start.27 = (f32[2,64,128]{2,1,0:T(8,128)S(1)}, f32[2,64,128]{2,1,0:T(8,128)S(1)}, u32[]{:S(2)}, u32[]{:S(2)}) collective-permute-start(f32[2,64,128]{2,1,0:T(8,128)S(1)} %pad_maximum_fusion.7), channel_id=1, source_target_pairs={{0,16},{1,17},{2,18},{3,19},{4,20},{5,21},{6,22},{7,23},{8,24},{9,... | collective-permute-start | bytes 196616 | tf_op jit(solution)/shard_map/ppermute | solution.py:53
  50.9 5.7 %collective-permute-start.15 = (f32[2,64,128]{2,1,0:T(8,128)S(1)}, f32[2,64,128]{2,1,0:T(8,128)S(1)}, u32[]{:S(2)}, u32[]{:S(2)}) collective-permute-start(f32[2,64,128]{2,1,0:T(8,128)S(1)} %pad_maximum_fusion.6), channel_id=1, source_target_pairs={{0,16},{1,17},{2,18},{3,19},{4,20},{5,21},{6,22},{7,23},{8,24},{9,... | collective-permute-start | bytes 196616 | tf_op jit(solution)/shard_map/ppermute | solution.py:53
  60.4 6.4 %collective-permute-start.29 = (f32[4,64,128]{2,1,0:T(8,128)S(1)}, f32[4,64,128]{2,1,0:T(8,128)S(1)}, u32[]{:S(2)}, u32[]{:S(2)}) collective-permute-start(f32[4,64,128]{2,1,0:T(8,128)S(1)} %pad_maximum_fusion.1.refs_1_), channel_id=1, source_target_pairs={{0,2},{1,5},{2,0},{3,7},{4,6},{5,1},{6,4},{7,3},{8,10},{9,13},{10,... | collective-permute-start | bytes 393224 | tf_op jit(solution)/shard_map/ppermute | solution.py:53
  61.3 6.1 %collective-permute-start.17 = (f32[4,64,128]{2,1,0:T(8,128)S(1)}, f32[4,64,128]{2,1,0:T(8,128)S(1)}, u32[]{:S(2)}, u32[]{:S(2)}) collective-permute-start(f32[4,64,128]{2,1,0:T(8,128)S(1)} %pad_maximum_fusion.refs_1_), channel_id=1, source_target_pairs={{0,4},{1,3},{2,6},{3,1},{4,0},{5,7},{6,2},{7,5},{8,12},{9,11},{10,... | collective-permute-start | bytes 393224 | tf_op jit(solution)/shard_map/ppermute | solution.py:53
  62.8 14.9 %collective-permute-start.33 = (f32[2,4,64,128]{3,2,1,0:T(8,128)S(1)}, f32[2,4,64,128]{3,2,1,0:T(8,128)S(1)}, u32[]{:S(2)}, u32[]{:S(2)}) collective-permute-start(f32[2,4,64,128]{3,2,1,0:T(8,128)S(1)} %get-tuple-element.85), channel_id=1, source_target_pairs={{0,4},{1,3},{2,6},{3,1},{4,0},{5,7},{6,2},{7,5},{8,12},{9,11},{10,... | collective-permute-start | bytes 786440 | tf_op jit(solution)/shard_map/ppermute | solution.py:53
  66.9 6.2 %collective-permute-start.18 = (f32[4,64,128]{2,1,0:T(8,128)S(1)}, f32[4,64,128]{2,1,0:T(8,128)S(1)}, u32[]{:S(2)}, u32[]{:S(2)}) collective-permute-start(f32[4,64,128]{2,1,0:T(8,128)S(1)} %pad_maximum_fusion.refs_1_), channel_id=1, source_target_pairs={{0,2},{1,5},{2,0},{3,7},{4,6},{5,1},{6,4},{7,3},{8,10},{9,13},{10,... | collective-permute-start | bytes 393224 | tf_op jit(solution)/shard_map/ppermute | solution.py:53
  67.4 7.0 %collective-permute-start.19 = (f32[4,64,128]{2,1,0:T(8,128)S(1)}, f32[4,64,128]{2,1,0:T(8,128)S(1)}, u32[]{:S(2)}, u32[]{:S(2)}) collective-permute-start(f32[4,64,128]{2,1,0:T(8,128)S(1)} %collective-permute-done.17.refs_2_), channel_id=1, source_target_pairs={{0,2},{1,5},{2,0},{3,7},{4,6},{5,1},{6,4},{7,3},{8,10},{9,13},{10,... | collective-permute-start | bytes 393224 | tf_op jit(solution)/shard_map/ppermute | solution.py:53
  68.9 6.4 %collective-permute-start.30 = (f32[4,64,128]{2,1,0:T(8,128)S(1)}, f32[4,64,128]{2,1,0:T(8,128)S(1)}, u32[]{:S(2)}, u32[]{:S(2)}) collective-permute-start(f32[4,64,128]{2,1,0:T(8,128)S(1)} %pad_maximum_fusion.1.refs_1_), channel_id=1, source_target_pairs={{0,4},{1,3},{2,6},{3,1},{4,0},{5,7},{6,2},{7,5},{8,12},{9,11},{10,... | collective-permute-start | bytes 393224 | tf_op jit(solution)/shard_map/ppermute | solution.py:53
  69.1 6.2 %collective-permute-start.31 = (f32[4,64,128]{2,1,0:T(8,128)S(1)}, f32[4,64,128]{2,1,0:T(8,128)S(1)}, u32[]{:S(2)}, u32[]{:S(2)}) collective-permute-start(f32[4,64,128]{2,1,0:T(8,128)S(1)} %collective-permute-done.29.refs_2_), channel_id=1, source_target_pairs={{0,4},{1,3},{2,6},{3,1},{4,0},{5,7},{6,2},{7,5},{8,12},{9,11},{10,... | collective-permute-start | bytes 393224 | tf_op jit(solution)/shard_map/ppermute | solution.py:53
  76.6 5.2 %collective-permute-start.36 = (f32[1,64,128]{2,1,0:T(8,128)S(1)}, f32[1,64,128]{2,1,0:T(8,128)S(1)}, u32[]{:S(2)}, u32[]{:S(2)}) collective-permute-start(f32[1,64,128]{2,1,0:T(8,128)S(1)} %add.82), channel_id=1, source_target_pairs={{0,16},{1,17},{2,18},{3,19},{4,20},{5,21},{6,22},{7,23},{8,24},{9,... | collective-permute-start | bytes 98312 | tf_op jit(solution)/shard_map/ppermute | solution.py:53
  77.8 13.4 %collective-permute-start.34 = (f32[2,2,64,128]{3,2,1,0:T(8,128)S(1)}, f32[2,2,64,128]{3,2,1,0:T(8,128)S(1)}, u32[]{:S(2)}, u32[]{:S(2)}) collective-permute-start(f32[2,2,64,128]{3,2,1,0:T(8,128)S(1)} %get-tuple-element.87), channel_id=1, source_target_pairs={{0,8},{1,9},{2,10},{3,11},{4,12},{5,13},{6,14},{7,15},{8,0},{9,1},... | collective-permute-start | bytes 393224 | tf_op jit(solution)/shard_map/ppermute | solution.py:53
  86.1 6.9 %collective-permute-start.38 = (f32[4,64,128]{2,1,0:T(8,128)S(1)}, f32[4,64,128]{2,1,0:T(8,128)S(1)}, u32[]{:S(2)}, u32[]{:S(2)}) collective-permute-start(f32[4,64,128]{2,1,0:T(8,128)S(1)} %pad_maximum_fusion.2.refs_1_), channel_id=1, source_target_pairs={{0,4},{1,3},{2,6},{3,1},{4,0},{5,7},{6,2},{7,5},{8,12},{9,11},{10,... | collective-permute-start | bytes 393224 | tf_op jit(solution)/shard_map/ppermute | solution.py:53
  88.9 5.1 %collective-permute-start.52 = (f32[4,64,128]{2,1,0:T(8,128)S(1)}, f32[4,64,128]{2,1,0:T(8,128)S(1)}, u32[]{:S(2)}, u32[]{:S(2)}) collective-permute-start(f32[4,64,128]{2,1,0:T(8,128)S(1)} %pad_maximum_fusion.4.refs_1_), channel_id=1, source_target_pairs={{0,2},{1,5},{2,0},{3,7},{4,6},{5,1},{6,4},{7,3},{8,10},{9,13},{10,... | collective-permute-start | bytes 393224 | tf_op jit(solution)/shard_map/ppermute | solution.py:53
  91.2 11.8 %collective-permute-start.35 = (f32[2,2,64,128]{3,2,1,0:T(8,128)S(1)}, f32[2,2,64,128]{3,2,1,0:T(8,128)S(1)}, u32[]{:S(2)}, u32[]{:S(2)}) collective-permute-start(f32[2,2,64,128]{3,2,1,0:T(8,128)S(1)} %add.81), channel_id=1, source_target_pairs={{0,1},{1,0},{2,3},{3,2},{4,5},{5,4},{6,7},{7,6},{8,9},{9,8},{10,11... | collective-permute-start | bytes 393224 | tf_op jit(solution)/shard_map/ppermute | solution.py:53
  91.2 6.4 %collective-permute-start.39 = (f32[4,64,128]{2,1,0:T(8,128)S(1)}, f32[4,64,128]{2,1,0:T(8,128)S(1)}, u32[]{:S(2)}, u32[]{:S(2)}) collective-permute-start(f32[4,64,128]{2,1,0:T(8,128)S(1)} %pad_maximum_fusion.2.refs_1_), channel_id=1, source_target_pairs={{0,2},{1,5},{2,0},{3,7},{4,6},{5,1},{6,4},{7,3},{8,10},{9,13},{10,... | collective-permute-start | bytes 393224 | tf_op jit(solution)/shard_map/ppermute | solution.py:53
  91.3 10.0 %collective-permute-start.53 = (f32[4,64,128]{2,1,0:T(8,128)S(1)}, f32[4,64,128]{2,1,0:T(8,128)S(1)}, u32[]{:S(2)}, u32[]{:S(2)}) collective-permute-start(f32[4,64,128]{2,1,0:T(8,128)S(1)} %pad_maximum_fusion.4.refs_1_), channel_id=1, source_target_pairs={{0,4},{1,3},{2,6},{3,1},{4,0},{5,7},{6,2},{7,5},{8,12},{9,11},{10,... | collective-permute-start | bytes 393224 | tf_op jit(solution)/shard_map/ppermute | solution.py:53
  92.9 7.3 %collective-permute-start.40 = (f32[4,64,128]{2,1,0:T(8,128)S(1)}, f32[4,64,128]{2,1,0:T(8,128)S(1)}, u32[]{:S(2)}, u32[]{:S(2)}) collective-permute-start(f32[4,64,128]{2,1,0:T(8,128)S(1)} %collective-permute-done.38.refs_2_), channel_id=1, source_target_pairs={{0,2},{1,5},{2,0},{3,7},{4,6},{5,1},{6,4},{7,3},{8,10},{9,13},{10,... | collective-permute-start | bytes 393224 | tf_op jit(solution)/shard_map/ppermute | solution.py:53
  94.1 7.3 %collective-permute-start.54 = (f32[4,64,128]{2,1,0:T(8,128)S(1)}, f32[4,64,128]{2,1,0:T(8,128)S(1)}, u32[]{:S(2)}, u32[]{:S(2)}) collective-permute-start(f32[4,64,128]{2,1,0:T(8,128)S(1)} %collective-permute-done.52.refs_2_), channel_id=1, source_target_pairs={{0,4},{1,3},{2,6},{3,1},{4,0},{5,7},{6,2},{7,5},{8,12},{9,11},{10,... | collective-permute-start | bytes 393224 | tf_op jit(solution)/shard_map/ppermute | solution.py:53
  104.0 5.3 %collective-permute-start.43 = (f32[4,64,128]{2,1,0:T(8,128)S(1)}, f32[4,64,128]{2,1,0:T(8,128)S(1)}, u32[]{:S(2)}, u32[]{:S(2)}) collective-permute-start(f32[4,64,128]{2,1,0:T(8,128)S(1)} %get-tuple-element.91), channel_id=1, source_target_pairs={{0,2},{1,5},{2,0},{3,7},{4,6},{5,1},{6,4},{7,3},{8,10},{9,13},{10,... | collective-permute-start | bytes 393224 | tf_op jit(solution)/shard_map/ppermute | solution.py:53
  108.0 5.5 %collective-permute-start.57 = (f32[4,64,128]{2,1,0:T(8,128)S(1)}, f32[4,64,128]{2,1,0:T(8,128)S(1)}, u32[]{:S(2)}, u32[]{:S(2)}) collective-permute-start(f32[4,64,128]{2,1,0:T(8,128)S(1)} %get-tuple-element.97), channel_id=1, source_target_pairs={{0,4},{1,3},{2,6},{3,1},{4,0},{5,7},{6,2},{7,5},{8,12},{9,11},{10,... | collective-permute-start | bytes 393224 | tf_op jit(solution)/shard_map/ppermute | solution.py:53
  108.7 6.4 %collective-permute-start.42 = (f32[4,64,128]{2,1,0:T(8,128)S(1)}, f32[4,64,128]{2,1,0:T(8,128)S(1)}, u32[]{:S(2)}, u32[]{:S(2)}) collective-permute-start(f32[4,64,128]{2,1,0:T(8,128)S(1)} %get-tuple-element.89), channel_id=1, source_target_pairs={{0,2},{1,5},{2,0},{3,7},{4,6},{5,1},{6,4},{7,3},{8,10},{9,13},{10,... | collective-permute-start | bytes 393224 | tf_op jit(solution)/shard_map/ppermute | solution.py:53
  109.3 6.8 %collective-permute-start.44 = (f32[4,64,128]{2,1,0:T(8,128)S(1)}, f32[4,64,128]{2,1,0:T(8,128)S(1)}, u32[]{:S(2)}, u32[]{:S(2)}) collective-permute-start(f32[4,64,128]{2,1,0:T(8,128)S(1)} %add.84), channel_id=1, source_target_pairs={{0,4},{1,3},{2,6},{3,1},{4,0},{5,7},{6,2},{7,5},{8,12},{9,11},{10,... | collective-permute-start | bytes 393224 | tf_op jit(solution)/shard_map/ppermute | solution.py:53
  110.7 7.0 %collective-permute-start.56 = (f32[4,64,128]{2,1,0:T(8,128)S(1)}, f32[4,64,128]{2,1,0:T(8,128)S(1)}, u32[]{:S(2)}, u32[]{:S(2)}) collective-permute-start(f32[4,64,128]{2,1,0:T(8,128)S(1)} %get-tuple-element.95), channel_id=1, source_target_pairs={{0,4},{1,3},{2,6},{3,1},{4,0},{5,7},{6,2},{7,5},{8,12},{9,11},{10,... | collective-permute-start | bytes 393224 | tf_op jit(solution)/shard_map/ppermute | solution.py:53
  113.5 5.2 %collective-permute-start.58 = (f32[4,64,128]{2,1,0:T(8,128)S(1)}, f32[4,64,128]{2,1,0:T(8,128)S(1)}, u32[]{:S(2)}, u32[]{:S(2)}) collective-permute-start(f32[4,64,128]{2,1,0:T(8,128)S(1)} %add.89), channel_id=1, source_target_pairs={{0,2},{1,5},{2,0},{3,7},{4,6},{5,1},{6,4},{7,3},{8,10},{9,13},{10,... | collective-permute-start | bytes 393224 | tf_op jit(solution)/shard_map/ppermute | solution.py:53
  116.2 6.1 %collective-permute-start.45 = (f32[4,64,128]{2,1,0:T(8,128)S(1)}, f32[4,64,128]{2,1,0:T(8,128)S(1)}, u32[]{:S(2)}, u32[]{:S(2)}) collective-permute-start(f32[4,64,128]{2,1,0:T(8,128)S(1)} %pad_maximum_fusion.3), channel_id=1, source_target_pairs={{0,8},{1,9},{2,10},{3,11},{4,12},{5,13},{6,14},{7,15},{8,0},{9,1},... | collective-permute-start | bytes 393224 | tf_op jit(solution)/shard_map/ppermute | solution.py:53
  118.8 5.0 %collective-permute-start.59 = (f32[4,64,128]{2,1,0:T(8,128)S(1)}, f32[4,64,128]{2,1,0:T(8,128)S(1)}, u32[]{:S(2)}, u32[]{:S(2)}) collective-permute-start(f32[4,64,128]{2,1,0:T(8,128)S(1)} %pad_maximum_fusion.5), channel_id=1, source_target_pairs={{0,8},{1,9},{2,10},{3,11},{4,12},{5,13},{6,14},{7,15},{8,0},{9,1},... | collective-permute-start | bytes 393224 | tf_op jit(solution)/shard_map/ppermute | solution.py:53
  122.2 6.4 %collective-permute-start.46 = (f32[4,64,128]{2,1,0:T(8,128)S(1)}, f32[4,64,128]{2,1,0:T(8,128)S(1)}, u32[]{:S(2)}, u32[]{:S(2)}) collective-permute-start(f32[4,64,128]{2,1,0:T(8,128)S(1)} %add.86.refs_1_), channel_id=1, source_target_pairs={{0,4},{1,3},{2,6},{3,1},{4,0},{5,7},{6,2},{7,5},{8,12},{9,11},{10,... | collective-permute-start | bytes 393224 | tf_op jit(solution)/shard_map/ppermute | solution.py:53
  123.9 6.3 %collective-permute-start.60 = (f32[4,64,128]{2,1,0:T(8,128)S(1)}, f32[4,64,128]{2,1,0:T(8,128)S(1)}, u32[]{:S(2)}, u32[]{:S(2)}) collective-permute-start(f32[4,64,128]{2,1,0:T(8,128)S(1)} %add.91.refs_1_), channel_id=1, source_target_pairs={{0,2},{1,5},{2,0},{3,7},{4,6},{5,1},{6,4},{7,3},{8,10},{9,13},{10,... | collective-permute-start | bytes 393224 | tf_op jit(solution)/shard_map/ppermute | solution.py:53
  124.5 8.4 %collective-permute-start.47 = (f32[4,64,128]{2,1,0:T(8,128)S(1)}, f32[4,64,128]{2,1,0:T(8,128)S(1)}, u32[]{:S(2)}, u32[]{:S(2)}) collective-permute-start(f32[4,64,128]{2,1,0:T(8,128)S(1)} %add.86.refs_1_), channel_id=1, source_target_pairs={{0,2},{1,5},{2,0},{3,7},{4,6},{5,1},{6,4},{7,3},{8,10},{9,13},{10,... | collective-permute-start | bytes 393224 | tf_op jit(solution)/shard_map/ppermute | solution.py:53
  128.7 5.8 %collective-permute-start.48 = (f32[4,64,128]{2,1,0:T(8,128)S(1)}, f32[4,64,128]{2,1,0:T(8,128)S(1)}, u32[]{:S(2)}, u32[]{:S(2)}) collective-permute-start(f32[4,64,128]{2,1,0:T(8,128)S(1)} %collective-permute-done.46.refs_2_), channel_id=1, source_target_pairs={{0,2},{1,5},{2,0},{3,7},{4,6},{5,1},{6,4},{7,3},{8,10},{9,13},{10,... | collective-permute-start | bytes 393224 | tf_op jit(solution)/shard_map/ppermute | solution.py:53
  128.7 7.0 %collective-permute-start.61 = (f32[4,64,128]{2,1,0:T(8,128)S(1)}, f32[4,64,128]{2,1,0:T(8,128)S(1)}, u32[]{:S(2)}, u32[]{:S(2)}) collective-permute-start(f32[4,64,128]{2,1,0:T(8,128)S(1)} %add.91.refs_1_), channel_id=1, source_target_pairs={{0,4},{1,3},{2,6},{3,1},{4,0},{5,7},{6,2},{7,5},{8,12},{9,11},{10,... | collective-permute-start | bytes 393224 | tf_op jit(solution)/shard_map/ppermute | solution.py:53
  130.2 5.5 %collective-permute-start.62 = (f32[4,64,128]{2,1,0:T(8,128)S(1)}, f32[4,64,128]{2,1,0:T(8,128)S(1)}, u32[]{:S(2)}, u32[]{:S(2)}) collective-permute-start(f32[4,64,128]{2,1,0:T(8,128)S(1)} %collective-permute-done.60.refs_2_), channel_id=1, source_target_pairs={{0,4},{1,3},{2,6},{3,1},{4,0},{5,7},{6,2},{7,5},{8,12},{9,11},{10,... | collective-permute-start | bytes 393224 | tf_op jit(solution)/shard_map/ppermute | solution.py:53
  (23 other events, 94.2 us)
